TPU v7x, 128 devices: a whole 4x4x4 slice. The times are simulated.
128 devices in a mesh: cam: 4 (over x_hi, core), frame: 32 (over z, y, x_lo).
Axes of the slice: x: 4 (x_hi: 2, x_lo: 2; x = x_hi * 2 + x_lo), y: 4, z: 4, core: 2. Of those that a mesh axis runs over, the one named last changes fastest.
Arguments:
- hidden: bfloat16 [4, 32, 512, 2048], P('cam', 'frame'), may hold values from -6 to 6
- t_query: bfloat16 [4, 32, 512, 1024], P('cam', 'frame'), may hold values from -16 to 16
- t_key: bfloat16 [4, 32, 512, 1024], P('cam', 'frame'), may hold values from -6 to 6
- t_value: bfloat16 [4, 32, 512, 1024], P('cam', 'frame'), may hold values from -6 to 6
- frame_offsets: int32 [32], replicated, may hold values from 0 to 63, as said below
- cycle_sides: int32 [4, 2], P('cam'), may hold values from 0 to 3, as said below
- w_temporal_out: bfloat16 [1024, 2048], replicated, may hold values from -0.1875 to 0.1875
- norm_gain: bfloat16 [2048], replicated, may hold values from 0.099609375 to 1.8984375
- w_query: bfloat16 [2048, 1024], replicated, may hold values from -0.25 to 0.25
- w_key: bfloat16 [2048, 1024], replicated, may hold values from -0.25 to 0.25
- w_value: bfloat16 [2048, 1024], replicated, may hold values from -0.125 to 0.125
- w_cross_out: bfloat16 [1024, 2048], replicated, may hold values from -0.1875 to 0.1875
- side_embed: bfloat16 [2, 1024], replicated, may hold values from -4 to 4
Outputs:
- mixed: bfloat16 [4, 32, 512, 2048], P('cam', 'frame')
Inputs may be any that keep to these rules, and one draw needn't show every extreme that they name: `frame_offsets`: offset of frame f is 2 f or 2 f + 1; the last frame's is 63. `cycle_sides`: row c holds (c - 1) mod 4 and (c + 1) mod 4 in either order.
All inputs are finite; a program needn't handle non-finite values.
Results may differ from a plain program's by a relative error of at most 0.03.
Values may be sent and summed in bfloat16 or wider, within the bound.
No kernel may reach another device: no remote copies, remote signals or barrier semaphores. Data moves between devices by JAX's collectives and lax.ppermute only.
A program may use at most 256 MiB of HBM per device.

v0:
```python
import math

import jax
import jax.numpy as jnp
from jax import lax
from jax.sharding import PartitionSpec as P

HEADS = 8
HEAD_DIM = 128


def from_behind(value, axis, steps):
    count = lax.axis_size(axis)
    pairs = [(source, (source + steps) % count) for source in range(count)]
    return lax.ppermute(value, axis, pairs)


def rotary_angles(offsets):
    half_dim = HEAD_DIM // 2
    steps_f = jnp.arange(half_dim).astype(jnp.float32)
    frequencies = 10000.0 ** (-steps_f / half_dim)
    return offsets.astype(jnp.float32)[..., None] * frequencies


def rotate_pairs(values_in, angles):
    half_dim = values_in.shape[-1] // 2
    cosine = jnp.cos(angles)
    sine = jnp.sin(angles)
    first = values_in[..., :half_dim]
    second = values_in[..., half_dim:]
    return jnp.concatenate(
        [first * cosine - second * sine, first * sine + second * cosine], axis=-1
    )


def softmax_rows(scores):
    top_val = jnp.max(scores, axis=-1, keepdims=True)
    expo = jnp.exp(scores - top_val)
    return expo / jnp.sum(expo, axis=-1, keepdims=True)


def attend_frames(queries, keys_in, values_in):
    score_scale = 1.0 / math.sqrt(HEAD_DIM)
    scores = (
        jnp.einsum("cfphd,cgphd->cphfg", queries, keys_in, preferred_element_type=jnp.float32)
        * score_scale
    )
    weights_t = softmax_rows(scores).astype(jnp.bfloat16)
    result = jnp.einsum(
        "cphfg,cgphd->cfphd", weights_t, values_in, preferred_element_type=jnp.float32
    )
    return result.astype(jnp.bfloat16)


def shards(
    hidden,
    t_query,
    t_key,
    t_value,
    frame_offsets,
    cycle_sides,
    w_temporal_out,
    norm_gain,
    w_query,
    w_key,
    w_value,
    w_cross_out,
    side_embed,
):
    rows_here = hidden.shape[2]
    model_width = hidden.shape[3]
    inner_width = t_query.shape[3]
    score_scale = 1.0 / math.sqrt(HEAD_DIM)
    shape5 = (1, 1, rows_here, HEADS, HEAD_DIM)
    frame_index = lax.axis_index("frame")
    offset_here = lax.dynamic_index_in_dim(frame_offsets, frame_index, 0, keepdims=False)
    angles = rotary_angles(offset_here)
    queries = rotate_pairs(t_query.reshape(shape5).astype(jnp.float32), angles).astype(jnp.bfloat16)
    keys_rot = rotate_pairs(t_key.reshape(shape5).astype(jnp.float32), angles).astype(jnp.bfloat16)
    values_t = t_value.reshape(shape5)
    part_q = lax.all_to_all(queries, "frame", split_axis=2, concat_axis=1, tiled=True)
    part_k = lax.all_to_all(keys_rot, "frame", split_axis=2, concat_axis=1, tiled=True)
    part_v = lax.all_to_all(values_t, "frame", split_axis=2, concat_axis=1, tiled=True)
    result = attend_frames(part_q, part_k, part_v)
    temporal = lax.all_to_all(result, "frame", split_axis=1, concat_axis=2, tiled=True)
    temporal_proj = jnp.dot(
        temporal.reshape(rows_here, inner_width), w_temporal_out, preferred_element_type=jnp.float32
    )
    stream = (hidden.reshape(rows_here, model_width).astype(jnp.float32) + temporal_proj).astype(
        jnp.bfloat16
    )
    stream_f = stream.astype(jnp.float32)
    normed = (
        stream_f
        * lax.rsqrt(jnp.mean(stream_f * stream_f, axis=-1, keepdims=True) + 1e-06)
        * norm_gain.astype(jnp.float32)
    ).astype(jnp.bfloat16)
    cross_q = jnp.dot(normed, w_query, preferred_element_type=jnp.float32).astype(jnp.bfloat16)
    cross_k = jnp.dot(normed, w_key, preferred_element_type=jnp.float32).astype(jnp.bfloat16)
    cross_v = jnp.dot(normed, w_value, preferred_element_type=jnp.float32).astype(jnp.bfloat16)
    key_value = jnp.stack([cross_k, cross_v])
    left_cam = cycle_sides[0, 0]
    right_cam = cycle_sides[0, 1]
    cam_count = lax.axis_size("cam")
    lower_cam = (lax.axis_index("cam") + cam_count - 1) % cam_count
    from_lower = from_behind(key_value, "cam", 1)
    from_upper = from_behind(key_value, "cam", -1)
    left_pair = jnp.where(left_cam == lower_cam, from_lower, from_upper)
    right_pair = jnp.where(right_cam == lower_cam, from_lower, from_upper)
    side_f = side_embed.astype(jnp.float32)
    left_key = (left_pair[0].astype(jnp.float32) + side_f[0]).astype(jnp.bfloat16)
    right_key = (right_pair[0].astype(jnp.float32) + side_f[1]).astype(jnp.bfloat16)
    keys_all = jnp.concatenate([cross_k, left_key, right_key], axis=0).reshape(
        3 * rows_here, HEADS, HEAD_DIM
    )
    vals_all = jnp.concatenate([cross_v, left_pair[1], right_pair[1]], axis=0).reshape(
        3 * rows_here, HEADS, HEAD_DIM
    )
    query_rows = cross_q.reshape(rows_here, HEADS, HEAD_DIM)
    scores_c = (
        jnp.einsum("qhd,khd->hqk", query_rows, keys_all, preferred_element_type=jnp.float32)
        * score_scale
    )
    weights_c = softmax_rows(scores_c).astype(jnp.bfloat16)
    cross = jnp.einsum(
        "hqk,khd->qhd", weights_c, vals_all, preferred_element_type=jnp.float32
    ).astype(jnp.bfloat16)
    cross_proj = jnp.dot(
        cross.reshape(rows_here, inner_width), w_cross_out, preferred_element_type=jnp.float32
    )
    mixed = (stream.astype(jnp.float32) + cross_proj).astype(jnp.bfloat16)
    return mixed.reshape(1, 1, rows_here, model_width)


def solution(mesh):
    in_specs = (
        P("cam", "frame", None, None),
        P("cam", "frame", None, None),
        P("cam", "frame", None, None),
        P("cam", "frame", None, None),
        P(),
        P("cam", None),
        P(),
        P(),
        P(),
        P(),
        P(),
        P(),
        P(),
    )
    out_specs = P("cam", "frame", None, None)
    return jax.shard_map(shards, mesh=mesh, in_specs=in_specs, out_specs=out_specs, check_vma=False)
```

profile of v0, /device:TPU:1, one launch (start us, length us, event | category | flops | bytes accessed | tf_op | source)
XLA Modules:
  0.0 195.5 jit_solution(6542898905501557058)
XLA Ops:
  0.0 1.2 dynamic_slice.4
  1.9 0.0 copy-start.2
  2.0 1.6 convert_bitcast_fusion.1
  3.5 0.5 copy.46
  4.0 0.0 copy-done.2
  4.0 0.2 convert_bitcast_fusion
  4.2 0.5 copy.47
  4.7 1.4 subtract_convert_fusion.1
  6.1 1.6 pad_maximum_fusion.1
  7.7 9.9 %all-to-all-start = ((bf16[1,1,512,8,128]{4,3,1,0,2:T(8,128)(2,1)}), bf16[1,1,512,8,128]{4,3,1,0,2:T(8,128)(2,1)}, u32[]{:S(2)}, u32[]{:S(2)}) async-start(bf16[1,1,512,8,128]{4,3,1,0,2:T(8,128)(2,1)} %pad_maximum_fusion.1), calls=%async_computation | async-start | bytes 2097152 | tf_op jit(solution)/shard_map/all_to_all | solution.py:81
  17.6 0.0 copy-start.3
  17.6 1.5 pad_maximum_fusion.2
  19.2 15.1 %all-to-all-done = bf16[1,1,512,8,128]{4,3,1,0,2:T(8,128)(2,1)} async-done(((bf16[1,1,512,8,128]{4,3,1,0,2:T(8,128)(2,1)}), bf16[1,1,512,8,128]{4,3,1,0,2:T(8,128)(2,1)}, u32[]{:S(2)}, u32[]{:S(2)}) %all-to-all-start) | async-done | bytes 1048608 | tf_op jit(solution)/shard_map/all_to_all | solution.py:81
  34.3 3.9 %all-to-all-start.1 = ((bf16[1,1,512,8,128]{4,3,1,0,2:T(8,128)(2,1)}), bf16[1,1,512,8,128]{4,3,1,0,2:T(8,128)(2,1)S(1)}, u32[]{:S(2)}, u32[]{:S(2)}) async-start(bf16[1,1,512,8,128]{4,3,1,0,2:T(8,128)(2,1)} %pad_maximum_fusion.2), calls=%async_computation.1 | async-start | bytes 2097152 | tf_op jit(solution)/shard_map/all_to_all | solution.py:82
  38.3 0.0 copy-done.3
  38.3 1.3 copy.48
  39.6 14.4 %all-to-all-done.1 = bf16[1,1,512,8,128]{4,3,1,0,2:T(8,128)(2,1)S(1)} async-done(((bf16[1,1,512,8,128]{4,3,1,0,2:T(8,128)(2,1)}), bf16[1,1,512,8,128]{4,3,1,0,2:T(8,128)(2,1)S(1)}, u32[]{:S(2)}, u32[]{:S(2)}) %all-to-all-start.1) | async-done | bytes 1048608 | tf_op jit(solution)/shard_map/all_to_all | solution.py:82
  54.0 4.4 %all-to-all-start.2 = ((bf16[1,1,512,8,128]{4,3,1,0,2:T(8,128)(2,1)}), bf16[1,1,512,8,128]{4,3,1,0,2:T(8,128)(2,1)S(1)}, u32[]{:S(2)}, u32[]{:S(2)}) async-start(bf16[1,1,512,8,128]{4,3,1,0,2:T(8,128)(2,1)} %bitcast.49), calls=%async_computation.2 | async-start | bytes 2097152 | tf_op jit(solution)/shard_map/all_to_all | solution.py:83
  58.4 4.4 %fusion.86 = (f32[16,8,32]{2,1,0:T(8,128)S(1)}, f32[16,8,32,32]{2,3,1,0:T(8,128)}) fusion(bf16[32,16,8,128]{3,2,1,0:T(8,128)(2,1)S(1)} %bitcast.114, bf16[32,16,8,128]{3,2,1,0:T(8,128)(2,1)} %bitcast.2), kind=kOutput, calls=%fused_computation.81 | convolution fusion | flops 33947680 | bytes 2637824 | tf_op jit(solution)/shard_map/sub | solution.py:38
  62.8 10.8 %all-to-all-done.2 = bf16[1,1,512,8,128]{4,3,1,0,2:T(8,128)(2,1)S(1)} async-done(((bf16[1,1,512,8,128]{4,3,1,0,2:T(8,128)(2,1)}), bf16[1,1,512,8,128]{4,3,1,0,2:T(8,128)(2,1)S(1)}, u32[]{:S(2)}, u32[]{:S(2)}) %all-to-all-start.2) | async-done | bytes 1048608 | tf_op jit(solution)/shard_map/all_to_all | solution.py:83
  73.6 2.5 %fusion.34 = bf16[1,32,16,8,128]{4,1,3,2,0:T(8,128)(2,1)S(1)} fusion(f32[16,8,32,32]{2,3,1,0:T(8,128)} %get-tuple-element.18, bf16[32,16,8,128]{3,2,1,0:T(8,128)(2,1)S(1)} %bitcast.115, f32[16,8,32]{2,1,0:T(8,128)S(1)} %get-tuple-element.17), kind=kOutput, calls=%fused_computation.53 | convolution fusion | flops 34340864 | bytes 2637824 | tf_op jit(solution)/shard_map/cphfg,cgphd->cfphd/dot_general | solution.py:49
  76.2 0.0 copy-start.7
  76.2 0.0 copy-start.11
  76.2 1.4 copy.34
  77.6 5.2 %all-to-all-start.3 = ((bf16[1,32,16,8,128]{4,3,2,0,1:T(8,128)(2,1)}), bf16[1,32,16,8,128]{4,3,2,0,1:T(8,128)(2,1)S(1)}, u32[]{:S(2)}, u32[]{:S(2)}) async-start(bf16[1,32,16,8,128]{4,3,2,0,1:T(8,128)(2,1)} %copy.34), calls=%async_computation.3 | async-start | bytes 2097152 | tf_op jit(solution)/shard_map/all_to_all | solution.py:85
  82.7 0.0 copy-done.7
  82.8 15.1 %all-to-all-done.3 = bf16[1,32,16,8,128]{4,3,2,0,1:T(8,128)(2,1)S(1)} async-done(((bf16[1,32,16,8,128]{4,3,2,0,1:T(8,128)(2,1)}), bf16[1,32,16,8,128]{4,3,2,0,1:T(8,128)(2,1)S(1)}, u32[]{:S(2)}, u32[]{:S(2)}) %all-to-all-start.3) | async-done | bytes 1048608 | tf_op jit(solution)/shard_map/all_to_all | solution.py:85
  97.8 0.0 copy-done.11
  97.8 0.0 copy-start.9
  97.8 5.0 %fusion.5 = (f32[512]{0:T(512)S(1)}, bf16[512,2048]{1,0:T(8,128)(2,1)S(1)}) fusion(bf16[1024,2048]{1,0:T(8,128)(2,1)} %param.19, bf16[64,8,8,128]{3,2,1,0:T(8,128)(2,1)S(1)} %bitcast.116, bf16[1,1,512,2048]{3,2,1,0:T(8,128)(2,1)S(1)} %copy-done.11), kind=kOutput, calls=%fused_computation.11 | convolution fusion | flops 2153774592 | bytes 9439232 | tf_op jit(solution)/shard_map/dot_general | solution.py:86
  102.8 0.0 copy-start
  102.8 0.0 copy-done.9
  102.8 0.0 copy-start.10
  102.8 2.4 %convolution_convert_fusion.2 = bf16[512,1024]{1,0:T(8,128)(2,1)S(1)} fusion(bf16[2048,1024]{1,0:T(8,128)(2,1)S(1)} %copy-done.9, bf16[512,2048]{1,0:T(8,128)(2,1)S(1)} %get-tuple-element.20, f32[2048]{0:T(1024)S(1)} %convert_element_type.155, f32[512]{0:T(512)S(1)} %add_rsqrt_fusion), kind=kOutput, calls=%fused_computation.49 | convolution fusion | flops 2152202240 | bytes 7350272 | tf_op jit(solution)/shard_map/dot_general | solution.py:99
  105.2 0.0 copy-done
  105.2 0.5 copy-done.10
  105.8 2.4 %convolution_convert_fusion.3 = bf16[512,1024]{1,0:T(8,128)(2,1)S(1)} fusion(bf16[2048,1024]{1,0:T(8,128)(2,1)S(1)} %copy-done.10, bf16[512,2048]{1,0:T(8,128)(2,1)S(1)} %get-tuple-element.20, f32[2048]{0:T(1024)S(1)} %convert_element_type.155, f32[512]{0:T(512)S(1)} %add_rsqrt_fusion), kind=kOutput, calls=%fused_computation.50 | convolution fusion | flops 2152202240 | bytes 7350272 | tf_op jit(solution)/shard_map/dot_general | solution.py:100
  108.1 0.0 copy-start.8
  108.2 0.0 copy-start.6
  108.2 0.0 copy-done.5
  108.2 1.5 pad_maximum_fusion
  109.7 6.0 %collective-permute-start = (bf16[2,512,1024]{2,1,0:T(8,128)(2,1)}, bf16[2,512,1024]{2,1,0:T(8,128)(2,1)S(1)}, u32[]{:S(2)}, u32[]{:S(2)}) collective-permute-start(bf16[2,512,1024]{2,1,0:T(8,128)(2,1)} %pad_maximum_fusion), channel_id=1, source_target_pairs={{0,32},{32,64},{64,96},{96,0},{1,33},{33,65},{65,97},{97,1},{2,34}... | collective-permute-start | bytes 6291464 | tf_op jit(solution)/shard_map/ppermute | solution.py:15
  115.6 0.0 collective-permute-start.1
  115.6 0.0 copy-done.8
  115.6 0.6 fusion.85
  117.5 0.0 copy-done.6
  117.6 1.3 copy.41
  118.9 6.2 %fusion.33 = bf16[64,8,8,128]{3,2,1,0:T(8,128)(2,1)} fusion(bf16[2048,1024]{1,0:T(8,128)(2,1)} %param.21, bf16[512,2048]{1,0:T(8,128)(2,1)} %copy-done, f32[2048]{0:T(1024)S(1)} %convert_element_type.155, f32[512]{0:T(512)S(1)} %add_rsqrt_fusion), kind=kOutput, calls=%fused_computation.52 | convolution fusion | flops 2152202240 | bytes 7350272 | tf_op jit(solution)/shard_map/dot_general | solution.py:98
  125.1 35.2 %collective-permute-done = bf16[2,512,1024]{2,1,0:T(8,128)(2,1)S(1)} collective-permute-done((bf16[2,512,1024]{2,1,0:T(8,128)(2,1)}, bf16[2,512,1024]{2,1,0:T(8,128)(2,1)S(1)}, u32[]{:S(2)}, u32[]{:S(2)}) %collective-permute-start) | collective-permute-done | bytes 2097184 | tf_op jit(solution)/shard_map/ppermute | solution.py:15
  160.3 2.1 %collective-permute-done.1 = bf16[2,512,1024]{2,1,0:T(8,128)(2,1)} collective-permute-done((bf16[2,512,1024]{2,1,0:T(8,128)(2,1)}, bf16[2,512,1024]{2,1,0:T(8,128)(2,1)}, u32[]{:S(2)}, u32[]{:S(2)}) %collective-permute-start.1) | collective-permute-done | bytes 2097184 | tf_op jit(solution)/shard_map/ppermute | solution.py:15
  162.4 1.9 broadcast_select_fusion.1
  164.2 0.1 slice.53
  164.3 0.2 fusion.27
  164.6 0.0 copy-start.4
  164.6 0.1 slice.52
  164.6 1.2 fusion.28
  165.9 1.3 copy.42
  167.2 1.3 copy.43
  168.5 0.0 copy-done.4
  168.5 8.7 %fusion.91 = f32[8,512]{1,0:T(8,128)S(1)} fusion(bf16[64,8,8,128]{3,2,1,0:T(8,128)(2,1)} %fusion.33, bf16[512,1024]{1,0:T(8,128)(2,1)S(1)} %fusion.27, bf16[512,1024]{1,0:T(8,128)(2,1)} %fusion.28, bf16[512,1024]{1,0:T(8,128)(2,1)} %copy-done.5), kind=kOutput, calls=%fused_computation.82 | convolution fusion | flops 1638925824 | bytes 4210688 | tf_op jit(solution)/shard_map/sub | solution.py:38
  177.2 0.0 copy-start.1
  177.3 12.4 %fusion.30 = bf16[8,128,512]{2,1,0:T(8,128)(2,1)S(1)} fusion(f32[8,512]{1,0:T(8,128)S(1)} %fusion.91, bf16[512,8,128]{0,2,1:T(8,128)(2,1)} %bitcast.118, bf16[512,8,128]{0,2,1:T(8,128)(2,1)} %bitcast.117, bf16[512,8,128]{0,2,1:T(8,128)(2,1)} %bitcast.113, bf16[64,8,8,128]{3,2,1,0:T(8,128)(2,1)} %fusion.33, bf16[512,1024]{1,0:T(8,128)(2,1)} %copy-done.4, ...), kind=kOutput, calls=%fused_computation.51 | convolution fusion | flops 3265795584 | bytes 8404992 | tf_op jit(solution)/shard_map/hqk,khd->qhd/dot_general | solution.py:125
  189.6 0.0 copy-done.1
  189.6 5.9 %fusion.26 = bf16[1,1,512,2048]{3,2,1,0:T(8,128)(2,1)} fusion(bf16[512,1024]{0,1:T(8,128)(2,1)S(1)} %bitcast.111, bf16[1024,2048]{1,0:T(8,128)(2,1)} %param.24, bf16[512,2048]{1,0:T(8,128)(2,1)S(1)} %copy-done.1), kind=kOutput, calls=%fused_computation.29 | convolution fusion | flops 2150629376 | bytes 9437184 | tf_op jit(solution)/shard_map/dot_general | solution.py:128
  (5 shorter events, 0.1 us)
Async XLA Ops:
  1.9 2.1 %copy-start.2 = (bf16[1,1,512,1024]{3,2,1,0:T(8,128)(2,1)S(1)}, bf16[1,1,512,1024]{3,2,1,0:T(8,128)(2,1)}, u32[]{:S(2)}) copy-start(bf16[1,1,512,1024]{3,2,1,0:T(8,128)(2,1)} %param.15) | copy-start | bytes 3145732
  7.7 26.6 %all-to-all-start = ((bf16[1,1,512,8,128]{4,3,1,0,2:T(8,128)(2,1)}), bf16[1,1,512,8,128]{4,3,1,0,2:T(8,128)(2,1)}, u32[]{:S(2)}, u32[]{:S(2)}) async-start(bf16[1,1,512,8,128]{4,3,1,0,2:T(8,128)(2,1)} %pad_maximum_fusion.1), calls=%async_computation | async-start | bytes 2097152 | tf_op jit(solution)/shard_map/all_to_all | solution.py:81
  17.6 20.6 %copy-start.3 = (bf16[1,1,512,1024]{3,2,1,0:T(8,128)(2,1)S(1)}, bf16[1,1,512,1024]{3,2,1,0:T(8,128)(2,1)}, u32[]{:S(2)}) copy-start(bf16[1,1,512,1024]{3,2,1,0:T(8,128)(2,1)} %param.16) | copy-start | bytes 3145732
  34.3 19.6 %all-to-all-start.1 = ((bf16[1,1,512,8,128]{4,3,1,0,2:T(8,128)(2,1)}), bf16[1,1,512,8,128]{4,3,1,0,2:T(8,128)(2,1)S(1)}, u32[]{:S(2)}, u32[]{:S(2)}) async-start(bf16[1,1,512,8,128]{4,3,1,0,2:T(8,128)(2,1)} %pad_maximum_fusion.2), calls=%async_computation.1 | async-start | bytes 2097152 | tf_op jit(solution)/shard_map/all_to_all | solution.py:82
  54.0 19.7 %all-to-all-start.2 = ((bf16[1,1,512,8,128]{4,3,1,0,2:T(8,128)(2,1)}), bf16[1,1,512,8,128]{4,3,1,0,2:T(8,128)(2,1)S(1)}, u32[]{:S(2)}, u32[]{:S(2)}) async-start(bf16[1,1,512,8,128]{4,3,1,0,2:T(8,128)(2,1)} %bitcast.49), calls=%async_computation.2 | async-start | bytes 2097152 | tf_op jit(solution)/shard_map/all_to_all | solution.py:83
  76.2 6.6 %copy-start.7 = (bf16[2048]{0:T(1024)(128)(2,1)S(1)}, bf16[2048]{0:T(1024)(128)(2,1)}, u32[]{:S(2)}) copy-start(bf16[2048]{0:T(1024)(128)(2,1)} %param.20) | copy-start | bytes 12292
  76.2 21.6 %copy-start.11 = (bf16[1,1,512,2048]{3,2,1,0:T(8,128)(2,1)S(1)}, bf16[1,1,512,2048]{3,2,1,0:T(8,128)(2,1)}, u32[]{:S(2)}) copy-start(bf16[1,1,512,2048]{3,2,1,0:T(8,128)(2,1)} %param.13) | copy-start | bytes 6291460
  77.6 20.2 %all-to-all-start.3 = ((bf16[1,32,16,8,128]{4,3,2,0,1:T(8,128)(2,1)}), bf16[1,32,16,8,128]{4,3,2,0,1:T(8,128)(2,1)S(1)}, u32[]{:S(2)}, u32[]{:S(2)}) async-start(bf16[1,32,16,8,128]{4,3,2,0,1:T(8,128)(2,1)} %copy.34), calls=%async_computation.3 | async-start | bytes 2097152 | tf_op jit(solution)/shard_map/all_to_all | solution.py:85
  97.8 5.0 %copy-start.9 = (bf16[2048,1024]{1,0:T(8,128)(2,1)S(1)}, bf16[2048,1024]{1,0:T(8,128)(2,1)}, u32[]{:S(2)}) copy-start(bf16[2048,1024]{1,0:T(8,128)(2,1)} %param.22) | copy-start | bytes 12582916
  102.8 2.4 %copy-start = (bf16[512,2048]{1,0:T(8,128)(2,1)}, bf16[512,2048]{1,0:T(8,128)(2,1)S(1)}, u32[]{:S(2)}) copy-start(bf16[512,2048]{1,0:T(8,128)(2,1)S(1)} %get-tuple-element.20) | copy-start | bytes 6291460
  102.8 2.9 %copy-start.10 = (bf16[2048,1024]{1,0:T(8,128)(2,1)S(1)}, bf16[2048,1024]{1,0:T(8,128)(2,1)}, u32[]{:S(2)}) copy-start(bf16[2048,1024]{1,0:T(8,128)(2,1)} %param.23) | copy-start | bytes 12582916
  105.8 2.4 %copy-start.5 = (bf16[512,1024]{1,0:T(8,128)(2,1)}, bf16[512,1024]{1,0:T(8,128)(2,1)S(1)}, u32[]{:S(2)}) copy-start(bf16[512,1024]{1,0:T(8,128)(2,1)S(1)} %convolution_convert_fusion.2) | copy-start | bytes 3145732
  108.1 7.5 %copy-start.8 = (s32[1,2]{1,0:T(1,128)S(1)}, s32[1,2]{1,0:T(1,128)}, u32[]{:S(2)}) copy-start(s32[1,2]{1,0:T(1,128)} %param.18) | copy-start | bytes 28
  108.2 9.4 %copy-start.6 = (bf16[2,1024]{1,0:T(2,128)(2,1)S(1)}, bf16[2,1024]{1,0:T(2,128)(2,1)}, u32[]{:S(2)}) copy-start(bf16[2,1024]{1,0:T(2,128)(2,1)} %param.25) | copy-start | bytes 12292
  109.7 50.6 %collective-permute-start = (bf16[2,512,1024]{2,1,0:T(8,128)(2,1)}, bf16[2,512,1024]{2,1,0:T(8,128)(2,1)S(1)}, u32[]{:S(2)}, u32[]{:S(2)}) collective-permute-start(bf16[2,512,1024]{2,1,0:T(8,128)(2,1)} %pad_maximum_fusion), channel_id=1, source_target_pairs={{0,32},{32,64},{64,96},{96,0},{1,33},{33,65},{65,97},{97,1},{2,34}... | collective-permute-start | bytes 6291464 | tf_op jit(solution)/shard_map/ppermute | solution.py:15
  115.6 46.7 %collective-permute-start.1 = (bf16[2,512,1024]{2,1,0:T(8,128)(2,1)}, bf16[2,512,1024]{2,1,0:T(8,128)(2,1)}, u32[]{:S(2)}, u32[]{:S(2)}) collective-permute-start(bf16[2,512,1024]{2,1,0:T(8,128)(2,1)} %pad_maximum_fusion), channel_id=1, source_target_pairs={{0,96},{32,0},{64,32},{96,64},{1,97},{33,1},{65,33},{97,65},{2,98}... | collective-permute-start | bytes 6291464 | tf_op jit(solution)/shard_map/ppermute | solution.py:15
  164.6 4.0 %copy-start.4 = (bf16[512,1024]{1,0:T(8,128)(2,1)}, bf16[512,1024]{1,0:T(8,128)(2,1)S(1)}, u32[]{:S(2)}) copy-start(bf16[512,1024]{1,0:T(8,128)(2,1)S(1)} %fusion.27) | copy-start | bytes 3145732
  177.2 12.4 %copy-start.1 = (bf16[512,2048]{1,0:T(8,128)(2,1)S(1)}, bf16[512,2048]{1,0:T(8,128)(2,1)}, u32[]{:S(2)}) copy-start(bf16[512,2048]{1,0:T(8,128)(2,1)} %copy-done) | copy-start | bytes 6291460
where the time goes:
time: 196 us
  waiting for transfers between devices  92.7 us (47%)
  matrix products  49.8 us (25%)
  starting transfers between devices  29.4 us (15%)
  other arithmetic  11.2 us (6%)
  local copies, waits for them, and re-layouts  10.2 us (5%)
  between operations  2.24 us (1%)
    ppermute x2, waiting for transfers between devices, from_behind(): return lax.ppermute(value, axis, pairs)  37.3 us
    all_to_all x1, waiting for transfers between devices, shards(): lax.all_to_all(queries, 'frame', split_axis=2, concat_axis=1, tiled=True)  15.1 us
    all_to_all x1, waiting for transfers between devices, shards(): lax.all_to_all(result, 'frame', split_axis=1, concat_axis=2, tiled=True)  15.1 us
    all_to_all x1, waiting for transfers between devices, shards(): lax.all_to_all(keys_rot, 'frame', split_axis=2, concat_axis=1, tiled=True)  14.4 us
    sub x2, matrix products, softmax_rows(): expo = jnp.exp(scores - top_val)  13.1 us
    dot_general x1, matrix products, shards(): jnp.einsum('hqk,khd->qhd', weights_c, vals_all, preferred_element_type=jn...  12.4 us
    all_to_all x1, waiting for transfers between devices, shards(): lax.all_to_all(values_t, 'frame', split_axis=2, concat_axis=1, tiled=True)  10.8 us
    all_to_all x1, starting transfers between devices, shards(): lax.all_to_all(queries, 'frame', split_axis=2, concat_axis=1, tiled=True)  9.94 us
  transfers between devices with their start and end apart: 6, of which 6 were waited for; matrix products, arithmetic and copies ran while one was open for 8% of the time, Pallas kernels for 0%

commit v1 on v0

v1 whole, which is shorter than its diff:
```python
import functools
import math

import jax
import jax.numpy as jnp
from jax import lax
from jax.experimental import pallas as pl
from jax.experimental.pallas import tpu as pltpu
from jax.sharding import PartitionSpec as P

HEADS = 8
HEAD_DIM = 128
MIB = 1 << 20
VMEM_LIMIT = 60 * MIB
F32 = jnp.float32
BF16 = jnp.bfloat16
EXP2_SCALE = math.log2(math.e) / math.sqrt(HEAD_DIM)


def dot_f32(a, b):
    return jnp.dot(a, b, preferred_element_type=F32)


def dot_nt(a, b):
    return lax.dot_general(a, b, (((1,), (1,)), ((), ())), preferred_element_type=F32)


def rotary_angles(offsets):
    half_dim = HEAD_DIM // 2
    steps_f = jnp.arange(half_dim).astype(F32)
    frequencies = 10000.0 ** (-steps_f / half_dim)
    return offsets.astype(F32)[..., None] * frequencies


def temporal_kernel(group, heads_at_once, *refs):
    q_ref, k_ref, v_ref, cos_ref, sin_ref = refs[:5]
    o_ref = refs[-1]
    rows = q_ref.shape[0]
    cosine = cos_ref[...]
    sine = sin_ref[...]
    row_at = lax.broadcasted_iota(jnp.int32, (rows, rows), 0)
    key_at = lax.broadcasted_iota(jnp.int32, (rows, rows), 1)
    same = lax.rem(row_at, group) == lax.rem(key_at, group)

    def rotated(part):
        part = part.astype(F32)
        return (part * cosine + pltpu.roll(part, HEAD_DIM // 2, 1) * sine).astype(BF16)

    for head in range(heads_at_once):
        at = slice(head * HEAD_DIM, (head + 1) * HEAD_DIM)
        scores = dot_nt(rotated(q_ref[:, at]), rotated(k_ref[:, at]))
        scores = jnp.where(same, scores, -jnp.inf)
        top = jnp.max(scores, axis=-1, keepdims=True)
        expo = jnp.exp2((scores - top) * EXP2_SCALE)
        weights = (expo * (1.0 / jnp.sum(expo, axis=-1, keepdims=True))).astype(BF16)
        o_ref[:, at] = dot_f32(weights, v_ref[:, at]).astype(BF16)


def temporal(packed, cosine, sine, group, into):
    rows = packed.shape[0]
    at_once = 2
    width = at_once * HEAD_DIM
    steps = HEADS // at_once
    in_specs = [
        pl.BlockSpec((rows, width), lambda i: (0, i)),
        pl.BlockSpec((rows, width), lambda i: (0, steps + i)),
        pl.BlockSpec((rows, width), lambda i: (0, 2 * steps + i)),
        pl.BlockSpec((rows, HEAD_DIM), lambda i: (0, 0)),
        pl.BlockSpec((rows, HEAD_DIM), lambda i: (0, 0)),
    ]
    args = [packed, packed, packed, cosine, sine]
    aliases = {}
    first = 0
    out_width = HEADS * HEAD_DIM
    if into is not None:
        in_specs.append(pl.BlockSpec(memory_space=pl.ANY))
        args.append(into)
        aliases = {5: 0}
        first = 3 * steps
        out_width = into.shape[1]
    return pl.pallas_call(
        functools.partial(temporal_kernel, group, at_once),
        grid=(steps,),
        in_specs=in_specs,
        out_specs=pl.BlockSpec((rows, width), lambda i: (0, first + i)),
        out_shape=jax.ShapeDtypeStruct((rows, out_width), BF16),
        input_output_aliases=aliases,
        compiler_params=pltpu.CompilerParams(vmem_limit_bytes=VMEM_LIMIT),
        cost_estimate=pl.CostEstimate(
            flops=4 * rows * rows * HEADS * HEAD_DIM,
            bytes_accessed=8 * rows * HEADS * HEAD_DIM,
            transcendentals=rows * rows * HEADS,
        ),
        name="temporal",
    )(*args)


def project_kernel(*refs):
    t_ref, hidden_ref, w_out_ref, gain_ref, w_key_ref, w_value_ref = refs[:6]
    stream_ref, normed_ref, kv_ref = refs[-3:]
    step = pl.program_id(0)

    @pl.when(step < 2)
    def _():
        cols = pl.ds(pl.multiple_of(step * 1024, 1024), 1024)
        part = dot_f32(t_ref[...], w_out_ref[...])
        stream_ref[:, cols] = (hidden_ref[:, cols].astype(F32) + part).astype(BF16)

    @pl.when(step == 2)
    def _():
        stream = stream_ref[...].astype(F32)
        scale = lax.rsqrt(jnp.mean(stream * stream, axis=-1, keepdims=True) + 1e-06)
        normed_ref[...] = (stream * scale * gain_ref[...].astype(F32)).astype(BF16)

    @pl.when((step >= 2) & (step < 4))
    def _():
        kv_ref[...] = dot_f32(normed_ref[...], w_key_ref[...]).astype(BF16)

    @pl.when(step >= 4)
    def _():
        kv_ref[...] = dot_f32(normed_ref[...], w_value_ref[...]).astype(BF16)


def project(t_out, t_block, hidden, w_out, gain, w_key, w_value, chunk, into):
    rows = t_out.shape[0]
    inner = HEADS * HEAD_DIM
    width = hidden.shape[1]
    in_specs = [
        pl.BlockSpec((rows, inner), lambda i: (0, t_block)),
        pl.BlockSpec((rows, width), lambda i: (chunk, 0)),
        pl.BlockSpec((inner, 1024), lambda i: (0, jnp.minimum(i, 1))),
        pl.BlockSpec((1, width), lambda i: (0, 0)),
        pl.BlockSpec((width, 512), lambda i: (0, jnp.clip(i - 2, 0, 1))),
        pl.BlockSpec((width, 512), lambda i: (0, jnp.clip(i - 4, 0, 1))),
    ]
    args = [t_out, hidden, w_out, gain, w_key, w_value]
    aliases = {}
    if into is not None:
        in_specs += [pl.BlockSpec(memory_space=pl.ANY)] * 2
        args += list(into)
        aliases = {6: 0, 7: 1}
    return pl.pallas_call(
        project_kernel,
        grid=(6,),
        in_specs=in_specs,
        out_specs=[
            pl.BlockSpec((rows, width), lambda i: (chunk, 0)),
            pl.BlockSpec((rows, width), lambda i: (chunk, 0)),
            pl.BlockSpec((rows, 512), lambda i: (0, jnp.clip(i - 2, 0, 3))),
        ],
        out_shape=[
            jax.ShapeDtypeStruct(hidden.shape, BF16),
            jax.ShapeDtypeStruct(hidden.shape, BF16),
            jax.ShapeDtypeStruct((rows, 2 * inner), BF16),
        ],
        input_output_aliases=aliases,
        compiler_params=pltpu.CompilerParams(vmem_limit_bytes=VMEM_LIMIT),
        cost_estimate=pl.CostEstimate(
            flops=6 * rows * inner * width,
            bytes_accessed=16 * MIB,
            transcendentals=0,
        ),
        name="project",
    )(*args)


def first_kernel(sides, heads_at_once, *refs):
    normed_ref, w_query_ref, embed_ref = refs[:3]
    count = len(sides)
    key_refs = refs[3 : 3 + count]
    value_refs = refs[3 + count : 3 + 2 * count]
    q_ref, acc_ref, top_ref, total_ref = refs[3 + 2 * count :]
    step = pl.program_id(0)
    lane = lax.broadcasted_iota(jnp.int32, (256, HEAD_DIM), 1)
    for block in range(2):
        rows = slice(block * 256, (block + 1) * 256)
        q_ref[rows, :] = dot_f32(normed_ref[rows, :], w_query_ref[...]).astype(BF16)
    for head in range(heads_at_once):
        at = slice(head * HEAD_DIM, (head + 1) * HEAD_DIM)
        keys = []
        for side, key_ref in zip(sides, key_refs):
            key = key_ref[:, at]
            if side is not None:
                key = (key.astype(F32) + embed_ref[side : side + 1, at]).astype(BF16)
            keys.append(key)
        for block in range(2):
            rows = slice(block * 256, (block + 1) * 256)
            query = q_ref[rows, at]
            scores = [dot_nt(query, key) for key in keys]
            top = functools.reduce(jnp.maximum, scores)
            top = jnp.max(top, axis=-1, keepdims=True)
            total = 0.0
            acc = 0.0
            for score, value_ref in zip(scores, value_refs):
                expo = jnp.exp2((score - top) * EXP2_SCALE)
                total = total + jnp.sum(expo, axis=-1, keepdims=True)
                acc = acc + dot_f32(expo.astype(BF16), value_ref[:, at])
            acc_ref[rows, at] = acc
            mine = lane == step * heads_at_once + head
            top_ref[rows, :] = jnp.where(mine, top, top_ref[rows, :])
            total_ref[rows, :] = jnp.where(mine, total, total_ref[rows, :])


def first_part(normed, w_query, embeds, views, sides):
    rows, width = normed.shape
    inner = HEADS * HEAD_DIM
    at_once = 2
    cols = at_once * HEAD_DIM
    steps = HEADS // at_once
    key_spec = pl.BlockSpec((views[0].shape[0], cols), lambda i: (0, i))
    value_spec = pl.BlockSpec((views[0].shape[0], cols), lambda i: (0, steps + i))
    return pl.pallas_call(
        functools.partial(first_kernel, sides, at_once),
        grid=(steps,),
        in_specs=[
            pl.BlockSpec((rows, width), lambda i: (0, 0)),
            pl.BlockSpec((width, cols), lambda i: (0, i)),
            pl.BlockSpec((2, cols), lambda i: (0, i)),
        ]
        + [key_spec] * len(views)
        + [value_spec] * len(views),
        out_specs=[
            pl.BlockSpec((rows, cols), lambda i: (0, i)),
            pl.BlockSpec((rows, cols), lambda i: (0, i)),
            pl.BlockSpec((rows, HEAD_DIM), lambda i: (0, 0)),
            pl.BlockSpec((rows, HEAD_DIM), lambda i: (0, 0)),
        ],
        out_shape=[
            jax.ShapeDtypeStruct((rows, inner), BF16),
            jax.ShapeDtypeStruct((rows, inner), F32),
            jax.ShapeDtypeStruct((rows, HEAD_DIM), F32),
            jax.ShapeDtypeStruct((rows, HEAD_DIM), F32),
        ],
        compiler_params=pltpu.CompilerParams(vmem_limit_bytes=VMEM_LIMIT),
        cost_estimate=pl.CostEstimate(
            flops=2 * rows * width * inner + 4 * rows * 256 * len(views) * inner,
            bytes_accessed=14 * MIB,
            transcendentals=rows * 256 * len(views) * HEADS,
        ),
        name="first_part",
    )(normed, w_query, embeds, *views, *views)


def last_kernel(
    q_ref, acc_ref, top_ref, total_ref, kv_ref, embed_ref, stream_ref, w_hbm, o_ref, w_ref, out_ref, sem
):
    step = pl.program_id(0)
    inner = HEADS * HEAD_DIM
    fetch = pltpu.make_async_copy(w_hbm, w_ref, sem)

    @pl.when(step == 0)
    def _():
        fetch.start()

    for head in range(HEADS):
        at = slice(head * HEAD_DIM, (head + 1) * HEAD_DIM)
        value_at = slice(inner + head * HEAD_DIM, inner + (head + 1) * HEAD_DIM)
        key = (kv_ref[:, at].astype(F32) + embed_ref[1:2, at]).astype(BF16)
        scores = dot_nt(q_ref[:, at], key)
        top_before = top_ref[:, head : head + 1]
        top = jnp.maximum(top_before, jnp.max(scores, axis=-1, keepdims=True))
        keep = jnp.exp2((top_before - top) * EXP2_SCALE)
        expo = jnp.exp2((scores - top) * EXP2_SCALE)
        total = total_ref[:, head : head + 1] * keep + jnp.sum(expo, axis=-1, keepdims=True)
        acc = acc_ref[:, at] * keep + dot_f32(expo.astype(BF16), kv_ref[:, value_at])
        out_ref[:, at] = (acc * (1.0 / total)).astype(BF16)

    @pl.when(step == 0)
    def _():
        fetch.wait()

    for part in range(4):
        cols = slice(part * 512, (part + 1) * 512)
        product = dot_f32(out_ref[...], w_ref[:, cols])
        o_ref[:, cols] = (stream_ref[:, cols].astype(F32) + product).astype(BF16)


def last_part(query, acc, top, total, view, embeds, stream, w_out):
    rows, width = stream.shape
    inner = HEADS * HEAD_DIM
    block = 256
    return pl.pallas_call(
        last_kernel,
        grid=(rows // block,),
        in_specs=[
            pl.BlockSpec((block, inner), lambda i: (i, 0)),
            pl.BlockSpec((block, inner), lambda i: (i, 0)),
            pl.BlockSpec((block, HEAD_DIM), lambda i: (i, 0)),
            pl.BlockSpec((block, HEAD_DIM), lambda i: (i, 0)),
            pl.BlockSpec(view.shape, lambda i: (0, 0)),
            pl.BlockSpec(embeds.shape, lambda i: (0, 0)),
            pl.BlockSpec((block, width), lambda i: (i, 0)),
            pl.BlockSpec(memory_space=pl.ANY),
        ],
        out_specs=pl.BlockSpec((block, width), lambda i: (i, 0)),
        out_shape=jax.ShapeDtypeStruct((rows, width), BF16),
        scratch_shapes=[
            pltpu.VMEM(w_out.shape, BF16),
            pltpu.VMEM((block, inner), BF16),
            pltpu.SemaphoreType.DMA,
        ],
        compiler_params=pltpu.CompilerParams(vmem_limit_bytes=VMEM_LIMIT),
        cost_estimate=pl.CostEstimate(
            flops=2 * rows * width * inner + 4 * rows * view.shape[0] * inner,
            bytes_accessed=12 * MIB,
            transcendentals=rows * view.shape[0] * HEADS,
        ),
        name="last_part",
    )(query, acc, top, total, view, embeds, stream, w_out)


def shards(
    hidden,
    t_query,
    t_key,
    t_value,
    frame_offsets,
    cycle_sides,
    w_temporal_out,
    norm_gain,
    w_query,
    w_key,
    w_value,
    w_cross_out,
    side_embed,
):
    rows_here = hidden.shape[2]
    model_width = hidden.shape[3]
    inner = t_query.shape[3]
    frames = lax.axis_size("frame")
    half = rows_here // 2
    group = half // frames
    hidden = hidden.reshape(rows_here, model_width)
    t_query = t_query.reshape(rows_here, inner)
    t_key = t_key.reshape(rows_here, inner)
    t_value = t_value.reshape(rows_here, inner)
    gain = norm_gain.reshape(1, model_width)

    angles = rotary_angles(frame_offsets)
    cosine = jnp.cos(angles)
    sine = jnp.sin(angles)
    cosine = jnp.repeat(jnp.concatenate([cosine, cosine], axis=-1), group, axis=0)
    sine = jnp.repeat(jnp.concatenate([-sine, sine], axis=-1), group, axis=0)

    def exchange(value):
        return lax.all_to_all(value, "frame", split_axis=0, concat_axis=0, tiled=True)

    def to_near(value):
        return lax.ppermute(value, "cam", [(0, 1), (1, 0), (2, 3), (3, 2)])

    def to_far(value):
        return lax.ppermute(value, "cam", [(0, 3), (3, 0), (1, 2), (2, 1)])

    near_cam = lax.axis_index("cam") ^ 1
    near_left = cycle_sides[0, 0] == near_cam
    side_f = side_embed.astype(F32)
    embeds = jnp.where(near_left, side_f, side_f[::-1])

    packed_a = jnp.concatenate([t_query[:half], t_key[:half], t_value[:half]], axis=1)
    packed_b = jnp.concatenate(
        [t_query[half:], t_key[half:], t_value[half:], jnp.zeros((half, inner), BF16)], axis=1
    )
    got_a = exchange(packed_a)
    packed_b = temporal(got_a, cosine, sine, group, packed_b)
    got_b = exchange(packed_b)
    out_b = temporal(got_b, cosine, sine, group, None)
    back_b = exchange(out_b)

    weights = (w_temporal_out, gain, w_key, w_value)
    stream, normed, kv_a = project(got_b, 3, hidden, *weights, 0, None)
    far_a = to_far(kv_a)
    near_a = to_near(kv_a)
    stream, normed, kv_b = project(back_b, 0, hidden, *weights, 1, (stream, normed))
    far_b = to_far(kv_b)
    near_b = to_near(kv_b)
    query, acc, top, total = first_part(
        normed, w_query, embeds, [kv_a, kv_b, near_a, near_b, far_a], (None, None, 0, 0, 1)
    )
    mixed = last_part(query, acc, top, total, far_b, embeds, stream, w_cross_out)
    return mixed.reshape(1, 1, rows_here, model_width)


def solution(mesh):
    in_specs = (
        P("cam", "frame", None, None),
        P("cam", "frame", None, None),
        P("cam", "frame", None, None),
        P("cam", "frame", None, None),
        P(),
        P("cam", None),
        P(),
        P(),
        P(),
        P(),
        P(),
        P(),
        P(),
    )
    out_specs = P("cam", "frame", None, None)
    return jax.shard_map(shards, mesh=mesh, in_specs=in_specs, out_specs=out_specs, check_vma=False)
```

time: 196 us -> 165 us (0.84)
  Pallas kernels: 0 us -> 64.9 us
  waiting for transfers between devices: 92.7 us -> 34.8 us
  matrix products: 49.8 us -> 0 us
  blocking collectives: 0 us -> 31.6 us
  starting transfers between devices: 29.4 us -> 20.5 us
  other arithmetic: 11.2 us -> 3.82 us
  local copies, waits for them, and re-layouts: 10.2 us -> 8.12 us
    pallas_call x0 -> x6, Pallas kernels: none -> 64.9 us  [the longest x2 22 us: project(): pl.pallas_call(project_kernel, grid=(6,), in_specs=in_specs, out_specs=[p...]
    dot_general x7 -> x0, matrix products: 36.7 us -> none  [the longest x1 12.4 us: shards(): jnp.einsum('hqk,khd->qhd', weights_c, vals_all, preferred_element_type=jn...]
    all_to_all x4 -> x2, waiting for transfers between devices: 55.5 us -> 19.1 us  [exchange(): lax.all_to_all(value, 'frame', split_axis=0, concat_axis=0, tiled=True)]
    all_to_all x0 -> x1, blocking collectives: none -> 31.6 us  [exchange(): lax.all_to_all(value, 'frame', split_axis=0, concat_axis=0, tiled=True)]
    ppermute x2 -> x4, waiting for transfers between devices: 37.3 us -> 15.7 us  [the longest x2 15.7 us: to_far(): return lax.ppermute(value, 'cam', [(0, 3), (3, 0), (1, 2), (2, 1)])]
    sub x2 -> x0, matrix products: 13.1 us -> none  [softmax_rows(): expo = jnp.exp(scores - top_val)]
    all_to_all x4 -> x2, starting transfers between devices: 23.5 us -> 14.6 us  [exchange(): lax.all_to_all(value, 'frame', split_axis=0, concat_axis=0, tiled=True)]
    concatenate x3 -> x1, local copies, waits for them, and re-layouts: 3.97 us -> 0.01 us  [shards(): jnp.concatenate([t_query[half:], t_key[half:], t_value[half:], jnp.zeros(...]
  transfers between devices with their start and end apart: 6 -> 6, of which waited for: 6 -> 3; matrix products, arithmetic and copies ran while one was open for 8% -> 3% of each run, Pallas kernels for 0% -> 23%
where the time goes in v1:
time: 165 us; the launch traced here: 164 us
  Pallas kernels  64.9 us (39%)
  waiting for transfers between devices  34.8 us (21%)
  blocking collectives  31.6 us (19%)
  starting transfers between devices  20.5 us (12%)
  local copies, waits for them, and re-layouts  8.12 us (5%)
  other arithmetic  3.82 us (2%)
    all_to_all x1, blocking collectives, exchange(): lax.all_to_all(value, 'frame', split_axis=0, concat_axis=0, tiled=True)  31.6 us
    pallas_call x2, Pallas kernels, project(): pl.pallas_call(project_kernel, grid=(6,), in_specs=in_specs, out_specs=[p...  22 us
    all_to_all x2, waiting for transfers between devices, exchange(): lax.all_to_all(value, 'frame', split_axis=0, concat_axis=0, tiled=True)  19.1 us
    pallas_call x1, Pallas kernels, first_part(): pl.pallas_call(functools.partial(first_kernel, sides, at_once), grid=(ste...  16.1 us
    ppermute x2, waiting for transfers between devices, to_far(): return lax.ppermute(value, 'cam', [(0, 3), (3, 0), (1, 2), (2, 1)])  15.7 us
    pallas_call x1, Pallas kernels, last_part(): pl.pallas_call(last_kernel, grid=(rows // block,), in_specs=[pl.BlockSpec...  14.7 us
    all_to_all x2, starting transfers between devices, exchange(): lax.all_to_all(value, 'frame', split_axis=0, concat_axis=0, tiled=True)  14.6 us
    pallas_call x2, Pallas kernels, temporal(): pl.pallas_call(functools.partial(temporal_kernel, group, at_once), grid=(...  12 us
  transfers between devices with their start and end apart: 6, of which 3 were waited for; matrix products, arithmetic and copies ran while one was open for 3% of the time, Pallas kernels for 23%

profile of v1, /device:TPU:1, one launch (start us, length us, event | category | flops | bytes accessed | tf_op | source)
XLA Modules:
  0.0 164.1 jit_solution(4214672145476271893)
XLA Ops:
  0.0 0.0 copy-start.3
  0.0 0.0 copy-start.2
  0.0 1.4 slice_bitcast_fusion.2
  1.4 0.1 copy-done.3
  1.5 0.3 copy-done.2
  1.9 0.2 slice_bitcast_fusion
  2.0 1.3 pad_maximum_fusion
  3.3 0.0 copy-start.9
  3.3 9.9 %all-to-all-start = ((bf16[32,8,3072]{2,1,0:T(8,128)(2,1)}), bf16[32,8,3072]{2,1,0:T(8,128)(2,1)S(1)}, u32[]{:S(2)}, u32[]{:S(2)}) async-start(bf16[32,8,3072]{2,1,0:T(8,128)(2,1)} %pad_maximum_fusion), calls=%async_computation | async-start | bytes 3145728 | tf_op jit(solution)/shard_map/all_to_all | solution.py:346
  13.3 0.0 copy-done.9
  13.3 0.1 fusion
  13.5 0.1 pad_maximum_fusion.1
  13.5 0.7 broadcast_bitcast_fusion.refs_4_
  14.2 0.7 broadcast_bitcast_fusion.1.refs_3_
  14.9 1.7 %maximum_maximum_fusion.refs_5_ = bf16[256,4096]{1,0:T(8,128)(2,1)} fusion(bf16[256,1024]{1,0:T(8,128)(2,1)S(1)} %get-tuple-element.29, bf16[256,1024]{1,0:T(8,128)(2,1)S(1)} %get-tuple-element.35, bf16[256,1024]{1,0:T(8,128)(2,1)S(1)} %get-tuple-element.25, bf16[4096]{0:T(1024)(128)(2,1)S(1)} %pad.3.clone), kind=kLoop, calls=%fused_computation | loop fusion | flops 8388608 | bytes 3678208 | tf_op jit(solution)/shard_map/concatenate | solution.py:360
  16.6 19.1 %all-to-all-done = bf16[32,8,3072]{2,1,0:T(8,128)(2,1)S(1)} async-done(((bf16[32,8,3072]{2,1,0:T(8,128)(2,1)}), bf16[32,8,3072]{2,1,0:T(8,128)(2,1)S(1)}, u32[]{:S(2)}, u32[]{:S(2)}) %all-to-all-start) | async-done | bytes 1572896 | tf_op jit(solution)/shard_map/all_to_all | solution.py:346
  35.7 0.0 copy-start
  35.7 1.2 copy-done
  36.9 6.0 %temporal.2 = bf16[256,4096]{1,0:T(8,128)(2,1)} custom-call(bf16[256,3072]{1,0:T(8,128)(2,1)} %bitcast.29, bf16[256,3072]{1,0:T(8,128)(2,1)} %bitcast.30, bf16[256,3072]{1,0:T(8,128)(2,1)} %bitcast.31, f32[256,128]{1,0:T(8,128)} %broadcast_bitcast_fusion.1.refs_3_, f32[256,128]{1,0:T(8,128)} %broadcast_bitcast_fusion.refs_4_, ...), custom_call_target="tpu_custom_call", output_to_operand_aliasing={{}: (5, {})} | custom-call | flops 268435456 | bytes 2097152 | tf_op jit(solution)/shard_map/temporal/pallas_call | solution.py:81
  42.9 31.6 %all_to_all.30 = bf16[32,8,4096]{2,1,0:T(8,128)(2,1)} all-to-all(bf16[32,8,4096]{2,1,0:T(8,128)(2,1)} %bitcast.32), channel_id=1, replica_groups=mesh['cam'=4,'frame'=32] {'frame'}, dimensions={0} | all-to-all | bytes 4194304 | tf_op jit(solution)/shard_map/all_to_all | solution.py:346
  74.5 0.0 copy-start.6
  74.5 6.0 %temporal.3 = bf16[256,1024]{1,0:T(8,128)(2,1)} custom-call(bf16[256,4096]{1,0:T(8,128)(2,1)} %bitcast.25, bf16[256,4096]{1,0:T(8,128)(2,1)} %bitcast.26, bf16[256,4096]{1,0:T(8,128)(2,1)} %bitcast.27, f32[256,128]{1,0:T(8,128)} %broadcast_bitcast_fusion.1.refs_3_, f32[256,128]{1,0:T(8,128)} %broadcast_bitcast_fusion.refs_4_), custom_call_target="tpu_custom_call" | custom-call | flops 268435456 | bytes 2097152 | tf_op jit(solution)/shard_map/temporal/pallas_call | solution.py:81
  80.5 4.6 %all-to-all-start.2 = ((bf16[32,8,1024]{2,1,0:T(8,128)(2,1)}), bf16[32,8,1024]{2,1,0:T(8,128)(2,1)S(1)}, u32[]{:S(2)}, u32[]{:S(2)}) async-start(bf16[32,8,1024]{2,1,0:T(8,128)(2,1)} %bitcast.36), calls=%async_computation.2 | async-start | bytes 1048576 | tf_op jit(solution)/shard_map/all_to_all | solution.py:346
  85.2 0.0 copy-done.6
  85.2 0.6 reshape.47.refs_3_
  85.8 11.0 %project.2 = (bf16[512,2048]{1,0:T(8,128)(2,1)}, bf16[512,2048]{1,0:T(8,128)(2,1)}, bf16[256,2048]{1,0:T(8,128)(2,1)}) custom-call(bf16[256,4096]{1,0:T(8,128)(2,1)} %bitcast.28, bf16[512,2048]{1,0:T(8,128)(2,1)} %bitcast.33, bf16[1024,2048]{1,0:T(8,128)(2,1)} %refs_2_.3, bf16[1,2048]{1,0:T(2,128)(2,1)} %reshape.47.refs_3_, bf16[2048,1024]{1,0:T(8,128)(2,1)} %refs_4_.3, ...), custom_call_target="tpu_custom_call" | custom-call | flops 3221225472 | bytes 16777216 | tf_op jit(solution)/shard_map/project/pallas_call | solution.py:142
  96.8 2.4 %collective-permute-start = (bf16[256,2048]{1,0:T(8,128)(2,1)}, bf16[256,2048]{1,0:T(8,128)(2,1)S(1)}, u32[]{:S(2)}, u32[]{:S(2)}) collective-permute-start(bf16[256,2048]{1,0:T(8,128)(2,1)} %get-tuple-element.18.refs_3_.refs_8_), channel_id=1, source_target_pairs={{0,32},{32,0},{64,96},{96,64},{1,33},{33,1},{65,97},{97,65},{2,34}... | collective-permute-start | bytes 3145736 | tf_op jit(solution)/shard_map/ppermute | solution.py:349
  99.2 2.4 %collective-permute-start.2 = (bf16[256,2048]{1,0:T(8,128)(2,1)}, bf16[256,2048]{1,0:T(8,128)(2,1)S(1)}, u32[]{:S(2)}, u32[]{:S(2)}) collective-permute-start(bf16[256,2048]{1,0:T(8,128)(2,1)} %get-tuple-element.18.refs_3_.refs_8_), channel_id=1, source_target_pairs={{0,96},{96,0},{32,64},{64,32},{1,97},{97,1},{33,65},{65,33},{2,98}... | collective-permute-start | bytes 3145736 | tf_op jit(solution)/shard_map/ppermute | solution.py:352
  101.6 0.0 all-to-all-done.2
  101.6 0.0 copy-start.1
  101.6 0.8 copy-done.1
  102.4 0.0 copy-start.5
  102.4 0.0 copy-start.10
  102.4 11.0 %project.3 = (bf16[512,2048]{1,0:T(8,128)(2,1)}, bf16[512,2048]{1,0:T(8,128)(2,1)}, bf16[256,2048]{1,0:T(8,128)(2,1)}) custom-call(bf16[256,1024]{1,0:T(8,128)(2,1)} %bitcast.35, bf16[512,2048]{1,0:T(8,128)(2,1)} %bitcast.34, bf16[1024,2048]{1,0:T(8,128)(2,1)} %refs_2_.3, ...), custom_call_target="tpu_custom_call", output_to_operand_aliasing={{0}: (6, {}), {1}: (7, {})} | custom-call | flops 3221225472 | bytes 16777216 | tf_op jit(solution)/shard_map/project/pallas_call | solution.py:142
  113.5 0.4 collective-permute-start.1
  113.9 0.7 collective-permute-start.3
  114.6 0.0 copy-done.5
  114.6 0.2 rev.3
  114.8 0.0 copy-done.10
  114.8 0.6 broadcast_select_fusion.refs_2_.embed_ref
  115.4 0.0 collective-permute-done.refs_5_.refs_10_
  115.4 0.0 copy-start.7
  115.4 11.2 %collective-permute-done.2.refs_7_.refs_12_ = bf16[256,2048]{1,0:T(8,128)(2,1)S(1)} collective-permute-done((bf16[256,2048]{1,0:T(8,128)(2,1)}, bf16[256,2048]{1,0:T(8,128)(2,1)S(1)}, u32[]{:S(2)}, u32[]{:S(2)}) %collective-permute-start.2) | collective-permute-done | bytes 1048608 | tf_op jit(solution)/shard_map/ppermute | solution.py:352
  126.6 0.0 copy-start.8
  126.6 0.0 collective-permute-done.1.refs_6_.refs_11_
  126.6 0.0 copy-done.7
  126.6 1.0 copy-done.8
  127.6 16.1 %first_part.1 = (bf16[512,1024]{1,0:T(8,128)(2,1)}, f32[512,1024]{1,0:T(8,128)}, f32[512,128]{1,0:T(8,128)}, f32[512,128]{1,0:T(8,128)}) custom-call(bf16[512,2048]{1,0:T(8,128)(2,1)} %get-tuple-element.17.refs_0_, bf16[2048,1024]{1,0:T(8,128)(2,1)} %refs_1_.1, f32[2,1024]{1,0:T(2,128)} %broadcast_select_fusion.refs_2_.embed_ref, ...), custom_call_target="tpu_custom_call" | custom-call | flops 4831838208 | bytes 14680064 | tf_op jit(solution)/shard_map/first_part/pallas_call | solution.py:212
  143.8 4.5 %collective-permute-done.3.kv_ref = bf16[256,2048]{1,0:T(8,128)(2,1)S(1)} collective-permute-done((bf16[256,2048]{1,0:T(8,128)(2,1)}, bf16[256,2048]{1,0:T(8,128)(2,1)S(1)}, u32[]{:S(2)}, u32[]{:S(2)}) %collective-permute-start.3) | collective-permute-done | bytes 1048608 | tf_op jit(solution)/shard_map/ppermute | solution.py:352
  148.2 0.0 copy-start.4
  148.2 1.0 copy-done.4
  149.2 14.7 %last_part.1 = bf16[512,2048]{1,0:T(8,128)(2,1)} custom-call(bf16[512,1024]{1,0:T(8,128)(2,1)} %get-tuple-element.20.q_ref, f32[512,1024]{1,0:T(8,128)} %get-tuple-element.21.acc_ref, f32[512,128]{1,0:T(8,128)} %get-tuple-element.22.top_ref, f32[512,128]{1,0:T(8,128)} %get-tuple-element.23.total_ref, bf16[256,2048]{1,0:T(8,128)(2,1)} %copy-done.4, ...), custom_call_target="tpu_custom_call" | custom-call | flops 2684354560 | bytes 12582912 | tf_op jit(solution)/shard_map/last_part/pallas_call | solution.py:282
  (4 shorter events, 0.0 us)
Async XLA Ops:
  0.0 1.5 copy-start.3
  0.0 1.9 %copy-start.2 = (bf16[1,1,512,1024]{3,2,1,0:T(8,128)(2,1)S(1)}, bf16[1,1,512,1024]{3,2,1,0:T(8,128)(2,1)}, u32[]{:S(2)}) copy-start(bf16[1,1,512,1024]{3,2,1,0:T(8,128)(2,1)} %param.16) | copy-start | bytes 3145732
  3.3 10.0 %copy-start.9 = (s32[32]{0:T(128)S(1)}, s32[32]{0:T(128)}, u32[]{:S(2)}) copy-start(s32[32]{0:T(128)} %param.17) | copy-start | bytes 388
  3.3 32.4 %all-to-all-start = ((bf16[32,8,3072]{2,1,0:T(8,128)(2,1)}), bf16[32,8,3072]{2,1,0:T(8,128)(2,1)S(1)}, u32[]{:S(2)}, u32[]{:S(2)}) async-start(bf16[32,8,3072]{2,1,0:T(8,128)(2,1)} %pad_maximum_fusion), calls=%async_computation | async-start | bytes 3145728 | tf_op jit(solution)/shard_map/all_to_all | solution.py:346
  35.7 1.2 copy-start
  74.5 10.7 %copy-start.6 = (bf16[2048]{0:T(1024)(128)(2,1)S(1)}, bf16[2048]{0:T(1024)(128)(2,1)}, u32[]{:S(2)}) copy-start(bf16[2048]{0:T(1024)(128)(2,1)} %param.20) | copy-start | bytes 12292
  80.5 21.1 %all-to-all-start.2 = ((bf16[32,8,1024]{2,1,0:T(8,128)(2,1)}), bf16[32,8,1024]{2,1,0:T(8,128)(2,1)S(1)}, u32[]{:S(2)}, u32[]{:S(2)}) async-start(bf16[32,8,1024]{2,1,0:T(8,128)(2,1)} %bitcast.36), calls=%async_computation.2 | async-start | bytes 1048576 | tf_op jit(solution)/shard_map/all_to_all | solution.py:346
  96.8 18.7 %collective-permute-start = (bf16[256,2048]{1,0:T(8,128)(2,1)}, bf16[256,2048]{1,0:T(8,128)(2,1)S(1)}, u32[]{:S(2)}, u32[]{:S(2)}) collective-permute-start(bf16[256,2048]{1,0:T(8,128)(2,1)} %get-tuple-element.18.refs_3_.refs_8_), channel_id=1, source_target_pairs={{0,32},{32,0},{64,96},{96,64},{1,33},{33,1},{65,97},{97,65},{2,34}... | collective-permute-start | bytes 3145736 | tf_op jit(solution)/shard_map/ppermute | solution.py:349
  99.2 27.4 %collective-permute-start.2 = (bf16[256,2048]{1,0:T(8,128)(2,1)}, bf16[256,2048]{1,0:T(8,128)(2,1)S(1)}, u32[]{:S(2)}, u32[]{:S(2)}) collective-permute-start(bf16[256,2048]{1,0:T(8,128)(2,1)} %get-tuple-element.18.refs_3_.refs_8_), channel_id=1, source_target_pairs={{0,96},{96,0},{32,64},{64,32},{1,97},{97,1},{33,65},{65,33},{2,98}... | collective-permute-start | bytes 3145736 | tf_op jit(solution)/shard_map/ppermute | solution.py:352
  101.6 0.8 copy-start.1
  102.4 12.1 %copy-start.5 = (bf16[2,1024]{1,0:T(2,128)(2,1)S(1)}, bf16[2,1024]{1,0:T(2,128)(2,1)}, u32[]{:S(2)}) copy-start(bf16[2,1024]{1,0:T(2,128)(2,1)} %param.25) | copy-start | bytes 12292
  102.4 12.4 %copy-start.10 = (s32[1,2]{1,0:T(1,128)S(1)}, s32[1,2]{1,0:T(1,128)}, u32[]{:S(2)}) copy-start(s32[1,2]{1,0:T(1,128)} %param.18) | copy-start | bytes 28
  113.5 13.2 %collective-permute-start.1 = (bf16[256,2048]{1,0:T(8,128)(2,1)}, bf16[256,2048]{1,0:T(8,128)(2,1)}, u32[]{:S(2)}, u32[]{:S(2)}) collective-permute-start(bf16[256,2048]{1,0:T(8,128)(2,1)} %get-tuple-element.19.refs_4_.refs_9_), channel_id=1, source_target_pairs={{0,32},{32,0},{64,96},{96,64},{1,33},{33,1},{65,97},{97,65},{2,34}... | collective-permute-start | bytes 3145736 | tf_op jit(solution)/shard_map/ppermute | solution.py:349
  113.9 34.3 %collective-permute-start.3 = (bf16[256,2048]{1,0:T(8,128)(2,1)}, bf16[256,2048]{1,0:T(8,128)(2,1)S(1)}, u32[]{:S(2)}, u32[]{:S(2)}) collective-permute-start(bf16[256,2048]{1,0:T(8,128)(2,1)} %get-tuple-element.19.refs_4_.refs_9_), channel_id=1, source_target_pairs={{0,96},{96,0},{32,64},{64,32},{1,97},{97,1},{33,65},{65,33},{2,98}... | collective-permute-start | bytes 3145736 | tf_op jit(solution)/shard_map/ppermute | solution.py:352
  115.4 11.2 %copy-start.7 = (bf16[256,2048]{1,0:T(8,128)(2,1)}, bf16[256,2048]{1,0:T(8,128)(2,1)S(1)}, u32[]{:S(2)}) copy-start(bf16[256,2048]{1,0:T(8,128)(2,1)S(1)} %collective-permute-done.refs_5_.refs_10_) | copy-start | bytes 3145732
  126.6 1.0 copy-start.8
  148.2 1.0 copy-start.4

commit v2 on v0

v2 whole, which is shorter than its diff:
```python
import functools
import math

import jax
import jax.numpy as jnp
from jax import lax
from jax.experimental import pallas as pl
from jax.experimental.pallas import tpu as pltpu
from jax.sharding import PartitionSpec as P

HEADS = 8
HEAD_DIM = 128
MIB = 1 << 20
F32 = jnp.float32
BF16 = jnp.bfloat16
EXP2_SCALE = math.log2(math.e) / math.sqrt(HEAD_DIM)


def dot_f32(a, b):
    return jnp.dot(a, b, preferred_element_type=F32)


def dot_nt(a, b):
    return lax.dot_general(a, b, (((1,), (1,)), ((), ())), preferred_element_type=F32)


def rotary_frequencies():
    half_dim = HEAD_DIM // 2
    steps_f = jnp.arange(half_dim).astype(F32)
    frequencies = 10000.0 ** (-steps_f / half_dim)
    return jnp.concatenate([frequencies, frequencies])[None, :]


VMEM = pl.BlockSpec(memory_space=pltpu.VMEM)
HBM = pl.BlockSpec(memory_space=pltpu.HBM)


def columns(head):
    return slice(head * HEAD_DIM, (head + 1) * HEAD_DIM)


def with_ones(values):
    return jnp.concatenate([values, jnp.ones_like(values)], axis=1)


def copy_all(pairs, sems):
    copies = [pltpu.make_async_copy(a, b, sems.at[i]) for i, (a, b) in enumerate(pairs)]
    for copy in copies:
        copy.start()
    for copy in copies:
        copy.wait()


def in_hbm(*arrays):
    return [pltpu.with_memory_space_constraint(array, pltpu.HBM) for array in arrays]


def pack_kernel(q_ref, k_ref, v_ref, offset_ref, frequency_ref, o_ref, cos_ref, sin_ref, sems):
    rows, inner = o_ref.shape[0], q_ref.shape[1]
    moves = [
        pltpu.make_async_copy(ref.at[:rows, :], o_ref.at[:, i * inner : (i + 1) * inner], sems.at[i])
        for i, ref in enumerate((q_ref, k_ref, v_ref))
    ]
    for move in moves:
        move.start()
    frames = offset_ref.shape[0]
    group = rows // frames
    angles = offset_ref[...] * frequency_ref[...]
    lane = lax.broadcasted_iota(jnp.int32, angles.shape, 1)
    cosine = jnp.cos(angles)
    sine = jnp.sin(angles)
    sine = jnp.where(lane < HEAD_DIM // 2, -sine, sine)
    for frame in range(frames):
        at = slice(frame * group, (frame + 1) * group)
        cos_ref[at, :] = jnp.broadcast_to(cosine[frame : frame + 1, :], (group, HEAD_DIM))
        sin_ref[at, :] = jnp.broadcast_to(sine[frame : frame + 1, :], (group, HEAD_DIM))
    for move in moves:
        move.wait()


def pack(query, key, value, offsets, frequencies):
    rows, inner = query.shape
    half = rows // 2
    table = pltpu.VMEM((half, HEAD_DIM), F32)
    return pl.pallas_call(
        pack_kernel,
        in_specs=[HBM] * 3 + [VMEM] * 2,
        out_specs=[VMEM] * 3,
        out_shape=[pltpu.VMEM((half, 3 * inner), BF16), table, table],
        scratch_shapes=[pltpu.SemaphoreType.DMA((3,))],
        compiler_params=pltpu.CompilerParams(vmem_limit_bytes=4 * MIB),
        cost_estimate=pl.CostEstimate(flops=0, bytes_accessed=6 * rows * inner, transcendentals=0),
        name="pack",
    )(*in_hbm(query, key, value), offsets, frequencies)


def temporal_kernel(group, packed_ref, cos_ref, sin_ref, *refs):
    rows = packed_ref.shape[0]
    inner = HEADS * HEAD_DIM
    count = max(len(refs) - 2, 0)
    first = 0
    o_ref = refs[count]
    copies = []
    if count:
        first = count * inner
        for i, ref in enumerate(refs[:count]):
            to = o_ref.at[:, i * inner : (i + 1) * inner]
            copies.append(pltpu.make_async_copy(ref.at[rows:, :], to, refs[count + 1].at[i]))
            copies[-1].start()
    cosine = cos_ref[...]
    sine = sin_ref[...]
    row_at = lax.broadcasted_iota(jnp.int32, (rows, rows), 0)
    key_at = lax.broadcasted_iota(jnp.int32, (rows, rows), 1)
    same = lax.rem(row_at, group) == lax.rem(key_at, group)
    def rotated(part):
        part = part.astype(F32)
        return (part * cosine + pltpu.roll(part, HEAD_DIM // 2, 1) * sine).astype(BF16)

    for head in range(HEADS):
        query = rotated(packed_ref[:, columns(head)])
        key = rotated(packed_ref[:, columns(HEADS + head)])
        value = packed_ref[:, columns(2 * HEADS + head)]
        scores = jnp.where(same, dot_nt(query, key), -jnp.inf)
        top = jnp.max(scores, axis=-1, keepdims=True)
        expo = jnp.exp2((scores - top) * EXP2_SCALE).astype(BF16)
        both = dot_f32(expo, with_ones(value))
        result = both[:, :HEAD_DIM] / both[:, HEAD_DIM:]
        o_ref[:, first + head * HEAD_DIM : first + (head + 1) * HEAD_DIM] = result.astype(BF16)
    for copy in copies:
        copy.wait()


def temporal(packed, cosine, sine, group, following):
    rows = packed.shape[0]
    inner = HEADS * HEAD_DIM
    count = len(following)
    return pl.pallas_call(
        functools.partial(temporal_kernel, group),
        in_specs=[VMEM] * 3 + [HBM] * count,
        out_specs=VMEM,
        out_shape=jax.ShapeDtypeStruct((rows, inner * (1 + count)), BF16),
        scratch_shapes=[pltpu.SemaphoreType.DMA((3,))] if count else [],
        compiler_params=pltpu.CompilerParams(vmem_limit_bytes=6 * MIB),
        cost_estimate=pl.CostEstimate(
            flops=20_000_000_000 if count else 1, bytes_accessed=1, transcendentals=0
        ),
        name="temporal",
    )(packed, cosine, sine, *in_hbm(*following))


def project_rows(t_ref, hidden, w_out_ref, gain_ref, w_key_ref, w_value_ref, stream_ref, normed_ref, kv_ref, ready, done):
    inner, width = w_out_ref.shape
    part = 512
    squares = 0.0
    for i in range(width // part):
        at = slice(i * part, (i + 1) * part)
        ready(i)
        stream = (hidden[:, at].astype(F32) + dot_f32(t_ref[...], w_out_ref[:, at])).astype(BF16)
        stream_ref[:, at] = stream
        stream = stream.astype(F32)
        squares = squares + jnp.sum(stream * stream, axis=-1, keepdims=True)
    done(0)
    scale = lax.rsqrt(squares / width + 1e-06)
    normed_ref[...] = (stream_ref[...].astype(F32) * scale * gain_ref[...].astype(F32).reshape(1, width)).astype(BF16)
    done(1)
    for i in range(2 * inner // part):
        at = slice(i * part, (i + 1) * part)
        ready(width // part + i)
        w_ref = w_key_ref if i < inner // part else w_value_ref
        from_w = slice(i * part % inner, i * part % inner + part)
        kv_ref[:, at] = dot_f32(normed_ref[...], w_ref[:, from_w]).astype(BF16)
        done(2 + i)


def project_first_kernel(t_at, t_ref, hidden_ref, w_out_ref, gain_ref, w_key_ref, w_value_ref, *refs):
    outs, scratch, sems = refs[:3], refs[3:6], refs[6]
    rows = t_ref.shape[0]
    inner, width = w_out_ref.shape
    part = 512
    steps = 2 * inner // part
    cuts = [slice(i * part, (i + 1) * part) for i in range(steps)]
    copies = [pltpu.make_async_copy(scratch[i], outs[i], sems.at[i]) for i in range(2)]
    copies += [
        pltpu.make_async_copy(scratch[2].at[:, at], outs[2].at[:, at], sems.at[2 + i])
        for i, at in enumerate(cuts)
    ]

    project_rows(
        t_ref.at[:, t_at : t_at + inner],
        hidden_ref.at[:rows, :],
        w_out_ref,
        gain_ref,
        w_key_ref,
        w_value_ref,
        *scratch,
        lambda i: None,
        lambda i: copies[i].start(),
    )
    for copy in copies:
        copy.wait()


def project_first(t_out, t_at, hidden, w_out, gain, w_key, w_value):
    rows = t_out.shape[0]
    inner = HEADS * HEAD_DIM
    width = hidden.shape[1]
    shapes = [(rows, width), (rows, width), (rows, 2 * inner)]
    return pl.pallas_call(
        functools.partial(project_first_kernel, t_at),
        in_specs=[VMEM] * 6,
        out_specs=[HBM] * 3,
        out_shape=[pltpu.HBM(shape, BF16) for shape in shapes],
        scratch_shapes=[pltpu.VMEM(shape, BF16) for shape in shapes]
        + [pltpu.SemaphoreType.DMA((6,))],
        compiler_params=pltpu.CompilerParams(vmem_limit_bytes=10 * MIB),
        cost_estimate=pl.CostEstimate(flops=1, bytes_accessed=1, transcendentals=0),
        name="project_first",
    )(t_out, hidden, w_out, gain, w_key, w_value)


def project_second_kernel(t_ref, gain_ref, hidden_hbm, *refs):
    w_hbm, outs, hidden_ref, w_refs, sems = refs[:3], refs[3:6], refs[6], refs[7:10], refs[10]
    rows = t_ref.shape[0]
    part = 512
    get_hidden = pltpu.make_async_copy(hidden_hbm.at[rows:, :], hidden_ref, sems.at[8])
    get_hidden.start()
    copies = []
    for a, b in zip(w_hbm, w_refs):
        for i in range(a.shape[1] // part):
            at = slice(i * part, (i + 1) * part)
            copies.append(pltpu.make_async_copy(a.at[:, at], b.at[:, at], sems.at[len(copies)]))
            copies[-1].start()
    get_hidden.wait()
    project_rows(
        t_ref,
        hidden_ref,
        w_refs[0],
        gain_ref,
        w_refs[1],
        w_refs[2],
        *outs,
        lambda i: copies[i].wait(),
        lambda i: None,
    )


def project_second(t_out, hidden, w_out, gain, w_key, w_value):
    rows = t_out.shape[0]
    inner = HEADS * HEAD_DIM
    width = hidden.shape[1]
    shapes = [(rows, width), (rows, width), (rows, 2 * inner)]
    weights = (w_out, w_key, w_value)
    return pl.pallas_call(
        project_second_kernel,
        in_specs=[VMEM] * 2 + [HBM] * 4,
        out_specs=[VMEM] * 3,
        out_shape=[jax.ShapeDtypeStruct(shape, BF16) for shape in shapes],
        scratch_shapes=[pltpu.VMEM((rows, width), BF16)]
        + [pltpu.VMEM(w.shape, BF16) for w in weights]
        + [pltpu.SemaphoreType.DMA((9,))],
        compiler_params=pltpu.CompilerParams(vmem_limit_bytes=22 * MIB),
        cost_estimate=pl.CostEstimate(flops=1, bytes_accessed=1, transcendentals=0),
        name="project_second",
    )(t_out, gain, *in_hbm(hidden, *weights))


def first_kernel(sides, *refs):
    count = len(sides)
    normed_refs = refs[:2]
    w_query_ref, embed_ref = refs[2:4]
    kv_refs = refs[4 : 4 + count]
    q_ref, acc_ref, top_ref, total_ref = refs[4 + count :]
    inner = HEADS * HEAD_DIM
    rows = normed_refs[0].shape[0]
    for block, normed_ref in enumerate(normed_refs):
        q_ref[block * rows : (block + 1) * rows, :] = dot_f32(
            normed_ref[...], w_query_ref[...]
        ).astype(BF16)

    @pl.loop(0, HEADS)
    def _(head):
        at = pl.ds(pl.multiple_of(head * HEAD_DIM, HEAD_DIM), HEAD_DIM)
        value_at = pl.ds(pl.multiple_of(inner + head * HEAD_DIM, HEAD_DIM), HEAD_DIM)
        keys = []
        values = []
        for side, kv_ref in zip(sides, kv_refs):
            key = kv_ref[:, at]
            if side is not None:
                key = (key.astype(F32) + embed_ref[side : side + 1, at]).astype(BF16)
            keys.append(key)
            values.append(with_ones(kv_ref[:, value_at]))
        for block in range(2):
            here = slice(block * rows, (block + 1) * rows)
            query = q_ref[here, at]
            scores = [dot_nt(query, key) for key in keys]
            top = jnp.max(functools.reduce(jnp.maximum, scores), axis=-1, keepdims=True)
            acc = 0.0
            for score, value in zip(scores, values):
                acc = acc + dot_f32(jnp.exp2((score - top) * EXP2_SCALE).astype(BF16), value)
            acc_ref[here, at] = acc[:, :HEAD_DIM]
            total_ref[here, at] = acc[:, HEAD_DIM:]
            top_ref[here, at] = jnp.broadcast_to(top, (rows, HEAD_DIM))


def first_part(normed, w_query, embeds, views, sides):
    rows = 2 * normed[0].shape[0]
    inner, width = w_query.shape[1], w_query.shape[0]
    wide = jax.ShapeDtypeStruct((rows, inner), F32)
    return pl.pallas_call(
        functools.partial(first_kernel, sides),
        in_specs=[VMEM] * (4 + len(views)),
        out_specs=[VMEM] * 4,
        out_shape=[jax.ShapeDtypeStruct((rows, inner), BF16), wide, wide, wide],
        compiler_params=pltpu.CompilerParams(vmem_limit_bytes=12 * MIB),
        cost_estimate=pl.CostEstimate(
            flops=2 * rows * width * inner + 6 * rows * 256 * len(views) * inner,
            bytes_accessed=4 * MIB,
            transcendentals=rows * 256 * len(views) * HEADS,
        ),
        name="first_part",
    )(*normed, w_query, embeds, *views)


def last_kernel(
    q_ref, acc_ref, top_ref, total_ref, kv_ref, embed_ref, stream_a_ref, stream_b_ref, w_ref, o_ref, out_ref
):
    rows = stream_a_ref.shape[0]
    for block, stream_ref in enumerate((stream_a_ref, stream_b_ref)):
        here = slice(block * rows, (block + 1) * rows)
        for head in range(HEADS):
            at = columns(head)
            key = (kv_ref[:, at].astype(F32) + embed_ref[1:2, at]).astype(BF16)
            scores = dot_nt(q_ref[here, at], key)
            before = top_ref[here, at]
            top = jnp.maximum(before, jnp.max(scores, axis=-1, keepdims=True))
            keep = jnp.exp2((before - top) * EXP2_SCALE)
            expo = jnp.exp2((scores - jnp.concatenate([top, top], axis=1)) * EXP2_SCALE).astype(BF16)
            both = dot_f32(expo, with_ones(kv_ref[:, columns(HEADS + head)]))
            total = total_ref[here, at] * keep + both[:, HEAD_DIM:]
            acc = acc_ref[here, at] * keep + both[:, :HEAD_DIM]
            out_ref[here, at] = (acc / total).astype(BF16)
        product = dot_f32(out_ref[here, :], w_ref[...])
        o_ref[here, :] = (stream_ref[...].astype(F32) + product).astype(BF16)


def last_part(query, acc, top, total, view, embeds, streams, w_out):
    inner, width = w_out.shape
    rows = query.shape[0]
    return pl.pallas_call(
        last_kernel,
        in_specs=[VMEM] * 9,
        out_specs=VMEM,
        out_shape=jax.ShapeDtypeStruct((rows, width), BF16),
        scratch_shapes=[pltpu.VMEM((rows, inner), BF16)],
        compiler_params=pltpu.CompilerParams(vmem_limit_bytes=8 * MIB),
        cost_estimate=pl.CostEstimate(
            flops=2 * rows * width * inner + 6 * rows * view.shape[0] * inner,
            bytes_accessed=4 * MIB,
            transcendentals=rows * view.shape[0] * HEADS,
        ),
        name="last_part",
    )(query, acc, top, total, view, embeds, *streams, w_out)


def shards(
    hidden,
    t_query,
    t_key,
    t_value,
    frame_offsets,
    cycle_sides,
    w_temporal_out,
    norm_gain,
    w_query,
    w_key,
    w_value,
    w_cross_out,
    side_embed,
):
    rows_here = hidden.shape[2]
    model_width = hidden.shape[3]
    inner = t_query.shape[3]
    frames = lax.axis_size("frame")
    half = rows_here // 2
    group = half // frames
    hidden = hidden.reshape(rows_here, model_width)
    t_query = t_query.reshape(rows_here, inner)
    t_key = t_key.reshape(rows_here, inner)
    t_value = t_value.reshape(rows_here, inner)
    gain = norm_gain
    offsets = jnp.broadcast_to(frame_offsets.astype(F32)[:, None], (frames, HEAD_DIM))

    def exchange(value):
        return lax.all_to_all(value, "frame", split_axis=0, concat_axis=0, tiled=True)

    def to_near(value):
        return lax.ppermute(value, "cam", [(0, 1), (1, 0), (2, 3), (3, 2)])

    def to_far(value):
        return lax.ppermute(value, "cam", [(0, 3), (3, 0), (1, 2), (2, 1)])

    packed_a, cosine, sine = pack(t_query, t_key, t_value, offsets, rotary_frequencies())
    got_a = exchange(packed_a)
    weights = (w_temporal_out, gain, w_key, w_value)
    got_b = exchange(temporal(got_a, cosine, sine, group, [t_query, t_key, t_value]))
    stream_a, normed_a, kv_a = project_first(got_b, 3 * inner, hidden, *weights)
    far_a = to_far(kv_a)
    near_a = to_near(kv_a)
    got_b, kv_a = lax.optimization_barrier((got_b, kv_a))
    back_b = exchange(temporal(got_b, cosine, sine, group, []))
    stream_b, normed_b, kv_b = project_second(back_b, hidden, *weights)
    far_b = to_far(kv_b)
    near_b = to_near(kv_b)
    stream_b, cycle_sides, side_embed = lax.optimization_barrier((stream_b, cycle_sides, side_embed))
    near_cam = lax.axis_index("cam") ^ 1
    near_left = cycle_sides[0, 0] == near_cam
    side_f = side_embed.astype(F32)
    embeds = jnp.where(near_left, side_f, side_f[::-1])
    query, acc, top, total = first_part(
        [normed_a, normed_b], w_query, embeds, [kv_a, kv_b, near_a, near_b, far_a], (None, None, 0, 0, 1)
    )
    mixed = last_part(query, acc, top, total, far_b, embeds, [stream_a, stream_b], w_cross_out)
    return mixed.reshape(1, 1, rows_here, model_width)


def solution(mesh):
    in_specs = (
        P("cam", "frame", None, None),
        P("cam", "frame", None, None),
        P("cam", "frame", None, None),
        P("cam", "frame", None, None),
        P(),
        P("cam", None),
        P(),
        P(),
        P(),
        P(),
        P(),
        P(),
        P(),
    )
    out_specs = P("cam", "frame", None, None)
    return jax.shard_map(shards, mesh=mesh, in_specs=in_specs, out_specs=out_specs, check_vma=False)
```

time: 196 us -> 141 us (0.72)
  waiting for transfers between devices: 92.7 us -> 12.8 us
  blocking collectives: 0 us -> 62.7 us
  matrix products: 49.8 us -> 0 us
  Pallas kernels: 0 us -> 41.7 us
  starting transfers between devices: 29.4 us -> 16.9 us
  other arithmetic: 11.2 us -> 0.75 us
  local copies, waits for them, and re-layouts: 10.2 us -> 5.91 us
  between operations: 2.24 us -> 0.19 us
    all_to_all x0 -> x2, blocking collectives: none -> 62.7 us  [exchange(): lax.all_to_all(value, 'frame', split_axis=0, concat_axis=0, tiled=True)]
    all_to_all x4 -> x1, waiting for transfers between devices: 55.5 us -> 5 us  [exchange(): lax.all_to_all(value, 'frame', split_axis=0, concat_axis=0, tiled=True)]
    pallas_call x0 -> x7, Pallas kernels: none -> 41.7 us  [the longest x1 16 us: first_part(): pl.pallas_call(functools.partial(first_kernel, sides), in_specs=[VMEM] *...]
    dot_general x7 -> x0, matrix products: 36.7 us -> none  [the longest x1 12.4 us: shards(): jnp.einsum('hqk,khd->qhd', weights_c, vals_all, preferred_element_type=jn...]
    ppermute x2 -> x4, waiting for transfers between devices: 37.3 us -> 7.8 us  [the longest x2 7.79 us: to_far(): return lax.ppermute(value, 'cam', [(0, 3), (3, 0), (1, 2), (2, 1)])]
    all_to_all x4 -> x1, starting transfers between devices: 23.5 us -> 4.71 us  [exchange(): lax.all_to_all(value, 'frame', split_axis=0, concat_axis=0, tiled=True)]
    sub x2 -> x0, matrix products: 13.1 us -> none  [softmax_rows(): expo = jnp.exp(scores - top_val)]
    ppermute x2 -> x4, starting transfers between devices: 5.96 us -> 12.2 us  [the longest x2 6.45 us: to_near(): return lax.ppermute(value, 'cam', [(0, 1), (1, 0), (2, 3), (3, 2)])]
  transfers between devices with their start and end apart: 6 -> 5, of which waited for: 6 -> 2; matrix products, arithmetic and copies ran while one was open for 8% -> 0% of each run, Pallas kernels for 0% -> 17%
where the time goes in v2:
time: 141 us
  blocking collectives  62.7 us (44%)
  Pallas kernels  41.7 us (30%)
  starting transfers between devices  16.9 us (12%)
  waiting for transfers between devices  12.8 us (9%)
  local copies, waits for them, and re-layouts  5.91 us (4%)
    all_to_all x2, blocking collectives, exchange(): lax.all_to_all(value, 'frame', split_axis=0, concat_axis=0, tiled=True)  62.7 us
    pallas_call x1, Pallas kernels, first_part(): pl.pallas_call(functools.partial(first_kernel, sides), in_specs=[VMEM] *...  16 us
    pallas_call x1, Pallas kernels, project_second(): pl.pallas_call(project_second_kernel, in_specs=[VMEM] * 2 + [HBM] * 4, ou...  7.9 us
    ppermute x2, waiting for transfers between devices, to_far(): return lax.ppermute(value, 'cam', [(0, 3), (3, 0), (1, 2), (2, 1)])  7.79 us
    ppermute x2, starting transfers between devices, to_near(): return lax.ppermute(value, 'cam', [(0, 1), (1, 0), (2, 3), (3, 2)])  6.45 us
    pallas_call x2, Pallas kernels, temporal(): pl.pallas_call(functools.partial(temporal_kernel, group), in_specs=[VMEM]...  5.98 us
    pallas_call x1, Pallas kernels, last_part(): pl.pallas_call(last_kernel, in_specs=[VMEM] * 9, out_specs=VMEM, out_shap...  5.78 us
    ppermute x2, starting transfers between devices, to_far(): return lax.ppermute(value, 'cam', [(0, 3), (3, 0), (1, 2), (2, 1)])  5.7 us
  transfers between devices with their start and end apart: 5, of which 2 were waited for; matrix products, arithmetic and copies ran while one was open for 0% of the time, Pallas kernels for 17%

profile of v2, /device:TPU:1, one launch (start us, length us, event | category | flops | bytes accessed | tf_op | source)
XLA Modules:
  0.0 140.9 jit_solution(16363674668467569621)
XLA Ops:
  0.0 0.7 convert_element_type.11
  0.7 0.1 maximum_bitcast_fusion.frequency_ref
  0.7 0.1 broadcast_in_dim.4.offset_ref
  0.8 1.4 pack.1
  2.2 31.9 %all_to_all.33 = bf16[32,8,3072]{2,1,0:T(8,128)(2,1)S(1)} all-to-all(bf16[32,8,3072]{2,1,0:T(8,128)(2,1)S(1)} %bitcast.21), channel_id=1, replica_groups=mesh['cam'=4,'frame'=32] {'frame'}, dimensions={0} | all-to-all | bytes 3145728 | tf_op jit(solution)/shard_map/all_to_all | solution.py:394
  34.2 0.0 copy-start.1
  34.2 0.0 copy-start.2
  34.2 0.0 copy-start.3
  34.2 0.0 copy-start.6
  34.2 2.6 %temporal.2 = bf16[256,4096]{1,0:T(8,128)(2,1)S(1)} custom-call(bf16[256,3072]{1,0:T(8,128)(2,1)S(1)} %bitcast.22, f32[256,128]{1,0:T(8,128)S(1)} %get-tuple-element.24.cos_ref, f32[256,128]{1,0:T(8,128)S(1)} %get-tuple-element.25.sin_ref, bf16[512,1024]{1,0:T(8,128)(2,1)} %bitcast.24, bf16[512,1024]{1,0:T(8,128)(2,1)} %bitcast.26, bf16[512,1024]{1,0:T(8,128)(2,1)} %bitcast.28), custom_call_target="tpu_custom_call" | custom-call | flops 20000000000 | bytes 1 | tf_op jit(solution)/shard_map/temporal/pallas_call | solution.py:137
  36.8 0.0 copy-start
  36.8 30.7 %all_to_all.34 = bf16[32,8,4096]{2,1,0:T(8,128)(2,1)S(1)} all-to-all(bf16[32,8,4096]{2,1,0:T(8,128)(2,1)S(1)} %bitcast.20), channel_id=1, replica_groups=mesh['cam'=4,'frame'=32] {'frame'}, dimensions={0} | all-to-all | bytes 4194304 | tf_op jit(solution)/shard_map/all_to_all | solution.py:394
  67.5 0.0 copy-done.1
  67.5 0.0 copy-done.2
  67.6 0.0 copy-done.3
  67.6 0.0 copy-done.6
  67.6 0.0 copy-done
  67.6 4.6 %project_first.1 = (bf16[256,2048]{1,0:T(8,128)(2,1)}, bf16[256,2048]{1,0:T(8,128)(2,1)}, bf16[256,2048]{1,0:T(8,128)(2,1)}) custom-call(bf16[256,4096]{1,0:T(8,128)(2,1)S(1)} %bitcast.15, bf16[512,2048]{1,0:T(8,128)(2,1)S(1)} %bitcast.18, bf16[1024,2048]{1,0:T(8,128)(2,1)S(1)} %copy-done, bf16[2048]{0:T(1024)(128)(2,1)S(1)} %copy-done.6, ...), custom_call_target="tpu_custom_call" | custom-call | flops 1 | bytes 1 | tf_op jit(solution)/shard_map/project_first/pallas_call | solution.py:208
  72.2 3.4 %temporal.3 = bf16[256,1024]{1,0:T(8,128)(2,1)} custom-call(bf16[256,4096]{1,0:T(8,128)(2,1)S(1)} %bitcast.16, f32[256,128]{1,0:T(8,128)S(1)} %get-tuple-element.24.cos_ref, f32[256,128]{1,0:T(8,128)S(1)} %get-tuple-element.25.sin_ref), custom_call_target="tpu_custom_call" | custom-call | flops 1 | bytes 1 | tf_op jit(solution)/shard_map/temporal/pallas_call | solution.py:137
  75.6 4.7 %all-to-all-start.2 = ((bf16[32,8,1024]{2,1,0:T(8,128)(2,1)}), bf16[32,8,1024]{2,1,0:T(8,128)(2,1)S(1)}, u32[]{:S(2)}, u32[]{:S(2)}) async-start(bf16[32,8,1024]{2,1,0:T(8,128)(2,1)} %bitcast.9), calls=%async_computation.2 | async-start | bytes 1048576 | tf_op jit(solution)/shard_map/all_to_all | solution.py:394
  80.3 2.4 %collective-permute-start = (bf16[256,2048]{1,0:T(8,128)(2,1)}, bf16[256,2048]{1,0:T(8,128)(2,1)}, u32[]{:S(2)}, u32[]{:S(2)}) collective-permute-start(bf16[256,2048]{1,0:T(8,128)(2,1)} %get-tuple-element.33.refs_4_), channel_id=1, source_target_pairs={{0,32},{32,0},{64,96},{96,64},{1,33},{33,1},{65,97},{97,65},{2,34}... | collective-permute-start | bytes 3145736 | tf_op jit(solution)/shard_map/ppermute | solution.py:397
  82.7 2.6 %collective-permute-start.2 = (bf16[256,2048]{1,0:T(8,128)(2,1)}, bf16[256,2048]{1,0:T(8,128)(2,1)}, u32[]{:S(2)}, u32[]{:S(2)}) collective-permute-start(bf16[256,2048]{1,0:T(8,128)(2,1)} %get-tuple-element.33.refs_4_), channel_id=1, source_target_pairs={{0,96},{96,0},{32,64},{64,32},{1,97},{97,1},{33,65},{65,33},{2,98}... | collective-permute-start | bytes 3145736 | tf_op jit(solution)/shard_map/ppermute | solution.py:400
  85.3 5.0 %all-to-all-done.2 = bf16[32,8,1024]{2,1,0:T(8,128)(2,1)S(1)} async-done(((bf16[32,8,1024]{2,1,0:T(8,128)(2,1)}), bf16[32,8,1024]{2,1,0:T(8,128)(2,1)S(1)}, u32[]{:S(2)}, u32[]{:S(2)}) %all-to-all-start.2) | async-done | bytes 524320 | tf_op jit(solution)/shard_map/all_to_all | solution.py:394
  90.3 0.0 copy-start.11
  90.3 0.0 copy-start.12
  90.3 7.9 %project_second.1 = (bf16[256,2048]{1,0:T(8,128)(2,1)S(1)}, bf16[256,2048]{1,0:T(8,128)(2,1)S(1)}, bf16[256,2048]{1,0:T(8,128)(2,1)}) custom-call(bf16[256,1024]{1,0:T(8,128)(2,1)S(1)} %bitcast.19, bf16[2048]{0:T(1024)(128)(2,1)S(1)} %copy-done.6, bf16[512,2048]{1,0:T(8,128)(2,1)} %bitcast.17, bf16[1024,2048]{1,0:T(8,128)(2,1)} %refs_0_.1, ...), custom_call_target="tpu_custom_call" | custom-call | flops 1 | bytes 1 | tf_op jit(solution)/shard_map/project_second/pallas_call | solution.py:253
  98.2 0.0 copy-start.9
  98.2 1.0 copy-done.9
  99.2 4.1 %collective-permute-start.1 = (bf16[256,2048]{1,0:T(8,128)(2,1)}, bf16[256,2048]{1,0:T(8,128)(2,1)}, u32[]{:S(2)}, u32[]{:S(2)}) collective-permute-start(bf16[256,2048]{1,0:T(8,128)(2,1)} %get-tuple-element.34.refs_5_), channel_id=1, source_target_pairs={{0,32},{32,0},{64,96},{96,64},{1,33},{33,1},{65,97},{97,65},{2,34}... | collective-permute-start | bytes 3145736 | tf_op jit(solution)/shard_map/ppermute | solution.py:397
  103.3 3.1 %collective-permute-start.3 = (bf16[256,2048]{1,0:T(8,128)(2,1)}, bf16[256,2048]{1,0:T(8,128)(2,1)S(1)}, u32[]{:S(2)}, u32[]{:S(2)}) collective-permute-start(bf16[256,2048]{1,0:T(8,128)(2,1)} %get-tuple-element.34.refs_5_), channel_id=1, source_target_pairs={{0,96},{96,0},{32,64},{64,32},{1,97},{97,1},{33,65},{65,33},{2,98}... | collective-permute-start | bytes 3145736 | tf_op jit(solution)/shard_map/ppermute | solution.py:400
  106.3 0.0 copy-done.11
  106.3 0.2 rev.3
  106.6 0.0 copy-done.12
  106.6 0.0 collective-permute-done.refs_6_
  106.6 7.8 %collective-permute-done.2.refs_8_ = bf16[256,2048]{1,0:T(8,128)(2,1)} collective-permute-done((bf16[256,2048]{1,0:T(8,128)(2,1)}, bf16[256,2048]{1,0:T(8,128)(2,1)}, u32[]{:S(2)}, u32[]{:S(2)}) %collective-permute-start.2) | collective-permute-done | bytes 1048608 | tf_op jit(solution)/shard_map/ppermute | solution.py:400
  114.4 0.0 collective-permute-done.1.refs_7_
  114.4 0.0 copy-start.7
  114.4 2.2 %copy-done.7 = bf16[2048,1024]{1,0:T(8,128)(2,1)S(1)} copy-done((bf16[2048,1024]{1,0:T(8,128)(2,1)S(1)}, bf16[2048,1024]{1,0:T(8,128)(2,1)}, u32[]{:S(2)}) %copy-start.7) | copy-done | bytes 4194328
  116.6 0.0 copy-start.8
  116.6 1.2 copy-done.8
  117.8 0.0 copy-start.10
  117.8 1.2 copy-done.10
  119.1 0.0 copy-start.4
  119.1 0.0 copy-start.5
  119.1 16.0 %first_part.1 = (bf16[512,1024]{1,0:T(8,128)(2,1)S(1)}, f32[512,1024]{1,0:T(8,128)S(1)}, f32[512,1024]{1,0:T(8,128)S(1)}, f32[512,1024]{1,0:T(8,128)S(1)}) custom-call(bf16[256,2048]{1,0:T(8,128)(2,1)S(1)} %copy-done.8, bf16[256,2048]{1,0:T(8,128)(2,1)S(1)} %copy-done.10, bf16[2048,1024]{1,0:T(8,128)(2,1)S(1)} %copy-done.7, ...), custom_call_target="tpu_custom_call" | custom-call | flops 6174015488 | bytes 4194304 | tf_op jit(solution)/shard_map/first_part/pallas_call | solution.py:309
  135.1 0.0 collective-permute-done.3.kv_ref
  135.1 0.0 copy-done.4
  135.1 0.0 copy-done.5
  135.1 5.8 %last_part.1 = bf16[512,2048]{1,0:T(8,128)(2,1)} custom-call(bf16[512,1024]{1,0:T(8,128)(2,1)S(1)} %get-tuple-element.35.q_ref, f32[512,1024]{1,0:T(8,128)S(1)} %get-tuple-element.36.acc_ref, f32[512,1024]{1,0:T(8,128)S(1)} %get-tuple-element.37.top_ref, f32[512,1024]{1,0:T(8,128)S(1)} %get-tuple-element.38.total_ref, ...), custom_call_target="tpu_custom_call" | custom-call | flops 2952790016 | bytes 4194304 | tf_op jit(solution)/shard_map/last_part/pallas_call | solution.py:349
  (2 shorter events, 0.0 us)
Async XLA Ops:
  34.2 33.4 %copy-start.1 = (bf16[2048,1024]{1,0:T(8,128)(2,1)S(1)}, bf16[2048,1024]{1,0:T(8,128)(2,1)}, u32[]{:S(2)}) copy-start(bf16[2048,1024]{1,0:T(8,128)(2,1)} %refs_1_.1) | copy-start | bytes 12582916
  34.2 33.4 %copy-start.2 = (bf16[2048,1024]{1,0:T(8,128)(2,1)S(1)}, bf16[2048,1024]{1,0:T(8,128)(2,1)}, u32[]{:S(2)}) copy-start(bf16[2048,1024]{1,0:T(8,128)(2,1)} %refs_2_.2) | copy-start | bytes 12582916
  34.2 33.4 %copy-start.3 = (bf16[1,1,512,2048]{3,2,1,0:T(8,128)(2,1)S(1)}, bf16[1,1,512,2048]{3,2,1,0:T(8,128)(2,1)}, u32[]{:S(2)}) copy-start(bf16[1,1,512,2048]{3,2,1,0:T(8,128)(2,1)} %param.13) | copy-start | bytes 6291460
  34.2 33.4 %copy-start.6 = (bf16[2048]{0:T(1024)(128)(2,1)S(1)}, bf16[2048]{0:T(1024)(128)(2,1)}, u32[]{:S(2)}) copy-start(bf16[2048]{0:T(1024)(128)(2,1)} %gain_ref.3) | copy-start | bytes 12292
  36.8 30.8 %copy-start = (bf16[1024,2048]{1,0:T(8,128)(2,1)S(1)}, bf16[1024,2048]{1,0:T(8,128)(2,1)}, u32[]{:S(2)}) copy-start(bf16[1024,2048]{1,0:T(8,128)(2,1)} %refs_0_.1) | copy-start | bytes 12582916
  75.6 14.7 %all-to-all-start.2 = ((bf16[32,8,1024]{2,1,0:T(8,128)(2,1)}), bf16[32,8,1024]{2,1,0:T(8,128)(2,1)S(1)}, u32[]{:S(2)}, u32[]{:S(2)}) async-start(bf16[32,8,1024]{2,1,0:T(8,128)(2,1)} %bitcast.9), calls=%async_computation.2 | async-start | bytes 1048576 | tf_op jit(solution)/shard_map/all_to_all | solution.py:394
  80.3 26.3 %collective-permute-start = (bf16[256,2048]{1,0:T(8,128)(2,1)}, bf16[256,2048]{1,0:T(8,128)(2,1)}, u32[]{:S(2)}, u32[]{:S(2)}) collective-permute-start(bf16[256,2048]{1,0:T(8,128)(2,1)} %get-tuple-element.33.refs_4_), channel_id=1, source_target_pairs={{0,32},{32,0},{64,96},{96,64},{1,33},{33,1},{65,97},{97,65},{2,34}... | collective-permute-start | bytes 3145736 | tf_op jit(solution)/shard_map/ppermute | solution.py:397
  82.7 31.8 %collective-permute-start.2 = (bf16[256,2048]{1,0:T(8,128)(2,1)}, bf16[256,2048]{1,0:T(8,128)(2,1)}, u32[]{:S(2)}, u32[]{:S(2)}) collective-permute-start(bf16[256,2048]{1,0:T(8,128)(2,1)} %get-tuple-element.33.refs_4_), channel_id=1, source_target_pairs={{0,96},{96,0},{32,64},{64,32},{1,97},{97,1},{33,65},{65,33},{2,98}... | collective-permute-start | bytes 3145736 | tf_op jit(solution)/shard_map/ppermute | solution.py:400
  90.3 16.1 %copy-start.11 = (bf16[2,1024]{1,0:T(2,128)(2,1)S(1)}, bf16[2,1024]{1,0:T(2,128)(2,1)}, u32[]{:S(2)}) copy-start(bf16[2,1024]{1,0:T(2,128)(2,1)} %param.25) | copy-start | bytes 12292
  90.3 16.3 %copy-start.12 = (s32[1,2]{1,0:T(1,128)S(1)}, s32[1,2]{1,0:T(1,128)}, u32[]{:S(2)}) copy-start(s32[1,2]{1,0:T(1,128)} %param.18) | copy-start | bytes 28
  98.2 1.0 copy-start.9
  99.2 15.3 %collective-permute-start.1 = (bf16[256,2048]{1,0:T(8,128)(2,1)}, bf16[256,2048]{1,0:T(8,128)(2,1)}, u32[]{:S(2)}, u32[]{:S(2)}) collective-permute-start(bf16[256,2048]{1,0:T(8,128)(2,1)} %get-tuple-element.34.refs_5_), channel_id=1, source_target_pairs={{0,32},{32,0},{64,96},{96,64},{1,33},{33,1},{65,97},{97,65},{2,34}... | collective-permute-start | bytes 3145736 | tf_op jit(solution)/shard_map/ppermute | solution.py:397
  103.3 31.8 %collective-permute-start.3 = (bf16[256,2048]{1,0:T(8,128)(2,1)}, bf16[256,2048]{1,0:T(8,128)(2,1)S(1)}, u32[]{:S(2)}, u32[]{:S(2)}) collective-permute-start(bf16[256,2048]{1,0:T(8,128)(2,1)} %get-tuple-element.34.refs_5_), channel_id=1, source_target_pairs={{0,96},{96,0},{32,64},{64,32},{1,97},{97,1},{33,65},{65,33},{2,98}... | collective-permute-start | bytes 3145736 | tf_op jit(solution)/shard_map/ppermute | solution.py:400
  114.4 2.2 %copy-start.7 = (bf16[2048,1024]{1,0:T(8,128)(2,1)S(1)}, bf16[2048,1024]{1,0:T(8,128)(2,1)}, u32[]{:S(2)}) copy-start(bf16[2048,1024]{1,0:T(8,128)(2,1)} %refs_2_.3) | copy-start | bytes 12582916
  116.6 1.2 copy-start.8
  117.8 1.2 copy-start.10
  119.1 16.1 %copy-start.4 = (bf16[1024,2048]{1,0:T(8,128)(2,1)S(1)}, bf16[1024,2048]{1,0:T(8,128)(2,1)}, u32[]{:S(2)}) copy-start(bf16[1024,2048]{1,0:T(8,128)(2,1)} %w_ref.1) | copy-start | bytes 12582916
  119.1 16.1 %copy-start.5 = (bf16[256,2048]{1,0:T(8,128)(2,1)S(1)}, bf16[256,2048]{1,0:T(8,128)(2,1)}, u32[]{:S(2)}) copy-start(bf16[256,2048]{1,0:T(8,128)(2,1)} %get-tuple-element.39.stream_a_ref) | copy-start | bytes 3145732

commit v3 on v2

--- a/solution.py
+++ b/solution.py
@@ -97,15 +97,17 @@
 def temporal_kernel(group, packed_ref, cos_ref, sin_ref, *refs):
     rows = packed_ref.shape[0]
     inner = HEADS * HEAD_DIM
-    count = max(len(refs) - 2, 0)
+    count = len(refs) - 3 if len(refs) > 3 else 0
     first = 0
-    o_ref = refs[count]
     copies = []
-    if count:
+    if not count:
+        o_hbm, o_ref, sems = refs
+    else:
+        o_ref = refs[count]
         first = count * inner
         for i, ref in enumerate(refs[:count]):
             to = o_ref.at[:, i * inner : (i + 1) * inner]
-            copies.append(pltpu.make_async_copy(ref.at[rows:, :], to, refs[count + 1].at[i]))
+            copies.append(pltpu.make_async_copy(ref.at[rows:, :], to, refs[count + 2].at[i]))
             copies[-1].start()
     cosine = cos_ref[...]
     sine = sin_ref[...]
@@ -126,6 +128,10 @@
         both = dot_f32(expo, with_ones(value))
         result = both[:, :HEAD_DIM] / both[:, HEAD_DIM:]
         o_ref[:, first + head * HEAD_DIM : first + (head + 1) * HEAD_DIM] = result.astype(BF16)
+        if not count and head % 4 == 3:
+            at = slice((head - 3) * HEAD_DIM, (head + 1) * HEAD_DIM)
+            copies.append(pltpu.make_async_copy(o_ref.at[:, at], o_hbm.at[:, at], sems.at[head // 4]))
+            copies[-1].start()
     for copy in copies:
         copy.wait()
 
@@ -134,12 +140,13 @@
     rows = packed.shape[0]
     inner = HEADS * HEAD_DIM
     count = len(following)
+    shape = (rows, inner * (1 + count))
     return pl.pallas_call(
         functools.partial(temporal_kernel, group),
         in_specs=[VMEM] * 3 + [HBM] * count,
-        out_specs=VMEM,
-        out_shape=jax.ShapeDtypeStruct((rows, inner * (1 + count)), BF16),
-        scratch_shapes=[pltpu.SemaphoreType.DMA((3,))] if count else [],
+        out_specs=VMEM if count else HBM,
+        out_shape=jax.ShapeDtypeStruct(shape, BF16) if count else pltpu.HBM(shape, BF16),
+        scratch_shapes=[pltpu.VMEM((8, 128) if count else shape, BF16), pltpu.SemaphoreType.DMA((3,))],
         compiler_params=pltpu.CompilerParams(vmem_limit_bytes=6 * MIB),
         cost_estimate=pl.CostEstimate(
             flops=20_000_000_000 if count else 1, bytes_accessed=1, transcendentals=0
@@ -173,7 +180,7 @@
 
 
 def project_first_kernel(t_at, t_ref, hidden_ref, w_out_ref, gain_ref, w_key_ref, w_value_ref, *refs):
-    outs, scratch, sems = refs[:3], refs[3:6], refs[6]
+    outs, alone, scratch, sems = refs[:3], refs[3:5], refs[5:8], refs[8]
     rows = t_ref.shape[0]
     inner, width = w_out_ref.shape
     part = 512
@@ -185,6 +192,15 @@
         for i, at in enumerate(cuts)
     ]
 
+
+    def done(i):
+        copies[i].start()
+        if i >= 2:
+            j = i - 2
+            to = alone[j // (steps // 2)].at[:, cuts[j % (steps // 2)]]
+            copies.append(pltpu.make_async_copy(scratch[2].at[:, cuts[j]], to, sems.at[2 + steps + j]))
+            copies[-1].start()
+
     project_rows(
         t_ref.at[:, t_at : t_at + inner],
         hidden_ref.at[:rows, :],
@@ -194,7 +210,7 @@
         w_value_ref,
         *scratch,
         lambda i: None,
-        lambda i: copies[i].start(),
+        done,
     )
     for copy in copies:
         copy.wait()
@@ -208,10 +224,10 @@
     return pl.pallas_call(
         functools.partial(project_first_kernel, t_at),
         in_specs=[VMEM] * 6,
-        out_specs=[HBM] * 3,
-        out_shape=[pltpu.HBM(shape, BF16) for shape in shapes],
+        out_specs=[HBM] * 5,
+        out_shape=[pltpu.HBM(shape, BF16) for shape in shapes + [(rows, inner)] * 2],
         scratch_shapes=[pltpu.VMEM(shape, BF16) for shape in shapes]
-        + [pltpu.SemaphoreType.DMA((6,))],
+        + [pltpu.SemaphoreType.DMA((10,))],
         compiler_params=pltpu.CompilerParams(vmem_limit_bytes=10 * MIB),
         cost_estimate=pl.CostEstimate(flops=1, bytes_accessed=1, transcendentals=0),
         name="project_first",
@@ -219,7 +235,8 @@
 
 
 def project_second_kernel(t_ref, gain_ref, hidden_hbm, *refs):
-    w_hbm, outs, hidden_ref, w_refs, sems = refs[:3], refs[3:6], refs[6], refs[7:10], refs[10]
+    w_hbm, outs, hidden_ref, normed_ref, kv_ref = refs[:3], refs[3:6], refs[6], refs[7], refs[8]
+    w_refs, sems = refs[9:12], refs[12]
     rows = t_ref.shape[0]
     part = 512
     get_hidden = pltpu.make_async_copy(hidden_hbm.at[rows:, :], hidden_ref, sems.at[8])
@@ -230,6 +247,18 @@
             at = slice(i * part, (i + 1) * part)
             copies.append(pltpu.make_async_copy(a.at[:, at], b.at[:, at], sems.at[len(copies)]))
             copies[-1].start()
+    leaving = []
+
+    def done(i):
+        if i == 1:
+            leaving.append(pltpu.make_async_copy(normed_ref, outs[1], sems.at[13]))
+            leaving[-1].start()
+        if i >= 2:
+            at = slice((i - 2) * part, (i - 1) * part)
+            copy = pltpu.make_async_copy(kv_ref.at[:, at], outs[2].at[:, at], sems.at[7 + i])
+            leaving.append(copy)
+            copy.start()
+
     get_hidden.wait()
     project_rows(
         t_ref,
@@ -238,10 +267,14 @@
         gain_ref,
         w_refs[1],
         w_refs[2],
-        *outs,
+        outs[0],
+        normed_ref,
+        kv_ref,
         lambda i: copies[i].wait(),
-        lambda i: None,
+        done,
     )
+    for copy in leaving:
+        copy.wait()
 
 
 def project_second(t_out, hidden, w_out, gain, w_key, w_value):
@@ -253,42 +286,56 @@
     return pl.pallas_call(
         project_second_kernel,
         in_specs=[VMEM] * 2 + [HBM] * 4,
-        out_specs=[VMEM] * 3,
-        out_shape=[jax.ShapeDtypeStruct(shape, BF16) for shape in shapes],
+        out_specs=[VMEM] + [HBM] * 2,
+        out_shape=[jax.ShapeDtypeStruct(shapes[0], BF16)]
+        + [pltpu.HBM(shape, BF16) for shape in shapes[1:]],
         scratch_shapes=[pltpu.VMEM((rows, width), BF16)]
+        + [pltpu.VMEM(shape, BF16) for shape in shapes[1:]]
         + [pltpu.VMEM(w.shape, BF16) for w in weights]
-        + [pltpu.SemaphoreType.DMA((9,))],
-        compiler_params=pltpu.CompilerParams(vmem_limit_bytes=22 * MIB),
+        + [pltpu.SemaphoreType.DMA((14,))],
+        compiler_params=pltpu.CompilerParams(vmem_limit_bytes=24 * MIB),
         cost_estimate=pl.CostEstimate(flops=1, bytes_accessed=1, transcendentals=0),
         name="project_second",
     )(t_out, gain, *in_hbm(hidden, *weights))
 
 
-def first_kernel(sides, *refs):
-    count = len(sides)
-    normed_refs = refs[:2]
-    w_query_ref, embed_ref = refs[2:4]
-    kv_refs = refs[4 : 4 + count]
-    q_ref, acc_ref, top_ref, total_ref = refs[4 + count :]
-    inner = HEADS * HEAD_DIM
+def first_kernel(embed_ref, *refs):
+    from_hbm, (q_ref, acc_ref, top_ref, total_ref), held, sems = refs[:9], refs[9:13], refs[13:22], refs[22]
+    normed_refs, w_ref, own_and_near, (far_k_ref, far_v_ref) = held[:2], held[2], held[3:7], held[7:9]
     rows = normed_refs[0].shape[0]
-    for block, normed_ref in enumerate(normed_refs):
-        q_ref[block * rows : (block + 1) * rows, :] = dot_f32(
-            normed_ref[...], w_query_ref[...]
-        ).astype(BF16)
-
-    @pl.loop(0, HEADS)
-    def _(head):
-        at = pl.ds(pl.multiple_of(head * HEAD_DIM, HEAD_DIM), HEAD_DIM)
-        value_at = pl.ds(pl.multiple_of(inner + head * HEAD_DIM, HEAD_DIM), HEAD_DIM)
-        keys = []
-        values = []
-        for side, kv_ref in zip(sides, kv_refs):
-            key = kv_ref[:, at]
-            if side is not None:
-                key = (key.astype(F32) + embed_ref[side : side + 1, at]).astype(BF16)
-            keys.append(key)
-            values.append(with_ones(kv_ref[:, value_at]))
+    part = 256
+    parts = w_ref.shape[1] // part
+
+    def fetch(i):
+        copy = pltpu.make_async_copy(from_hbm[i], held[i], sems.at[i])
+        copy.start()
+        return copy
+
+    w_copies = []
+    arrivals = [fetch(0)]
+    for i in range(parts):
+        at = slice(i * part, (i + 1) * part)
+        w_copies.append(
+            pltpu.make_async_copy(from_hbm[2].at[:, at], w_ref.at[:, at], sems.at[9 + i])
+        )
+        w_copies[-1].start()
+    arrivals += [fetch(1)] + [fetch(i) for i in range(3, 9)]
+    arrivals[0].wait()
+    for i in range(parts):
+        at = slice(i * part, (i + 1) * part)
+        w_copies[i].wait()
+        q_ref[:rows, at] = dot_f32(normed_refs[0][...], w_ref[:, at]).astype(BF16)
+    arrivals[1].wait()
+    q_ref[rows:, :] = dot_f32(normed_refs[1][...], w_ref[...]).astype(BF16)
+    for copy in arrivals[2:]:
+        copy.wait()
+    for head in range(HEADS):
+        at = columns(head)
+        keys = [kv_ref[:, at] for kv_ref in own_and_near] + [far_k_ref[:, at]]
+        values = [kv_ref[:, columns(HEADS + head)] for kv_ref in own_and_near] + [far_v_ref[:, at]]
+        values = [with_ones(value) for value in values]
+        for i, side in ((2, 0), (3, 0), (4, 1)):
+            keys[i] = (keys[i].astype(F32) + embed_ref[side : side + 1, at]).astype(BF16)
         for block in range(2):
             here = slice(block * rows, (block + 1) * rows)
             query = q_ref[here, at]
@@ -302,23 +349,26 @@
             top_ref[here, at] = jnp.broadcast_to(top, (rows, HEAD_DIM))
 
 
-def first_part(normed, w_query, embeds, views, sides):
+def first_part(normed, w_query, embeds, own, near, far_key, far_value):
     rows = 2 * normed[0].shape[0]
     inner, width = w_query.shape[1], w_query.shape[0]
     wide = jax.ShapeDtypeStruct((rows, inner), F32)
+    fetched = [*normed, w_query, *own, *near, far_key, far_value]
     return pl.pallas_call(
-        functools.partial(first_kernel, sides),
-        in_specs=[VMEM] * (4 + len(views)),
+        first_kernel,
+        in_specs=[VMEM] + [HBM] * len(fetched),
         out_specs=[VMEM] * 4,
         out_shape=[jax.ShapeDtypeStruct((rows, inner), BF16), wide, wide, wide],
-        compiler_params=pltpu.CompilerParams(vmem_limit_bytes=12 * MIB),
+        scratch_shapes=[pltpu.VMEM(array.shape, BF16) for array in fetched]
+        + [pltpu.SemaphoreType.DMA((13,))],
+        compiler_params=pltpu.CompilerParams(vmem_limit_bytes=24 * MIB),
         cost_estimate=pl.CostEstimate(
-            flops=2 * rows * width * inner + 6 * rows * 256 * len(views) * inner,
+            flops=2 * rows * width * inner + 30 * rows * 256 * inner,
             bytes_accessed=4 * MIB,
-            transcendentals=rows * 256 * len(views) * HEADS,
+            transcendentals=rows * 256 * 5 * HEADS,
         ),
         name="first_part",
-    )(*normed, w_query, embeds, *views)
+    )(embeds, *in_hbm(*fetched))
 
 
 def last_kernel(
@@ -403,21 +453,29 @@
     got_a = exchange(packed_a)
     weights = (w_temporal_out, gain, w_key, w_value)
     got_b = exchange(temporal(got_a, cosine, sine, group, [t_query, t_key, t_value]))
-    stream_a, normed_a, kv_a = project_first(got_b, 3 * inner, hidden, *weights)
-    far_a = to_far(kv_a)
+    stream_a, normed_a, kv_a, key_a, value_a = project_first(got_b, 3 * inner, hidden, *weights)
+    far_key_a = to_far(key_a)
+    far_key_a, value_a = lax.optimization_barrier((far_key_a, value_a))
+    far_value_a = to_far(value_a)
     near_a = to_near(kv_a)
-    got_b, kv_a = lax.optimization_barrier((got_b, kv_a))
+    got_b, key_a = lax.optimization_barrier((got_b, key_a))
     back_b = exchange(temporal(got_b, cosine, sine, group, []))
     stream_b, normed_b, kv_b = project_second(back_b, hidden, *weights)
     far_b = to_far(kv_b)
     near_b = to_near(kv_b)
+    token = side_embed[:, :HEAD_DIM]
+    far_value_a, token = lax.optimization_barrier((far_value_a, token))
+    token = to_near(token)
+    token = to_near(token + 1)
     stream_b, cycle_sides, side_embed = lax.optimization_barrier((stream_b, cycle_sides, side_embed))
     near_cam = lax.axis_index("cam") ^ 1
     near_left = cycle_sides[0, 0] == near_cam
     side_f = side_embed.astype(F32)
     embeds = jnp.where(near_left, side_f, side_f[::-1])
+    embeds, token = lax.optimization_barrier((embeds, token))
+    embeds = embeds + 0.0 * token[:1, :1].astype(F32)
     query, acc, top, total = first_part(
-        [normed_a, normed_b], w_query, embeds, [kv_a, kv_b, near_a, near_b, far_a], (None, None, 0, 0, 1)
+        [normed_a, normed_b], w_query, embeds, [kv_a, kv_b], [near_a, near_b], far_key_a, far_value_a
     )
     mixed = last_part(query, acc, top, total, far_b, embeds, [stream_a, stream_b], w_cross_out)
     return mixed.reshape(1, 1, rows_here, model_width)

time: 141 us -> 138 us (0.979)
  waiting for transfers between devices: 12.8 us -> 21.2 us
  local copies, waits for them, and re-layouts: 5.91 us -> 0.32 us
  Pallas kernels: 41.7 us -> 38 us
  starting transfers between devices: 16.9 us -> 14.9 us
    ppermute x2 -> x3, waiting for transfers between devices: 7.79 us -> 16.1 us  [to_far(): return lax.ppermute(value, 'cam', [(0, 3), (3, 0), (1, 2), (2, 1)])]
    unnamed x26 -> x22, local copies, waits for them, and re-layouts: 5.64 us -> 0.05 us
    ppermute x2 -> x4, starting transfers between devices: 6.45 us -> 1.01 us  [to_near(): return lax.ppermute(value, 'cam', [(0, 1), (1, 0), (2, 3), (3, 2)])]
    ppermute x2 -> x3, starting transfers between devices: 5.7 us -> 9.96 us  [to_far(): return lax.ppermute(value, 'cam', [(0, 3), (3, 0), (1, 2), (2, 1)])]
    pallas_call x1, Pallas kernels: 16 us -> 12.5 us  [first_part(): pl.pallas_call(first_kernel, in_specs=[VMEM] + [HBM] * len(fetched), out_...]
  transfers between devices with their start and end apart: 5 -> 8, of which waited for: 2 -> 6; matrix products, arithmetic and copies ran while one was open for 0% -> 0% of each run, Pallas kernels for 17% -> 17%
where the time goes in v3:
time: 138 us
  blocking collectives  62.7 us (45%)
  Pallas kernels  38 us (28%)
  waiting for transfers between devices  21.2 us (15%)
  starting transfers between devices  14.9 us (11%)
    all_to_all x2, blocking collectives, exchange(): lax.all_to_all(value, 'frame', split_axis=0, concat_axis=0, tiled=True)  62.7 us
    ppermute x3, waiting for transfers between devices, to_far(): return lax.ppermute(value, 'cam', [(0, 3), (3, 0), (1, 2), (2, 1)])  16.1 us
    pallas_call x1, Pallas kernels, first_part(): pl.pallas_call(first_kernel, in_specs=[VMEM] + [HBM] * len(fetched), out_...  12.5 us
    ppermute x3, starting transfers between devices, to_far(): return lax.ppermute(value, 'cam', [(0, 3), (3, 0), (1, 2), (2, 1)])  9.96 us
    pallas_call x1, Pallas kernels, project_second(): pl.pallas_call(project_second_kernel, in_specs=[VMEM] * 2 + [HBM] * 4, ou...  7.73 us
    pallas_call x2, Pallas kernels, temporal(): pl.pallas_call(functools.partial(temporal_kernel, group), in_specs=[VMEM]...  5.92 us
    pallas_call x1, Pallas kernels, last_part(): pl.pallas_call(last_kernel, in_specs=[VMEM] * 9, out_specs=VMEM, out_shap...  5.81 us
    pallas_call x1, Pallas kernels, project_first(): pl.pallas_call(functools.partial(project_first_kernel, t_at), in_specs=[V...  4.66 us
  transfers between devices with their start and end apart: 8, of which 6 were waited for; matrix products, arithmetic and copies ran while one was open for 0% of the time, Pallas kernels for 17%

profile of v3, /device:TPU:1, one launch (start us, length us, event | category | flops | bytes accessed | tf_op | source)
XLA Modules:
  0.0 138.2 jit_solution(16237689818592797431)
XLA Ops:
  0.0 0.7 convert_element_type.14
  0.7 0.1 maximum_bitcast_fusion.frequency_ref
  0.7 0.1 broadcast_in_dim.4.offset_ref
  0.8 1.4 %pack.1 = (bf16[256,3072]{1,0:T(8,128)(2,1)S(1)}, f32[256,128]{1,0:T(8,128)S(1)}, f32[256,128]{1,0:T(8,128)S(1)}) custom-call(bf16[512,1024]{1,0:T(8,128)(2,1)} %bitcast.26, bf16[512,1024]{1,0:T(8,128)(2,1)} %bitcast.28, bf16[512,1024]{1,0:T(8,128)(2,1)} %bitcast.30, f32[32,128]{1,0:T(8,128)S(1)} %broadcast_in_dim.4.offset_ref, ...), custom_call_target="tpu_custom_call" | custom-call | bytes 3145728 | tf_op jit(solution)/shard_map/pack/pallas_call | solution.py:85
  2.2 31.9 %all_to_all.33 = bf16[32,8,3072]{2,1,0:T(8,128)(2,1)S(1)} all-to-all(bf16[32,8,3072]{2,1,0:T(8,128)(2,1)S(1)} %bitcast.23), channel_id=1, replica_groups=mesh['cam'=4,'frame'=32] {'frame'}, dimensions={0} | all-to-all | bytes 3145728 | tf_op jit(solution)/shard_map/all_to_all | solution.py:444
  34.2 0.0 copy-start.1
  34.2 0.0 copy-start.2
  34.2 0.0 copy-start.3
  34.2 0.0 copy-start.6
  34.2 2.6 %temporal.2 = bf16[256,4096]{1,0:T(8,128)(2,1)S(1)} custom-call(bf16[256,3072]{1,0:T(8,128)(2,1)S(1)} %bitcast.24, f32[256,128]{1,0:T(8,128)S(1)} %get-tuple-element.31.cos_ref, f32[256,128]{1,0:T(8,128)S(1)} %get-tuple-element.32.sin_ref, bf16[512,1024]{1,0:T(8,128)(2,1)} %bitcast.27, bf16[512,1024]{1,0:T(8,128)(2,1)} %bitcast.29, bf16[512,1024]{1,0:T(8,128)(2,1)} %bitcast.31), custom_call_target="tpu_custom_call" | custom-call | flops 20000000000 | bytes 1 | tf_op jit(solution)/shard_map/temporal/pallas_call | solution.py:144
  36.8 0.0 copy-start
  36.8 30.7 %all_to_all.34 = bf16[32,8,4096]{2,1,0:T(8,128)(2,1)S(1)} all-to-all(bf16[32,8,4096]{2,1,0:T(8,128)(2,1)S(1)} %bitcast.22), channel_id=1, replica_groups=mesh['cam'=4,'frame'=32] {'frame'}, dimensions={0} | all-to-all | bytes 4194304 | tf_op jit(solution)/shard_map/all_to_all | solution.py:444
  67.5 0.0 copy-done.1
  67.5 0.0 copy-done.2
  67.6 0.0 copy-done.3
  67.6 0.0 copy-done.6
  67.6 0.0 copy-done
  67.6 4.7 %project_first.1 = (bf16[256,2048]{1,0:T(8,128)(2,1)}, bf16[256,2048]{1,0:T(8,128)(2,1)}, bf16[256,2048]{1,0:T(8,128)(2,1)}, bf16[256,1024]{1,0:T(8,128)(2,1)}, bf16[256,1024]{1,0:T(8,128)(2,1)}) custom-call(bf16[256,4096]{1,0:T(8,128)(2,1)S(1)} %bitcast.17, bf16[512,2048]{1,0:T(8,128)(2,1)S(1)} %bitcast.20, bf16[1024,2048]{1,0:T(8,128)(2,1)S(1)} %copy-done, ...), custom_call_target="tpu_custom_call" | custom-call | flops 1 | bytes 1 | tf_op jit(solution)/shard_map/project_first/pallas_call | solution.py:224
  72.2 0.0 copy-start.8
  72.3 5.5 %collective-permute-start = (bf16[256,1024]{1,0:T(8,128)(2,1)}, bf16[256,1024]{1,0:T(8,128)(2,1)S(1)}, u32[]{:S(2)}, u32[]{:S(2)}) collective-permute-start(bf16[256,1024]{1,0:T(8,128)(2,1)} %get-tuple-element.33), channel_id=1, source_target_pairs={{0,96},{96,0},{32,64},{64,32},{1,97},{97,1},{33,65},{65,33},{2,98}... | collective-permute-start | bytes 1572872 | tf_op jit(solution)/shard_map/ppermute | solution.py:450
  77.8 3.3 %temporal.3 = bf16[256,1024]{1,0:T(8,128)(2,1)} custom-call(bf16[256,4096]{1,0:T(8,128)(2,1)S(1)} %bitcast.18, f32[256,128]{1,0:T(8,128)S(1)} %get-tuple-element.31.cos_ref, f32[256,128]{1,0:T(8,128)S(1)} %get-tuple-element.32.sin_ref), custom_call_target="tpu_custom_call" | custom-call | flops 1 | bytes 1 | tf_op jit(solution)/shard_map/temporal/pallas_call | solution.py:144
  81.1 3.9 %all-to-all-start.2 = ((bf16[32,8,1024]{2,1,0:T(8,128)(2,1)}), bf16[32,8,1024]{2,1,0:T(8,128)(2,1)S(1)}, u32[]{:S(2)}, u32[]{:S(2)}) async-start(bf16[32,8,1024]{2,1,0:T(8,128)(2,1)} %bitcast.25), calls=%async_computation.2 | async-start | bytes 1048576 | tf_op jit(solution)/shard_map/all_to_all | solution.py:444
  85.0 5.5 %collective-permute-done.refs_7_ = bf16[256,1024]{1,0:T(8,128)(2,1)S(1)} collective-permute-done((bf16[256,1024]{1,0:T(8,128)(2,1)}, bf16[256,1024]{1,0:T(8,128)(2,1)S(1)}, u32[]{:S(2)}, u32[]{:S(2)}) %collective-permute-start) | collective-permute-done | bytes 524320 | tf_op jit(solution)/shard_map/ppermute | solution.py:450
  90.5 0.0 copy-start.9
  90.5 3.2 %collective-permute-start.1 = (bf16[256,1024]{1,0:T(8,128)(2,1)}, bf16[256,1024]{1,0:T(8,128)(2,1)}, u32[]{:S(2)}, u32[]{:S(2)}) collective-permute-start(bf16[256,1024]{1,0:T(8,128)(2,1)} %get-tuple-element.39), channel_id=1, source_target_pairs={{0,96},{96,0},{32,64},{64,32},{1,97},{97,1},{33,65},{65,33},{2,98}... | collective-permute-start | bytes 1572872 | tf_op jit(solution)/shard_map/ppermute | solution.py:450
  93.8 0.0 copy-done.8
  93.8 0.0 collective-permute-start.4
  93.8 3.7 %all-to-all-done.2 = bf16[32,8,1024]{2,1,0:T(8,128)(2,1)S(1)} async-done(((bf16[32,8,1024]{2,1,0:T(8,128)(2,1)}), bf16[32,8,1024]{2,1,0:T(8,128)(2,1)S(1)}, u32[]{:S(2)}, u32[]{:S(2)}) %all-to-all-start.2) | async-done | bytes 524320 | tf_op jit(solution)/shard_map/all_to_all | solution.py:444
  97.5 0.0 copy-done.9
  97.5 0.0 copy-start.7
  97.5 0.0 copy-start.10
  97.5 7.7 %project_second.1 = (bf16[256,2048]{1,0:T(8,128)(2,1)S(1)}, bf16[256,2048]{1,0:T(8,128)(2,1)}, bf16[256,2048]{1,0:T(8,128)(2,1)}) custom-call(bf16[256,1024]{1,0:T(8,128)(2,1)S(1)} %bitcast.21, bf16[2048]{0:T(1024)(128)(2,1)S(1)} %copy-done.6, bf16[512,2048]{1,0:T(8,128)(2,1)} %bitcast.19, bf16[1024,2048]{1,0:T(8,128)(2,1)} %refs_0_.1, ...), custom_call_target="tpu_custom_call" | custom-call | flops 1 | bytes 1 | tf_op jit(solution)/shard_map/project_second/pallas_call | solution.py:286
  105.3 0.1 collective-permute-start.5
  105.4 0.0 copy-done.7
  105.4 1.2 collective-permute-start.6
  106.6 0.9 collective-permute-done.1.refs_8_
  107.5 0.6 collective-permute-start.2
  108.1 0.2 rev.3
  108.3 0.0 copy-done.10
  108.4 0.6 collective-permute-done.2
  108.9 0.3 collective-permute-start.3
  109.3 0.8 collective-permute-done.3
  110.1 0.0 collective-permute-done.4.refs_5_
  110.1 0.0 collective-permute-done.5.refs_6_
  110.1 0.0 copy-start.4
  110.2 0.0 copy-start.5
  110.2 12.5 %first_part.1 = (bf16[512,1024]{1,0:T(8,128)(2,1)S(1)}, f32[512,1024]{1,0:T(8,128)S(1)}, f32[512,1024]{1,0:T(8,128)S(1)}, f32[512,1024]{1,0:T(8,128)S(1)}) custom-call(f32[2,1024]{1,0:T(2,128)S(1)} %broadcast_add_fusion.embed_ref, bf16[256,2048]{1,0:T(8,128)(2,1)} %get-tuple-element.43.refs_0_, bf16[256,2048]{1,0:T(8,128)(2,1)} %get-tuple-element.44.refs_1_, ...), custom_call_target="tpu_custom_call" | custom-call | flops 6174015488 | bytes 4194304 | tf_op jit(solution)/shard_map/first_part/pallas_call | solution.py:357
  122.7 9.7 %collective-permute-done.6.kv_ref = bf16[256,2048]{1,0:T(8,128)(2,1)S(1)} collective-permute-done((bf16[256,2048]{1,0:T(8,128)(2,1)}, bf16[256,2048]{1,0:T(8,128)(2,1)S(1)}, u32[]{:S(2)}, u32[]{:S(2)}) %collective-permute-start.6) | collective-permute-done | bytes 1048608 | tf_op jit(solution)/shard_map/ppermute | solution.py:450
  132.4 0.0 copy-done.4
  132.4 0.0 copy-done.5
  132.4 5.8 %last_part.1 = bf16[512,2048]{1,0:T(8,128)(2,1)} custom-call(bf16[512,1024]{1,0:T(8,128)(2,1)S(1)} %get-tuple-element.49.q_ref, f32[512,1024]{1,0:T(8,128)S(1)} %get-tuple-element.50.acc_ref, f32[512,1024]{1,0:T(8,128)S(1)} %get-tuple-element.51.top_ref, f32[512,1024]{1,0:T(8,128)S(1)} %get-tuple-element.52.total_ref, ...), custom_call_target="tpu_custom_call" | custom-call | flops 2952790016 | bytes 4194304 | tf_op jit(solution)/shard_map/last_part/pallas_call | solution.py:399
  (5 shorter events, 0.0 us)
Async XLA Ops:
  34.2 33.4 %copy-start.1 = (bf16[2048,1024]{1,0:T(8,128)(2,1)S(1)}, bf16[2048,1024]{1,0:T(8,128)(2,1)}, u32[]{:S(2)}) copy-start(bf16[2048,1024]{1,0:T(8,128)(2,1)} %refs_1_.1) | copy-start | bytes 12582916
  34.2 33.4 %copy-start.2 = (bf16[2048,1024]{1,0:T(8,128)(2,1)S(1)}, bf16[2048,1024]{1,0:T(8,128)(2,1)}, u32[]{:S(2)}) copy-start(bf16[2048,1024]{1,0:T(8,128)(2,1)} %refs_2_.2) | copy-start | bytes 12582916
  34.2 33.4 %copy-start.3 = (bf16[1,1,512,2048]{3,2,1,0:T(8,128)(2,1)S(1)}, bf16[1,1,512,2048]{3,2,1,0:T(8,128)(2,1)}, u32[]{:S(2)}) copy-start(bf16[1,1,512,2048]{3,2,1,0:T(8,128)(2,1)} %param.13) | copy-start | bytes 6291460
  34.2 33.4 %copy-start.6 = (bf16[2048]{0:T(1024)(128)(2,1)S(1)}, bf16[2048]{0:T(1024)(128)(2,1)}, u32[]{:S(2)}) copy-start(bf16[2048]{0:T(1024)(128)(2,1)} %gain_ref.3) | copy-start | bytes 12292
  36.8 30.8 %copy-start = (bf16[1024,2048]{1,0:T(8,128)(2,1)S(1)}, bf16[1024,2048]{1,0:T(8,128)(2,1)}, u32[]{:S(2)}) copy-start(bf16[1024,2048]{1,0:T(8,128)(2,1)} %refs_0_.1) | copy-start | bytes 12582916
  72.2 21.5 %copy-start.8 = (bf16[256,2048]{1,0:T(8,128)(2,1)S(1)}, bf16[256,2048]{1,0:T(8,128)(2,1)}, u32[]{:S(2)}) copy-start(bf16[256,2048]{1,0:T(8,128)(2,1)} %get-tuple-element.45.refs_3_) | copy-start | bytes 3145732
  72.3 18.3 %collective-permute-start = (bf16[256,1024]{1,0:T(8,128)(2,1)}, bf16[256,1024]{1,0:T(8,128)(2,1)S(1)}, u32[]{:S(2)}, u32[]{:S(2)}) collective-permute-start(bf16[256,1024]{1,0:T(8,128)(2,1)} %get-tuple-element.33), channel_id=1, source_target_pairs={{0,96},{96,0},{32,64},{64,32},{1,97},{97,1},{33,65},{65,33},{2,98}... | collective-permute-start | bytes 1572872 | tf_op jit(solution)/shard_map/ppermute | solution.py:450
  81.1 16.4 %all-to-all-start.2 = ((bf16[32,8,1024]{2,1,0:T(8,128)(2,1)}), bf16[32,8,1024]{2,1,0:T(8,128)(2,1)S(1)}, u32[]{:S(2)}, u32[]{:S(2)}) async-start(bf16[32,8,1024]{2,1,0:T(8,128)(2,1)} %bitcast.25), calls=%async_computation.2 | async-start | bytes 1048576 | tf_op jit(solution)/shard_map/all_to_all | solution.py:444
  90.5 7.0 %copy-start.9 = (bf16[256,1024]{1,0:T(8,128)(2,1)}, bf16[256,1024]{1,0:T(8,128)(2,1)S(1)}, u32[]{:S(2)}) copy-start(bf16[256,1024]{1,0:T(8,128)(2,1)S(1)} %collective-permute-done.refs_7_) | copy-start | bytes 1572868
  90.5 17.0 %collective-permute-start.1 = (bf16[256,1024]{1,0:T(8,128)(2,1)}, bf16[256,1024]{1,0:T(8,128)(2,1)}, u32[]{:S(2)}, u32[]{:S(2)}) collective-permute-start(bf16[256,1024]{1,0:T(8,128)(2,1)} %get-tuple-element.39), channel_id=1, source_target_pairs={{0,96},{96,0},{32,64},{64,32},{1,97},{97,1},{33,65},{65,33},{2,98}... | collective-permute-start | bytes 1572872 | tf_op jit(solution)/shard_map/ppermute | solution.py:450
  93.8 16.3 %collective-permute-start.4 = (bf16[256,2048]{1,0:T(8,128)(2,1)S(1)}, bf16[256,2048]{1,0:T(8,128)(2,1)}, u32[]{:S(2)}, u32[]{:S(2)}) collective-permute-start(bf16[256,2048]{1,0:T(8,128)(2,1)S(1)} %copy-done.8), channel_id=1, source_target_pairs={{0,32},{32,0},{64,96},{96,64},{1,33},{33,1},{65,97},{97,65},{2,34}... | collective-permute-start | bytes 3145736 | tf_op jit(solution)/shard_map/ppermute | solution.py:447
  97.5 7.8 %copy-start.7 = (bf16[2,1024]{1,0:T(2,128)(2,1)S(1)}, bf16[2,1024]{1,0:T(2,128)(2,1)}, u32[]{:S(2)}) copy-start(bf16[2,1024]{1,0:T(2,128)(2,1)} %param.25) | copy-start | bytes 12292
  97.5 10.8 %copy-start.10 = (s32[1,2]{1,0:T(1,128)S(1)}, s32[1,2]{1,0:T(1,128)}, u32[]{:S(2)}) copy-start(s32[1,2]{1,0:T(1,128)} %param.18) | copy-start | bytes 28
  105.3 4.9 %collective-permute-start.5 = (bf16[256,2048]{1,0:T(8,128)(2,1)}, bf16[256,2048]{1,0:T(8,128)(2,1)}, u32[]{:S(2)}, u32[]{:S(2)}) collective-permute-start(bf16[256,2048]{1,0:T(8,128)(2,1)} %get-tuple-element.46.refs_4_), channel_id=1, source_target_pairs={{0,32},{32,0},{64,96},{96,64},{1,33},{33,1},{65,97},{97,65},{2,34}... | collective-permute-start | bytes 3145736 | tf_op jit(solution)/shard_map/ppermute | solution.py:447
  105.4 27.0 %collective-permute-start.6 = (bf16[256,2048]{1,0:T(8,128)(2,1)}, bf16[256,2048]{1,0:T(8,128)(2,1)S(1)}, u32[]{:S(2)}, u32[]{:S(2)}) collective-permute-start(bf16[256,2048]{1,0:T(8,128)(2,1)} %get-tuple-element.46.refs_4_), channel_id=1, source_target_pairs={{0,96},{96,0},{32,64},{64,32},{1,97},{97,1},{33,65},{65,33},{2,98}... | collective-permute-start | bytes 3145736 | tf_op jit(solution)/shard_map/ppermute | solution.py:450
  107.5 1.4 %collective-permute-start.2 = (bf16[2,128]{1,0:T(2,128)(2,1)S(1)}, bf16[2,128]{1,0:T(2,128)(2,1)S(1)}, u32[]{:S(2)}, u32[]{:S(2)}) collective-permute-start(bf16[2,128]{1,0:T(2,128)(2,1)S(1)} %slice.10), channel_id=1, source_target_pairs={{0,32},{32,0},{64,96},{96,64},{1,33},{33,1},{65,97},{97,65},{2,34}... | collective-permute-start | bytes 1544 | tf_op jit(solution)/shard_map/ppermute | solution.py:447
  108.9 1.1 collective-permute-start.3
  110.1 22.2 %copy-start.4 = (bf16[1024,2048]{1,0:T(8,128)(2,1)S(1)}, bf16[1024,2048]{1,0:T(8,128)(2,1)}, u32[]{:S(2)}) copy-start(bf16[1024,2048]{1,0:T(8,128)(2,1)} %w_ref.1) | copy-start | bytes 12582916
  110.2 22.2 %copy-start.5 = (bf16[256,2048]{1,0:T(8,128)(2,1)S(1)}, bf16[256,2048]{1,0:T(8,128)(2,1)}, u32[]{:S(2)}) copy-start(bf16[256,2048]{1,0:T(8,128)(2,1)} %get-tuple-element.53.stream_a_ref) | copy-start | bytes 3145732

commit v4 on v3

--- a/solution.py
+++ b/solution.py
@@ -22,6 +22,16 @@
 
 def dot_nt(a, b):
     return lax.dot_general(a, b, (((1,), (1,)), ((), ())), preferred_element_type=F32)
+
+
+FIRST_PIECE = 1536
+KV_CUTS = [slice(0, 512), slice(512, 1024), slice(1024, 1536), slice(1536, 2048)]
+
+
+def alone_part(refs, at, split):
+    second = at.start >= split
+    first = at.start - split * second
+    return refs[second].at[:, first : first + at.stop - at.start]
 
 
 def rotary_frequencies():
@@ -170,11 +180,10 @@
     scale = lax.rsqrt(squares / width + 1e-06)
     normed_ref[...] = (stream_ref[...].astype(F32) * scale * gain_ref[...].astype(F32).reshape(1, width)).astype(BF16)
     done(1)
-    for i in range(2 * inner // part):
-        at = slice(i * part, (i + 1) * part)
+    for i, at in enumerate(KV_CUTS):
         ready(width // part + i)
-        w_ref = w_key_ref if i < inner // part else w_value_ref
-        from_w = slice(i * part % inner, i * part % inner + part)
+        w_ref = w_key_ref if at.start < inner else w_value_ref
+        from_w = slice(at.start % inner, at.start % inner + at.stop - at.start)
         kv_ref[:, at] = dot_f32(normed_ref[...], w_ref[:, from_w]).astype(BF16)
         done(2 + i)
 
@@ -182,24 +191,20 @@
 def project_first_kernel(t_at, t_ref, hidden_ref, w_out_ref, gain_ref, w_key_ref, w_value_ref, *refs):
     outs, alone, scratch, sems = refs[:3], refs[3:5], refs[5:8], refs[8]
     rows = t_ref.shape[0]
-    inner, width = w_out_ref.shape
-    part = 512
-    steps = 2 * inner // part
-    cuts = [slice(i * part, (i + 1) * part) for i in range(steps)]
-    copies = [pltpu.make_async_copy(scratch[i], outs[i], sems.at[i]) for i in range(2)]
-    copies += [
-        pltpu.make_async_copy(scratch[2].at[:, at], outs[2].at[:, at], sems.at[2 + i])
-        for i, at in enumerate(cuts)
-    ]
-
+    inner = w_out_ref.shape[0]
+    copies = []
+
+    def leave(a, b):
+        copies.append(pltpu.make_async_copy(a, b, sems.at[len(copies)]))
+        copies[-1].start()
 
     def done(i):
-        copies[i].start()
-        if i >= 2:
-            j = i - 2
-            to = alone[j // (steps // 2)].at[:, cuts[j % (steps // 2)]]
-            copies.append(pltpu.make_async_copy(scratch[2].at[:, cuts[j]], to, sems.at[2 + steps + j]))
-            copies[-1].start()
+        if i < 2:
+            leave(scratch[i], outs[i])
+        else:
+            at = KV_CUTS[i - 2]
+            leave(scratch[2].at[:, at], alone_part(alone, at, inner))
+            leave(scratch[2].at[:, at], outs[2].at[:, at])
 
     project_rows(
         t_ref.at[:, t_at : t_at + inner],
@@ -227,7 +232,7 @@
         out_specs=[HBM] * 5,
         out_shape=[pltpu.HBM(shape, BF16) for shape in shapes + [(rows, inner)] * 2],
         scratch_shapes=[pltpu.VMEM(shape, BF16) for shape in shapes]
-        + [pltpu.SemaphoreType.DMA((10,))],
+        + [pltpu.SemaphoreType.DMA((12,))],
         compiler_params=pltpu.CompilerParams(vmem_limit_bytes=10 * MIB),
         cost_estimate=pl.CostEstimate(flops=1, bytes_accessed=1, transcendentals=0),
         name="project_first",
@@ -235,29 +240,36 @@
 
 
 def project_second_kernel(t_ref, gain_ref, hidden_hbm, *refs):
-    w_hbm, outs, hidden_ref, normed_ref, kv_ref = refs[:3], refs[3:6], refs[6], refs[7], refs[8]
-    w_refs, sems = refs[9:12], refs[12]
+    w_hbm, outs, alone, hidden_ref, normed_ref, kv_ref = refs[:3], refs[3:6], refs[6:8], *refs[8:11]
+    w_refs, arrived, left = refs[11:14], refs[14], refs[15]
     rows = t_ref.shape[0]
+    inner = HEADS * HEAD_DIM
     part = 512
-    get_hidden = pltpu.make_async_copy(hidden_hbm.at[rows:, :], hidden_ref, sems.at[8])
+    get_hidden = pltpu.make_async_copy(hidden_hbm.at[rows:, :], hidden_ref, arrived.at[9])
     get_hidden.start()
+    cuts = [(0, slice(i, i + part)) for i in range(0, w_hbm[0].shape[1], part)]
+    for at in KV_CUTS:
+        first = at.start % inner
+        cuts.append((1 + at.start // inner, slice(first, first + at.stop - at.start)))
     copies = []
-    for a, b in zip(w_hbm, w_refs):
-        for i in range(a.shape[1] // part):
-            at = slice(i * part, (i + 1) * part)
-            copies.append(pltpu.make_async_copy(a.at[:, at], b.at[:, at], sems.at[len(copies)]))
-            copies[-1].start()
+    for i, (which, at) in enumerate(cuts):
+        copies.append(
+            pltpu.make_async_copy(w_hbm[which].at[:, at], w_refs[which].at[:, at], arrived.at[i])
+        )
+        copies[-1].start()
     leaving = []
+
+    def leave(a, b):
+        leaving.append(pltpu.make_async_copy(a, b, left.at[len(leaving)]))
+        leaving[-1].start()
 
     def done(i):
         if i == 1:
-            leaving.append(pltpu.make_async_copy(normed_ref, outs[1], sems.at[13]))
-            leaving[-1].start()
+            leave(normed_ref, outs[1])
         if i >= 2:
-            at = slice((i - 2) * part, (i - 1) * part)
-            copy = pltpu.make_async_copy(kv_ref.at[:, at], outs[2].at[:, at], sems.at[7 + i])
-            leaving.append(copy)
-            copy.start()
+            at = KV_CUTS[i - 2]
+            leave(kv_ref.at[:, at], alone_part(alone, at, FIRST_PIECE))
+            leave(kv_ref.at[:, at], outs[2].at[:, at])
 
     get_hidden.wait()
     project_rows(
@@ -286,13 +298,16 @@
     return pl.pallas_call(
         project_second_kernel,
         in_specs=[VMEM] * 2 + [HBM] * 4,
-        out_specs=[VMEM] + [HBM] * 2,
+        out_specs=[VMEM] + [HBM] * 4,
         out_shape=[jax.ShapeDtypeStruct(shapes[0], BF16)]
-        + [pltpu.HBM(shape, BF16) for shape in shapes[1:]],
+        + [
+            pltpu.HBM(shape, BF16)
+            for shape in shapes[1:] + [(rows, FIRST_PIECE), (rows, 2 * inner - FIRST_PIECE)]
+        ],
         scratch_shapes=[pltpu.VMEM((rows, width), BF16)]
         + [pltpu.VMEM(shape, BF16) for shape in shapes[1:]]
         + [pltpu.VMEM(w.shape, BF16) for w in weights]
-        + [pltpu.SemaphoreType.DMA((14,))],
+        + [pltpu.SemaphoreType.DMA((10,)), pltpu.SemaphoreType.DMA((11,))],
         compiler_params=pltpu.CompilerParams(vmem_limit_bytes=24 * MIB),
         cost_estimate=pl.CostEstimate(flops=1, bytes_accessed=1, transcendentals=0),
         name="project_second",
@@ -362,54 +377,74 @@
         scratch_shapes=[pltpu.VMEM(array.shape, BF16) for array in fetched]
         + [pltpu.SemaphoreType.DMA((13,))],
         compiler_params=pltpu.CompilerParams(vmem_limit_bytes=24 * MIB),
-        cost_estimate=pl.CostEstimate(
-            flops=2 * rows * width * inner + 30 * rows * 256 * inner,
-            bytes_accessed=4 * MIB,
-            transcendentals=rows * 256 * 5 * HEADS,
-        ),
+        cost_estimate=pl.CostEstimate(flops=1, bytes_accessed=1, transcendentals=0),
         name="first_part",
     )(embeds, *in_hbm(*fetched))
 
 
-def last_kernel(
-    q_ref, acc_ref, top_ref, total_ref, kv_ref, embed_ref, stream_a_ref, stream_b_ref, w_ref, o_ref, out_ref
-):
-    rows = stream_a_ref.shape[0]
-    for block, stream_ref in enumerate((stream_a_ref, stream_b_ref)):
-        here = slice(block * rows, (block + 1) * rows)
-        for head in range(HEADS):
-            at = columns(head)
-            key = (kv_ref[:, at].astype(F32) + embed_ref[1:2, at]).astype(BF16)
+def weigh_kernel(q_ref, acc_ref, top_ref, total_ref, key_ref, embed_ref, keep_ref, inverse_ref, weight_ref):
+    half = key_ref.shape[0]
+    for head in range(HEADS):
+        at = columns(head)
+        key = (key_ref[:, at].astype(F32) + embed_ref[1:2, at]).astype(BF16)
+        for block in range(q_ref.shape[0] // half):
+            here = slice(block * half, (block + 1) * half)
             scores = dot_nt(q_ref[here, at], key)
             before = top_ref[here, at]
             top = jnp.maximum(before, jnp.max(scores, axis=-1, keepdims=True))
             keep = jnp.exp2((before - top) * EXP2_SCALE)
             expo = jnp.exp2((scores - jnp.concatenate([top, top], axis=1)) * EXP2_SCALE).astype(BF16)
-            both = dot_f32(expo, with_ones(kv_ref[:, columns(HEADS + head)]))
-            total = total_ref[here, at] * keep + both[:, HEAD_DIM:]
-            acc = acc_ref[here, at] * keep + both[:, :HEAD_DIM]
-            out_ref[here, at] = (acc / total).astype(BF16)
+            weight_ref[here, head * half : (head + 1) * half] = expo
+            total = dot_f32(expo, jnp.ones((half, HEAD_DIM), BF16)) + total_ref[here, at] * keep
+            inverse_ref[here, at] = 1.0 / total
+            keep_ref[here, at] = acc_ref[here, at] * keep
+
+
+def weigh(query, acc, top, total, key, embeds):
+    rows, inner = query.shape
+    wide = jax.ShapeDtypeStruct((rows, inner), F32)
+    return pl.pallas_call(
+        weigh_kernel,
+        in_specs=[VMEM] * 6,
+        out_specs=[VMEM] * 3,
+        out_shape=[wide, wide, jax.ShapeDtypeStruct((rows, HEADS * key.shape[0]), BF16)],
+        compiler_params=pltpu.CompilerParams(vmem_limit_bytes=6 * MIB),
+        cost_estimate=pl.CostEstimate(flops=1, bytes_accessed=1, transcendentals=0),
+        name="weigh",
+    )(query, acc, top, total, key, embeds)
+
+
+def last_kernel(acc_ref, inverse_ref, weight_ref, piece_a_ref, piece_b_ref, stream_a_ref, stream_b_ref, w_ref, o_ref, out_ref):
+    rows = stream_a_ref.shape[0]
+    keys = piece_a_ref.shape[0]
+    inner = HEADS * HEAD_DIM
+    for block, stream_ref in enumerate((stream_a_ref, stream_b_ref)):
+        here = slice(block * rows, (block + 1) * rows)
+        for head in range(HEADS):
+            at = columns(head)
+            weights = weight_ref[here, head * keys : (head + 1) * keys]
+            first = inner + head * HEAD_DIM
+            value_at = slice(first, first + HEAD_DIM)
+            value = alone_part((piece_a_ref, piece_b_ref), value_at, FIRST_PIECE)[...]
+            acc = acc_ref[here, at] + dot_f32(weights, value)
+            out_ref[here, at] = (acc * inverse_ref[here, at]).astype(BF16)
         product = dot_f32(out_ref[here, :], w_ref[...])
         o_ref[here, :] = (stream_ref[...].astype(F32) + product).astype(BF16)
 
 
-def last_part(query, acc, top, total, view, embeds, streams, w_out):
+def last_part(acc, inverse, weights, pieces, streams, w_out):
     inner, width = w_out.shape
-    rows = query.shape[0]
+    rows = acc.shape[0]
     return pl.pallas_call(
         last_kernel,
-        in_specs=[VMEM] * 9,
+        in_specs=[VMEM] * 8,
         out_specs=VMEM,
         out_shape=jax.ShapeDtypeStruct((rows, width), BF16),
         scratch_shapes=[pltpu.VMEM((rows, inner), BF16)],
         compiler_params=pltpu.CompilerParams(vmem_limit_bytes=8 * MIB),
-        cost_estimate=pl.CostEstimate(
-            flops=2 * rows * width * inner + 6 * rows * view.shape[0] * inner,
-            bytes_accessed=4 * MIB,
-            transcendentals=rows * view.shape[0] * HEADS,
-        ),
+        cost_estimate=pl.CostEstimate(flops=1, bytes_accessed=1, transcendentals=0),
         name="last_part",
-    )(query, acc, top, total, view, embeds, *streams, w_out)
+    )(acc, inverse, weights, *pieces, *streams, w_out)
 
 
 def shards(
@@ -460,8 +495,9 @@
     near_a = to_near(kv_a)
     got_b, key_a = lax.optimization_barrier((got_b, key_a))
     back_b = exchange(temporal(got_b, cosine, sine, group, []))
-    stream_b, normed_b, kv_b = project_second(back_b, hidden, *weights)
-    far_b = to_far(kv_b)
+    stream_b, normed_b, kv_b, piece_b, rest_b = project_second(back_b, hidden, *weights)
+    far_piece_b = to_far(piece_b)
+    far_rest_b = to_far(rest_b)
     near_b = to_near(kv_b)
     token = side_embed[:, :HEAD_DIM]
     far_value_a, token = lax.optimization_barrier((far_value_a, token))
@@ -477,7 +513,8 @@
     query, acc, top, total = first_part(
         [normed_a, normed_b], w_query, embeds, [kv_a, kv_b], [near_a, near_b], far_key_a, far_value_a
     )
-    mixed = last_part(query, acc, top, total, far_b, embeds, [stream_a, stream_b], w_cross_out)
+    acc, inverse, last_weights = weigh(query, acc, top, total, far_piece_b, embeds)
+    mixed = last_part(acc, inverse, last_weights, [far_piece_b, far_rest_b], [stream_a, stream_b], w_cross_out)
     return mixed.reshape(1, 1, rows_here, model_width)
 
 

time: 138 us -> 137 us (level)
  waiting for transfers between devices: 21.2 us -> 18.2 us
    ppermute x3 -> x4, waiting for transfers between devices: 16.1 us -> 13.4 us  [to_far(): return lax.ppermute(value, 'cam', [(0, 3), (3, 0), (1, 2), (2, 1)])]
    ppermute x3 -> x4, starting transfers between devices: 9.96 us -> 11.3 us  [to_far(): return lax.ppermute(value, 'cam', [(0, 3), (3, 0), (1, 2), (2, 1)])]
    pallas_call x1 -> x2, Pallas kernels: 5.81 us -> 6.23 us  [the longest x1 4.19 us: last_part(): pl.pallas_call(last_kernel, in_specs=[VMEM] * 8, out_specs=VMEM, out_shap...]
  transfers between devices with their start and end apart: 8 -> 9, of which waited for: 6 -> 6; matrix products, arithmetic and copies ran while one was open for 0% -> 0% of each run, Pallas kernels for 17% -> 19%
where the time goes in v4:
time: 137 us
  blocking collectives  62.7 us (46%)
  Pallas kernels  38.5 us (28%)
  waiting for transfers between devices  18.2 us (13%)
  starting transfers between devices  16.1 us (12%)
    all_to_all x2, blocking collectives, exchange(): lax.all_to_all(value, 'frame', split_axis=0, concat_axis=0, tiled=True)  62.7 us
    ppermute x4, waiting for transfers between devices, to_far(): return lax.ppermute(value, 'cam', [(0, 3), (3, 0), (1, 2), (2, 1)])  13.4 us
    pallas_call x1, Pallas kernels, first_part(): pl.pallas_call(first_kernel, in_specs=[VMEM] + [HBM] * len(fetched), out_...  12.3 us
    ppermute x4, starting transfers between devices, to_far(): return lax.ppermute(value, 'cam', [(0, 3), (3, 0), (1, 2), (2, 1)])  11.3 us
    pallas_call x1, Pallas kernels, project_second(): pl.pallas_call(project_second_kernel, in_specs=[VMEM] * 2 + [HBM] * 4, ou...  7.86 us
    pallas_call x2, Pallas kernels, temporal(): pl.pallas_call(functools.partial(temporal_kernel, group), in_specs=[VMEM]...  5.93 us
    pallas_call x1, Pallas kernels, project_first(): pl.pallas_call(functools.partial(project_first_kernel, t_at), in_specs=[V...  4.71 us
    pallas_call x1, Pallas kernels, last_part(): pl.pallas_call(last_kernel, in_specs=[VMEM] * 8, out_specs=VMEM, out_shap...  4.19 us
  transfers between devices with their start and end apart: 9, of which 6 were waited for; matrix products, arithmetic and copies ran while one was open for 0% of the time, Pallas kernels for 19%

profile of v4, /device:TPU:1, one launch (start us, length us, event | category | flops | bytes accessed | tf_op | source)
XLA Modules:
  0.0 136.7 jit_solution(18074874536516596679)
XLA Ops:
  0.0 0.7 convert_element_type.14
  0.7 0.1 maximum_bitcast_fusion.frequency_ref
  0.7 0.1 broadcast_in_dim.4.offset_ref
  0.8 1.4 %pack.1 = (bf16[256,3072]{1,0:T(8,128)(2,1)S(1)}, f32[256,128]{1,0:T(8,128)S(1)}, f32[256,128]{1,0:T(8,128)S(1)}) custom-call(bf16[512,1024]{1,0:T(8,128)(2,1)} %bitcast.26, bf16[512,1024]{1,0:T(8,128)(2,1)} %bitcast.28, bf16[512,1024]{1,0:T(8,128)(2,1)} %bitcast.30, f32[32,128]{1,0:T(8,128)S(1)} %broadcast_in_dim.4.offset_ref, ...), custom_call_target="tpu_custom_call" | custom-call | bytes 3145728 | tf_op jit(solution)/shard_map/pack/pallas_call | solution.py:95
  2.2 31.9 %all_to_all.33 = bf16[32,8,3072]{2,1,0:T(8,128)(2,1)S(1)} all-to-all(bf16[32,8,3072]{2,1,0:T(8,128)(2,1)S(1)} %bitcast.23), channel_id=1, replica_groups=mesh['cam'=4,'frame'=32] {'frame'}, dimensions={0} | all-to-all | bytes 3145728 | tf_op jit(solution)/shard_map/all_to_all | solution.py:479
  34.2 0.0 copy-start.1
  34.2 0.0 copy-start.2
  34.2 0.0 copy-start.3
  34.2 0.0 copy-start.6
  34.2 2.6 %temporal.2 = bf16[256,4096]{1,0:T(8,128)(2,1)S(1)} custom-call(bf16[256,3072]{1,0:T(8,128)(2,1)S(1)} %bitcast.24, f32[256,128]{1,0:T(8,128)S(1)} %get-tuple-element.36.cos_ref, f32[256,128]{1,0:T(8,128)S(1)} %get-tuple-element.37.sin_ref, bf16[512,1024]{1,0:T(8,128)(2,1)} %bitcast.27, bf16[512,1024]{1,0:T(8,128)(2,1)} %bitcast.29, bf16[512,1024]{1,0:T(8,128)(2,1)} %bitcast.31), custom_call_target="tpu_custom_call" | custom-call | flops 20000000000 | bytes 1 | tf_op jit(solution)/shard_map/temporal/pallas_call | solution.py:154
  36.8 0.0 copy-start
  36.8 30.7 %all_to_all.34 = bf16[32,8,4096]{2,1,0:T(8,128)(2,1)S(1)} all-to-all(bf16[32,8,4096]{2,1,0:T(8,128)(2,1)S(1)} %bitcast.22), channel_id=1, replica_groups=mesh['cam'=4,'frame'=32] {'frame'}, dimensions={0} | all-to-all | bytes 4194304 | tf_op jit(solution)/shard_map/all_to_all | solution.py:479
  67.5 0.0 copy-done.1
  67.5 0.0 copy-done.2
  67.5 0.0 copy-done.3
  67.5 0.0 copy-done.6
  67.6 0.0 copy-done
  67.6 4.7 %project_first.1 = (bf16[256,2048]{1,0:T(8,128)(2,1)}, bf16[256,2048]{1,0:T(8,128)(2,1)}, bf16[256,2048]{1,0:T(8,128)(2,1)}, bf16[256,1024]{1,0:T(8,128)(2,1)}, bf16[256,1024]{1,0:T(8,128)(2,1)}) custom-call(bf16[256,4096]{1,0:T(8,128)(2,1)S(1)} %bitcast.17, bf16[512,2048]{1,0:T(8,128)(2,1)S(1)} %bitcast.20, bf16[1024,2048]{1,0:T(8,128)(2,1)S(1)} %copy-done, ...), custom_call_target="tpu_custom_call" | custom-call | flops 1 | bytes 1 | tf_op jit(solution)/shard_map/project_first/pallas_call | solution.py:229
  72.3 0.0 copy-start.7
  72.3 5.5 %collective-permute-start = (bf16[256,1024]{1,0:T(8,128)(2,1)}, bf16[256,1024]{1,0:T(8,128)(2,1)S(1)}, u32[]{:S(2)}, u32[]{:S(2)}) collective-permute-start(bf16[256,1024]{1,0:T(8,128)(2,1)} %get-tuple-element.38), channel_id=1, source_target_pairs={{0,96},{96,0},{32,64},{64,32},{1,97},{97,1},{33,65},{65,33},{2,98}... | collective-permute-start | bytes 1572872 | tf_op jit(solution)/shard_map/ppermute | solution.py:485
  77.8 3.3 %temporal.3 = bf16[256,1024]{1,0:T(8,128)(2,1)} custom-call(bf16[256,4096]{1,0:T(8,128)(2,1)S(1)} %bitcast.18, f32[256,128]{1,0:T(8,128)S(1)} %get-tuple-element.36.cos_ref, f32[256,128]{1,0:T(8,128)S(1)} %get-tuple-element.37.sin_ref), custom_call_target="tpu_custom_call" | custom-call | flops 1 | bytes 1 | tf_op jit(solution)/shard_map/temporal/pallas_call | solution.py:154
  81.1 3.9 %all-to-all-start.2 = ((bf16[32,8,1024]{2,1,0:T(8,128)(2,1)}), bf16[32,8,1024]{2,1,0:T(8,128)(2,1)S(1)}, u32[]{:S(2)}, u32[]{:S(2)}) async-start(bf16[32,8,1024]{2,1,0:T(8,128)(2,1)} %bitcast.25), calls=%async_computation.2 | async-start | bytes 1048576 | tf_op jit(solution)/shard_map/all_to_all | solution.py:479
  85.0 5.5 %collective-permute-done.refs_7_ = bf16[256,1024]{1,0:T(8,128)(2,1)S(1)} collective-permute-done((bf16[256,1024]{1,0:T(8,128)(2,1)}, bf16[256,1024]{1,0:T(8,128)(2,1)S(1)}, u32[]{:S(2)}, u32[]{:S(2)}) %collective-permute-start) | collective-permute-done | bytes 524320 | tf_op jit(solution)/shard_map/ppermute | solution.py:485
  90.6 0.0 copy-start.8
  90.6 3.2 %collective-permute-start.1 = (bf16[256,1024]{1,0:T(8,128)(2,1)}, bf16[256,1024]{1,0:T(8,128)(2,1)}, u32[]{:S(2)}, u32[]{:S(2)}) collective-permute-start(bf16[256,1024]{1,0:T(8,128)(2,1)} %get-tuple-element.44), channel_id=1, source_target_pairs={{0,96},{96,0},{32,64},{64,32},{1,97},{97,1},{33,65},{65,33},{2,98}... | collective-permute-start | bytes 1572872 | tf_op jit(solution)/shard_map/ppermute | solution.py:485
  93.8 0.0 copy-done.7
  93.8 0.0 collective-permute-start.4
  93.8 3.8 %all-to-all-done.2 = bf16[32,8,1024]{2,1,0:T(8,128)(2,1)S(1)} async-done(((bf16[32,8,1024]{2,1,0:T(8,128)(2,1)}), bf16[32,8,1024]{2,1,0:T(8,128)(2,1)S(1)}, u32[]{:S(2)}, u32[]{:S(2)}) %all-to-all-start.2) | async-done | bytes 524320 | tf_op jit(solution)/shard_map/all_to_all | solution.py:479
  97.6 0.0 copy-done.8
  97.6 0.0 copy-start.9
  97.6 0.0 copy-start.10
  97.6 7.9 %project_second.1 = (bf16[256,2048]{1,0:T(8,128)(2,1)S(1)}, bf16[256,2048]{1,0:T(8,128)(2,1)}, bf16[256,2048]{1,0:T(8,128)(2,1)}, bf16[256,1536]{1,0:T(8,128)(2,1)}, bf16[256,512]{1,0:T(8,128)(2,1)}) custom-call(bf16[256,1024]{1,0:T(8,128)(2,1)S(1)} %bitcast.21, bf16[2048]{0:T(1024)(128)(2,1)S(1)} %copy-done.6, bf16[512,2048]{1,0:T(8,128)(2,1)} %bitcast.19, ...), custom_call_target="tpu_custom_call" | custom-call | flops 1 | bytes 1 | tf_op jit(solution)/shard_map/project_second/pallas_call | solution.py:298
  105.5 0.1 collective-permute-start.5
  105.6 1.2 collective-permute-start.6
  106.8 0.0 copy-done.9
  106.8 0.8 collective-permute-done.1.refs_8_
  107.5 0.6 collective-permute-start.2
  108.1 0.2 rev.3
  108.4 1.3 collective-permute-start.7
  109.7 0.0 copy-done.10
  109.7 0.0 collective-permute-done.2
  109.7 0.2 collective-permute-start.3
  109.9 1.0 collective-permute-done.3
  111.0 0.0 collective-permute-done.4.refs_5_
  111.0 0.0 collective-permute-done.5.refs_6_
  111.0 12.3 %first_part.1 = (bf16[512,1024]{1,0:T(8,128)(2,1)S(1)}, f32[512,1024]{1,0:T(8,128)S(1)}, f32[512,1024]{1,0:T(8,128)S(1)}, f32[512,1024]{1,0:T(8,128)S(1)}) custom-call(f32[2,1024]{1,0:T(2,128)S(1)} %broadcast_add_fusion.embed_ref, bf16[256,2048]{1,0:T(8,128)(2,1)} %get-tuple-element.48.refs_0_, bf16[256,2048]{1,0:T(8,128)(2,1)} %get-tuple-element.49.refs_1_, ...), custom_call_target="tpu_custom_call" | custom-call | flops 1 | bytes 1 | tf_op jit(solution)/shard_map/first_part/pallas_call | solution.py:372
  123.4 4.1 %collective-permute-done.6.key_ref.piece_a_ref = bf16[256,1536]{1,0:T(8,128)(2,1)S(1)} collective-permute-done((bf16[256,1536]{1,0:T(8,128)(2,1)}, bf16[256,1536]{1,0:T(8,128)(2,1)S(1)}, u32[]{:S(2)}, u32[]{:S(2)}) %collective-permute-start.6) | collective-permute-done | bytes 786464 | tf_op jit(solution)/shard_map/ppermute | solution.py:485
  127.5 0.0 copy-start.4
  127.5 0.0 copy-start.5
  127.5 2.0 %weigh.1 = (f32[512,1024]{1,0:T(8,128)S(1)}, f32[512,1024]{1,0:T(8,128)S(1)}, bf16[512,2048]{1,0:T(8,128)(2,1)S(1)}) custom-call(bf16[512,1024]{1,0:T(8,128)(2,1)S(1)} %get-tuple-element.54.q_ref, f32[512,1024]{1,0:T(8,128)S(1)} %get-tuple-element.55.acc_ref, f32[512,1024]{1,0:T(8,128)S(1)} %get-tuple-element.56.top_ref, ...), custom_call_target="tpu_custom_call" | custom-call | flops 1 | bytes 1 | tf_op jit(solution)/shard_map/weigh/pallas_call | solution.py:406
  129.5 3.0 %collective-permute-done.7.piece_b_ref = bf16[256,512]{1,0:T(8,128)(2,1)S(1)} collective-permute-done((bf16[256,512]{1,0:T(8,128)(2,1)}, bf16[256,512]{1,0:T(8,128)(2,1)S(1)}, u32[]{:S(2)}, u32[]{:S(2)}) %collective-permute-start.7) | collective-permute-done | bytes 262176 | tf_op jit(solution)/shard_map/ppermute | solution.py:485
  132.6 0.0 copy-done.4
  132.6 0.0 copy-done.5
  132.6 4.2 %last_part.1 = bf16[512,2048]{1,0:T(8,128)(2,1)} custom-call(f32[512,1024]{1,0:T(8,128)S(1)} %get-tuple-element.59.acc_ref, f32[512,1024]{1,0:T(8,128)S(1)} %get-tuple-element.60.inverse_ref, bf16[512,2048]{1,0:T(8,128)(2,1)S(1)} %get-tuple-element.61.weight_ref, bf16[256,1536]{1,0:T(8,128)(2,1)S(1)} %collective-permute-done.6.key_ref.piece_a_ref, ...), custom_call_target="tpu_custom_call" | custom-call | flops 1 | bytes 1 | tf_op jit(solution)/shard_map/last_part/pallas_call | solution.py:438
  (5 shorter events, 0.0 us)
Async XLA Ops:
  34.2 33.4 %copy-start.1 = (bf16[2048,1024]{1,0:T(8,128)(2,1)S(1)}, bf16[2048,1024]{1,0:T(8,128)(2,1)}, u32[]{:S(2)}) copy-start(bf16[2048,1024]{1,0:T(8,128)(2,1)} %refs_1_.1) | copy-start | bytes 12582916
  34.2 33.4 %copy-start.2 = (bf16[2048,1024]{1,0:T(8,128)(2,1)S(1)}, bf16[2048,1024]{1,0:T(8,128)(2,1)}, u32[]{:S(2)}) copy-start(bf16[2048,1024]{1,0:T(8,128)(2,1)} %refs_2_.2) | copy-start | bytes 12582916
  34.2 33.4 %copy-start.3 = (bf16[1,1,512,2048]{3,2,1,0:T(8,128)(2,1)S(1)}, bf16[1,1,512,2048]{3,2,1,0:T(8,128)(2,1)}, u32[]{:S(2)}) copy-start(bf16[1,1,512,2048]{3,2,1,0:T(8,128)(2,1)} %param.13) | copy-start | bytes 6291460
  34.2 33.4 %copy-start.6 = (bf16[2048]{0:T(1024)(128)(2,1)S(1)}, bf16[2048]{0:T(1024)(128)(2,1)}, u32[]{:S(2)}) copy-start(bf16[2048]{0:T(1024)(128)(2,1)} %gain_ref.3) | copy-start | bytes 12292
  36.8 30.8 %copy-start = (bf16[1024,2048]{1,0:T(8,128)(2,1)S(1)}, bf16[1024,2048]{1,0:T(8,128)(2,1)}, u32[]{:S(2)}) copy-start(bf16[1024,2048]{1,0:T(8,128)(2,1)} %refs_0_.1) | copy-start | bytes 12582916
  72.3 21.5 %copy-start.7 = (bf16[256,2048]{1,0:T(8,128)(2,1)S(1)}, bf16[256,2048]{1,0:T(8,128)(2,1)}, u32[]{:S(2)}) copy-start(bf16[256,2048]{1,0:T(8,128)(2,1)} %get-tuple-element.50.refs_3_) | copy-start | bytes 3145732
  72.3 18.3 %collective-permute-start = (bf16[256,1024]{1,0:T(8,128)(2,1)}, bf16[256,1024]{1,0:T(8,128)(2,1)S(1)}, u32[]{:S(2)}, u32[]{:S(2)}) collective-permute-start(bf16[256,1024]{1,0:T(8,128)(2,1)} %get-tuple-element.38), channel_id=1, source_target_pairs={{0,96},{96,0},{32,64},{64,32},{1,97},{97,1},{33,65},{65,33},{2,98}... | collective-permute-start | bytes 1572872 | tf_op jit(solution)/shard_map/ppermute | solution.py:485
  81.1 16.4 %all-to-all-start.2 = ((bf16[32,8,1024]{2,1,0:T(8,128)(2,1)}), bf16[32,8,1024]{2,1,0:T(8,128)(2,1)S(1)}, u32[]{:S(2)}, u32[]{:S(2)}) async-start(bf16[32,8,1024]{2,1,0:T(8,128)(2,1)} %bitcast.25), calls=%async_computation.2 | async-start | bytes 1048576 | tf_op jit(solution)/shard_map/all_to_all | solution.py:479
  90.6 7.0 %copy-start.8 = (bf16[256,1024]{1,0:T(8,128)(2,1)}, bf16[256,1024]{1,0:T(8,128)(2,1)S(1)}, u32[]{:S(2)}) copy-start(bf16[256,1024]{1,0:T(8,128)(2,1)S(1)} %collective-permute-done.refs_7_) | copy-start | bytes 1572868
  90.6 17.0 %collective-permute-start.1 = (bf16[256,1024]{1,0:T(8,128)(2,1)}, bf16[256,1024]{1,0:T(8,128)(2,1)}, u32[]{:S(2)}, u32[]{:S(2)}) collective-permute-start(bf16[256,1024]{1,0:T(8,128)(2,1)} %get-tuple-element.44), channel_id=1, source_target_pairs={{0,96},{96,0},{32,64},{64,32},{1,97},{97,1},{33,65},{65,33},{2,98}... | collective-permute-start | bytes 1572872 | tf_op jit(solution)/shard_map/ppermute | solution.py:485
  93.8 17.2 %collective-permute-start.4 = (bf16[256,2048]{1,0:T(8,128)(2,1)S(1)}, bf16[256,2048]{1,0:T(8,128)(2,1)}, u32[]{:S(2)}, u32[]{:S(2)}) collective-permute-start(bf16[256,2048]{1,0:T(8,128)(2,1)S(1)} %copy-done.7), channel_id=1, source_target_pairs={{0,32},{32,0},{64,96},{96,64},{1,33},{33,1},{65,97},{97,65},{2,34}... | collective-permute-start | bytes 3145736 | tf_op jit(solution)/shard_map/ppermute | solution.py:482
  97.6 9.2 %copy-start.9 = (bf16[2,1024]{1,0:T(2,128)(2,1)S(1)}, bf16[2,1024]{1,0:T(2,128)(2,1)}, u32[]{:S(2)}) copy-start(bf16[2,1024]{1,0:T(2,128)(2,1)} %param.25) | copy-start | bytes 12292
  97.6 12.1 %copy-start.10 = (s32[1,2]{1,0:T(1,128)S(1)}, s32[1,2]{1,0:T(1,128)}, u32[]{:S(2)}) copy-start(s32[1,2]{1,0:T(1,128)} %param.18) | copy-start | bytes 28
  105.5 5.6 %collective-permute-start.5 = (bf16[256,2048]{1,0:T(8,128)(2,1)}, bf16[256,2048]{1,0:T(8,128)(2,1)}, u32[]{:S(2)}, u32[]{:S(2)}) collective-permute-start(bf16[256,2048]{1,0:T(8,128)(2,1)} %get-tuple-element.51.refs_4_), channel_id=1, source_target_pairs={{0,32},{32,0},{64,96},{96,64},{1,33},{33,1},{65,97},{97,65},{2,34}... | collective-permute-start | bytes 3145736 | tf_op jit(solution)/shard_map/ppermute | solution.py:482
  105.6 21.9 %collective-permute-start.6 = (bf16[256,1536]{1,0:T(8,128)(2,1)}, bf16[256,1536]{1,0:T(8,128)(2,1)S(1)}, u32[]{:S(2)}, u32[]{:S(2)}) collective-permute-start(bf16[256,1536]{1,0:T(8,128)(2,1)} %get-tuple-element.58), channel_id=1, source_target_pairs={{0,96},{96,0},{32,64},{64,32},{1,97},{97,1},{33,65},{65,33},{2,98}... | collective-permute-start | bytes 2359304 | tf_op jit(solution)/shard_map/ppermute | solution.py:485
  107.5 2.2 %collective-permute-start.2 = (bf16[2,128]{1,0:T(2,128)(2,1)S(1)}, bf16[2,128]{1,0:T(2,128)(2,1)S(1)}, u32[]{:S(2)}, u32[]{:S(2)}) collective-permute-start(bf16[2,128]{1,0:T(2,128)(2,1)S(1)} %slice.10), channel_id=1, source_target_pairs={{0,32},{32,0},{64,96},{96,64},{1,33},{33,1},{65,97},{97,65},{2,34}... | collective-permute-start | bytes 1544 | tf_op jit(solution)/shard_map/ppermute | solution.py:482
  108.4 24.2 %collective-permute-start.7 = (bf16[256,512]{1,0:T(8,128)(2,1)}, bf16[256,512]{1,0:T(8,128)(2,1)S(1)}, u32[]{:S(2)}, u32[]{:S(2)}) collective-permute-start(bf16[256,512]{1,0:T(8,128)(2,1)} %get-tuple-element.62), channel_id=1, source_target_pairs={{0,96},{96,0},{32,64},{64,32},{1,97},{97,1},{33,65},{65,33},{2,98}... | collective-permute-start | bytes 786440 | tf_op jit(solution)/shard_map/ppermute | solution.py:485
  109.7 1.2 collective-permute-start.3
  127.5 5.1 %copy-start.4 = (bf16[1024,2048]{1,0:T(8,128)(2,1)S(1)}, bf16[1024,2048]{1,0:T(8,128)(2,1)}, u32[]{:S(2)}) copy-start(bf16[1024,2048]{1,0:T(8,128)(2,1)} %w_ref.1) | copy-start | bytes 12582916
  127.5 5.1 %copy-start.5 = (bf16[256,2048]{1,0:T(8,128)(2,1)S(1)}, bf16[256,2048]{1,0:T(8,128)(2,1)}, u32[]{:S(2)}) copy-start(bf16[256,2048]{1,0:T(8,128)(2,1)} %get-tuple-element.63.stream_a_ref) | copy-start | bytes 3145732

commit v5 on v4

--- a/solution.py
+++ b/solution.py
@@ -138,9 +138,9 @@
         both = dot_f32(expo, with_ones(value))
         result = both[:, :HEAD_DIM] / both[:, HEAD_DIM:]
         o_ref[:, first + head * HEAD_DIM : first + (head + 1) * HEAD_DIM] = result.astype(BF16)
-        if not count and head % 4 == 3:
-            at = slice((head - 3) * HEAD_DIM, (head + 1) * HEAD_DIM)
-            copies.append(pltpu.make_async_copy(o_ref.at[:, at], o_hbm.at[:, at], sems.at[head // 4]))
+        if not count and head % 2 == 1:
+            at = slice((head - 1) * HEAD_DIM, (head + 1) * HEAD_DIM)
+            copies.append(pltpu.make_async_copy(o_ref.at[:, at], o_hbm.at[:, at], sems.at[head // 2]))
             copies[-1].start()
     for copy in copies:
         copy.wait()
@@ -156,7 +156,7 @@
         in_specs=[VMEM] * 3 + [HBM] * count,
         out_specs=VMEM if count else HBM,
         out_shape=jax.ShapeDtypeStruct(shape, BF16) if count else pltpu.HBM(shape, BF16),
-        scratch_shapes=[pltpu.VMEM((8, 128) if count else shape, BF16), pltpu.SemaphoreType.DMA((3,))],
+        scratch_shapes=[pltpu.VMEM((8, 128) if count else shape, BF16), pltpu.SemaphoreType.DMA((4,))],
         compiler_params=pltpu.CompilerParams(vmem_limit_bytes=6 * MIB),
         cost_estimate=pl.CostEstimate(
             flops=20_000_000_000 if count else 1, bytes_accessed=1, transcendentals=0
@@ -414,10 +414,11 @@
     )(query, acc, top, total, key, embeds)
 
 
-def last_kernel(acc_ref, inverse_ref, weight_ref, piece_a_ref, piece_b_ref, stream_a_ref, stream_b_ref, w_ref, o_ref, out_ref):
+def last_kernel(acc_ref, inverse_ref, weight_ref, piece_a_ref, piece_b_ref, stream_a_ref, stream_b_ref, w_ref, o_hbm, out_ref, o_ref, sems):
     rows = stream_a_ref.shape[0]
     keys = piece_a_ref.shape[0]
     inner = HEADS * HEAD_DIM
+    copies = []
     for block, stream_ref in enumerate((stream_a_ref, stream_b_ref)):
         here = slice(block * rows, (block + 1) * rows)
         for head in range(HEADS):
@@ -428,8 +429,18 @@
             value = alone_part((piece_a_ref, piece_b_ref), value_at, FIRST_PIECE)[...]
             acc = acc_ref[here, at] + dot_f32(weights, value)
             out_ref[here, at] = (acc * inverse_ref[here, at]).astype(BF16)
-        product = dot_f32(out_ref[here, :], w_ref[...])
-        o_ref[here, :] = (stream_ref[...].astype(F32) + product).astype(BF16)
+        for i in range(4):
+            cols = slice(i * 512, (i + 1) * 512)
+            product = dot_f32(out_ref[here, :], w_ref[:, cols])
+            o_ref[here, cols] = (stream_ref[:, cols].astype(F32) + product).astype(BF16)
+            copies.append(
+                pltpu.make_async_copy(
+                    o_ref.at[here, cols], o_hbm.at[here, cols], sems.at[len(copies)]
+                )
+            )
+            copies[-1].start()
+    for copy in copies:
+        copy.wait()
 
 
 def last_part(acc, inverse, weights, pieces, streams, w_out):
@@ -438,9 +449,13 @@
     return pl.pallas_call(
         last_kernel,
         in_specs=[VMEM] * 8,
-        out_specs=VMEM,
-        out_shape=jax.ShapeDtypeStruct((rows, width), BF16),
-        scratch_shapes=[pltpu.VMEM((rows, inner), BF16)],
+        out_specs=HBM,
+        out_shape=pltpu.HBM((rows, width), BF16),
+        scratch_shapes=[
+            pltpu.VMEM((rows, inner), BF16),
+            pltpu.VMEM((rows, width), BF16),
+            pltpu.SemaphoreType.DMA((8,)),
+        ],
         compiler_params=pltpu.CompilerParams(vmem_limit_bytes=8 * MIB),
         cost_estimate=pl.CostEstimate(flops=1, bytes_accessed=1, transcendentals=0),
         name="last_part",

time: 137 us -> 137 us (level)
  no operation moved by 1% of the time
where the time goes in v5:
time: 137 us; the launch traced here: 136 us
  blocking collectives  62.7 us (46%)
  Pallas kernels  37.9 us (28%)
  waiting for transfers between devices  18.3 us (13%)
  starting transfers between devices  16 us (12%)
    all_to_all x2, blocking collectives, exchange(): lax.all_to_all(value, 'frame', split_axis=0, concat_axis=0, tiled=True)  62.7 us
    ppermute x4, waiting for transfers between devices, to_far(): return lax.ppermute(value, 'cam', [(0, 3), (3, 0), (1, 2), (2, 1)])  13.5 us
    pallas_call x1, Pallas kernels, first_part(): pl.pallas_call(first_kernel, in_specs=[VMEM] + [HBM] * len(fetched), out_...  12.3 us
    ppermute x4, starting transfers between devices, to_far(): return lax.ppermute(value, 'cam', [(0, 3), (3, 0), (1, 2), (2, 1)])  11.2 us
    pallas_call x1, Pallas kernels, project_second(): pl.pallas_call(project_second_kernel, in_specs=[VMEM] * 2 + [HBM] * 4, ou...  7.86 us
    pallas_call x2, Pallas kernels, temporal(): pl.pallas_call(functools.partial(temporal_kernel, group), in_specs=[VMEM]...  5.89 us
    pallas_call x1, Pallas kernels, project_first(): pl.pallas_call(functools.partial(project_first_kernel, t_at), in_specs=[V...  4.71 us
    all_to_all x1, starting transfers between devices, exchange(): lax.all_to_all(value, 'frame', split_axis=0, concat_axis=0, tiled=True)  3.9 us
  transfers between devices with their start and end apart: 9, of which 6 were waited for; matrix products, arithmetic and copies ran while one was open for 0% of the time, Pallas kernels for 19%

profile of v5, /device:TPU:1, one launch (start us, length us, event | category | flops | bytes accessed | tf_op | source)
XLA Modules:
  0.0 136.3 jit_solution(16178067664498564085)
XLA Ops:
  0.0 0.7 convert_element_type.14
  0.7 0.1 maximum_bitcast_fusion.frequency_ref
  0.7 0.1 broadcast_in_dim.4.offset_ref
  0.8 1.4 %pack.1 = (bf16[256,3072]{1,0:T(8,128)(2,1)S(1)}, f32[256,128]{1,0:T(8,128)S(1)}, f32[256,128]{1,0:T(8,128)S(1)}) custom-call(bf16[512,1024]{1,0:T(8,128)(2,1)} %bitcast.26, bf16[512,1024]{1,0:T(8,128)(2,1)} %bitcast.28, bf16[512,1024]{1,0:T(8,128)(2,1)} %bitcast.30, f32[32,128]{1,0:T(8,128)S(1)} %broadcast_in_dim.4.offset_ref, ...), custom_call_target="tpu_custom_call" | custom-call | bytes 3145728 | tf_op jit(solution)/shard_map/pack/pallas_call | solution.py:95
  2.2 31.9 %all_to_all.33 = bf16[32,8,3072]{2,1,0:T(8,128)(2,1)S(1)} all-to-all(bf16[32,8,3072]{2,1,0:T(8,128)(2,1)S(1)} %bitcast.23), channel_id=1, replica_groups=mesh['cam'=4,'frame'=32] {'frame'}, dimensions={0} | all-to-all | bytes 3145728 | tf_op jit(solution)/shard_map/all_to_all | solution.py:494
  34.2 0.0 copy-start.1
  34.2 0.0 copy-start.2
  34.2 0.0 copy-start.3
  34.2 0.0 copy-start.6
  34.2 2.6 %temporal.2 = bf16[256,4096]{1,0:T(8,128)(2,1)S(1)} custom-call(bf16[256,3072]{1,0:T(8,128)(2,1)S(1)} %bitcast.24, f32[256,128]{1,0:T(8,128)S(1)} %get-tuple-element.36.cos_ref, f32[256,128]{1,0:T(8,128)S(1)} %get-tuple-element.37.sin_ref, bf16[512,1024]{1,0:T(8,128)(2,1)} %bitcast.27, bf16[512,1024]{1,0:T(8,128)(2,1)} %bitcast.29, bf16[512,1024]{1,0:T(8,128)(2,1)} %bitcast.31), custom_call_target="tpu_custom_call" | custom-call | flops 20000000000 | bytes 1 | tf_op jit(solution)/shard_map/temporal/pallas_call | solution.py:154
  36.8 0.0 copy-start
  36.8 30.7 %all_to_all.34 = bf16[32,8,4096]{2,1,0:T(8,128)(2,1)S(1)} all-to-all(bf16[32,8,4096]{2,1,0:T(8,128)(2,1)S(1)} %bitcast.22), channel_id=1, replica_groups=mesh['cam'=4,'frame'=32] {'frame'}, dimensions={0} | all-to-all | bytes 4194304 | tf_op jit(solution)/shard_map/all_to_all | solution.py:494
  67.5 0.0 copy-done.1
  67.6 0.0 copy-done.2
  67.6 0.0 copy-done.3
  67.6 0.0 copy-done.6
  67.6 0.0 copy-done
  67.6 4.7 %project_first.1 = (bf16[256,2048]{1,0:T(8,128)(2,1)}, bf16[256,2048]{1,0:T(8,128)(2,1)}, bf16[256,2048]{1,0:T(8,128)(2,1)}, bf16[256,1024]{1,0:T(8,128)(2,1)}, bf16[256,1024]{1,0:T(8,128)(2,1)}) custom-call(bf16[256,4096]{1,0:T(8,128)(2,1)S(1)} %bitcast.17, bf16[512,2048]{1,0:T(8,128)(2,1)S(1)} %bitcast.20, bf16[1024,2048]{1,0:T(8,128)(2,1)S(1)} %copy-done, ...), custom_call_target="tpu_custom_call" | custom-call | flops 1 | bytes 1 | tf_op jit(solution)/shard_map/project_first/pallas_call | solution.py:229
  72.3 0.0 copy-start.7
  72.3 5.5 %collective-permute-start = (bf16[256,1024]{1,0:T(8,128)(2,1)}, bf16[256,1024]{1,0:T(8,128)(2,1)S(1)}, u32[]{:S(2)}, u32[]{:S(2)}) collective-permute-start(bf16[256,1024]{1,0:T(8,128)(2,1)} %get-tuple-element.38), channel_id=1, source_target_pairs={{0,96},{96,0},{32,64},{64,32},{1,97},{97,1},{33,65},{65,33},{2,98}... | collective-permute-start | bytes 1572872 | tf_op jit(solution)/shard_map/ppermute | solution.py:500
  77.8 3.3 %temporal.3 = bf16[256,1024]{1,0:T(8,128)(2,1)} custom-call(bf16[256,4096]{1,0:T(8,128)(2,1)S(1)} %bitcast.18, f32[256,128]{1,0:T(8,128)S(1)} %get-tuple-element.36.cos_ref, f32[256,128]{1,0:T(8,128)S(1)} %get-tuple-element.37.sin_ref), custom_call_target="tpu_custom_call" | custom-call | flops 1 | bytes 1 | tf_op jit(solution)/shard_map/temporal/pallas_call | solution.py:154
  81.1 3.9 %all-to-all-start.2 = ((bf16[32,8,1024]{2,1,0:T(8,128)(2,1)}), bf16[32,8,1024]{2,1,0:T(8,128)(2,1)S(1)}, u32[]{:S(2)}, u32[]{:S(2)}) async-start(bf16[32,8,1024]{2,1,0:T(8,128)(2,1)} %bitcast.25), calls=%async_computation.2 | async-start | bytes 1048576 | tf_op jit(solution)/shard_map/all_to_all | solution.py:494
  85.0 5.6 %collective-permute-done.refs_7_ = bf16[256,1024]{1,0:T(8,128)(2,1)S(1)} collective-permute-done((bf16[256,1024]{1,0:T(8,128)(2,1)}, bf16[256,1024]{1,0:T(8,128)(2,1)S(1)}, u32[]{:S(2)}, u32[]{:S(2)}) %collective-permute-start) | collective-permute-done | bytes 524320 | tf_op jit(solution)/shard_map/ppermute | solution.py:500
  90.6 0.0 copy-start.8
  90.6 3.2 %collective-permute-start.1 = (bf16[256,1024]{1,0:T(8,128)(2,1)}, bf16[256,1024]{1,0:T(8,128)(2,1)}, u32[]{:S(2)}, u32[]{:S(2)}) collective-permute-start(bf16[256,1024]{1,0:T(8,128)(2,1)} %get-tuple-element.44), channel_id=1, source_target_pairs={{0,96},{96,0},{32,64},{64,32},{1,97},{97,1},{33,65},{65,33},{2,98}... | collective-permute-start | bytes 1572872 | tf_op jit(solution)/shard_map/ppermute | solution.py:500
  93.8 0.0 copy-done.7
  93.8 0.0 collective-permute-start.4
  93.8 3.7 %all-to-all-done.2 = bf16[32,8,1024]{2,1,0:T(8,128)(2,1)S(1)} async-done(((bf16[32,8,1024]{2,1,0:T(8,128)(2,1)}), bf16[32,8,1024]{2,1,0:T(8,128)(2,1)S(1)}, u32[]{:S(2)}, u32[]{:S(2)}) %all-to-all-start.2) | async-done | bytes 524320 | tf_op jit(solution)/shard_map/all_to_all | solution.py:494
  97.5 0.0 copy-done.8
  97.5 0.0 copy-start.9
  97.5 0.0 copy-start.10
  97.5 7.9 %project_second.1 = (bf16[256,2048]{1,0:T(8,128)(2,1)S(1)}, bf16[256,2048]{1,0:T(8,128)(2,1)}, bf16[256,2048]{1,0:T(8,128)(2,1)}, bf16[256,1536]{1,0:T(8,128)(2,1)}, bf16[256,512]{1,0:T(8,128)(2,1)}) custom-call(bf16[256,1024]{1,0:T(8,128)(2,1)S(1)} %bitcast.21, bf16[2048]{0:T(1024)(128)(2,1)S(1)} %copy-done.6, bf16[512,2048]{1,0:T(8,128)(2,1)} %bitcast.19, ...), custom_call_target="tpu_custom_call" | custom-call | flops 1 | bytes 1 | tf_op jit(solution)/shard_map/project_second/pallas_call | solution.py:298
  105.4 0.1 collective-permute-start.5
  105.5 1.2 collective-permute-start.6
  106.7 0.0 copy-done.9
  106.7 0.8 collective-permute-done.1.refs_8_
  107.5 0.6 collective-permute-start.2
  108.2 0.2 rev.3
  108.4 1.3 collective-permute-start.7
  109.6 0.0 copy-done.10
  109.7 0.0 collective-permute-done.2
  109.7 0.2 collective-permute-start.3
  109.9 1.0 collective-permute-done.3
  111.0 0.0 collective-permute-done.4.refs_5_
  111.0 0.0 collective-permute-done.5.refs_6_
  111.0 12.3 %first_part.1 = (bf16[512,1024]{1,0:T(8,128)(2,1)S(1)}, f32[512,1024]{1,0:T(8,128)S(1)}, f32[512,1024]{1,0:T(8,128)S(1)}, f32[512,1024]{1,0:T(8,128)S(1)}) custom-call(f32[2,1024]{1,0:T(2,128)S(1)} %broadcast_add_fusion.embed_ref, bf16[256,2048]{1,0:T(8,128)(2,1)} %get-tuple-element.48.refs_0_, bf16[256,2048]{1,0:T(8,128)(2,1)} %get-tuple-element.49.refs_1_, ...), custom_call_target="tpu_custom_call" | custom-call | flops 1 | bytes 1 | tf_op jit(solution)/shard_map/first_part/pallas_call | solution.py:372
  123.3 4.1 %collective-permute-done.6.key_ref.piece_a_ref = bf16[256,1536]{1,0:T(8,128)(2,1)S(1)} collective-permute-done((bf16[256,1536]{1,0:T(8,128)(2,1)}, bf16[256,1536]{1,0:T(8,128)(2,1)S(1)}, u32[]{:S(2)}, u32[]{:S(2)}) %collective-permute-start.6) | collective-permute-done | bytes 786464 | tf_op jit(solution)/shard_map/ppermute | solution.py:500
  127.4 0.0 copy-start.4
  127.4 0.0 copy-start.5
  127.4 2.0 %weigh.1 = (f32[512,1024]{1,0:T(8,128)S(1)}, f32[512,1024]{1,0:T(8,128)S(1)}, bf16[512,2048]{1,0:T(8,128)(2,1)S(1)}) custom-call(bf16[512,1024]{1,0:T(8,128)(2,1)S(1)} %get-tuple-element.54.q_ref, f32[512,1024]{1,0:T(8,128)S(1)} %get-tuple-element.55.acc_ref, f32[512,1024]{1,0:T(8,128)S(1)} %get-tuple-element.56.top_ref, ...), custom_call_target="tpu_custom_call" | custom-call | flops 1 | bytes 1 | tf_op jit(solution)/shard_map/weigh/pallas_call | solution.py:406
  129.5 3.0 %collective-permute-done.7.piece_b_ref = bf16[256,512]{1,0:T(8,128)(2,1)S(1)} collective-permute-done((bf16[256,512]{1,0:T(8,128)(2,1)}, bf16[256,512]{1,0:T(8,128)(2,1)S(1)}, u32[]{:S(2)}, u32[]{:S(2)}) %collective-permute-start.7) | collective-permute-done | bytes 262176 | tf_op jit(solution)/shard_map/ppermute | solution.py:500
  132.5 0.0 copy-done.4
  132.5 0.0 copy-done.5
  132.5 3.6 %last_part.1 = bf16[512,2048]{1,0:T(8,128)(2,1)} custom-call(f32[512,1024]{1,0:T(8,128)S(1)} %get-tuple-element.59.acc_ref, f32[512,1024]{1,0:T(8,128)S(1)} %get-tuple-element.60.inverse_ref, bf16[512,2048]{1,0:T(8,128)(2,1)S(1)} %get-tuple-element.61.weight_ref, bf16[256,1536]{1,0:T(8,128)(2,1)S(1)} %collective-permute-done.6.key_ref.piece_a_ref, ...), custom_call_target="tpu_custom_call" | custom-call | flops 1 | bytes 1 | tf_op jit(solution)/shard_map/last_part/pallas_call | solution.py:449
  (5 shorter events, 0.0 us)
Async XLA Ops:
  34.2 33.4 %copy-start.1 = (bf16[2048,1024]{1,0:T(8,128)(2,1)S(1)}, bf16[2048,1024]{1,0:T(8,128)(2,1)}, u32[]{:S(2)}) copy-start(bf16[2048,1024]{1,0:T(8,128)(2,1)} %refs_1_.1) | copy-start | bytes 12582916
  34.2 33.4 %copy-start.2 = (bf16[2048,1024]{1,0:T(8,128)(2,1)S(1)}, bf16[2048,1024]{1,0:T(8,128)(2,1)}, u32[]{:S(2)}) copy-start(bf16[2048,1024]{1,0:T(8,128)(2,1)} %refs_2_.2) | copy-start | bytes 12582916
  34.2 33.4 %copy-start.3 = (bf16[1,1,512,2048]{3,2,1,0:T(8,128)(2,1)S(1)}, bf16[1,1,512,2048]{3,2,1,0:T(8,128)(2,1)}, u32[]{:S(2)}) copy-start(bf16[1,1,512,2048]{3,2,1,0:T(8,128)(2,1)} %param.13) | copy-start | bytes 6291460
  34.2 33.4 %copy-start.6 = (bf16[2048]{0:T(1024)(128)(2,1)S(1)}, bf16[2048]{0:T(1024)(128)(2,1)}, u32[]{:S(2)}) copy-start(bf16[2048]{0:T(1024)(128)(2,1)} %gain_ref.3) | copy-start | bytes 12292
  36.8 30.8 %copy-start = (bf16[1024,2048]{1,0:T(8,128)(2,1)S(1)}, bf16[1024,2048]{1,0:T(8,128)(2,1)}, u32[]{:S(2)}) copy-start(bf16[1024,2048]{1,0:T(8,128)(2,1)} %refs_0_.1) | copy-start | bytes 12582916
  72.3 21.5 %copy-start.7 = (bf16[256,2048]{1,0:T(8,128)(2,1)S(1)}, bf16[256,2048]{1,0:T(8,128)(2,1)}, u32[]{:S(2)}) copy-start(bf16[256,2048]{1,0:T(8,128)(2,1)} %get-tuple-element.50.refs_3_) | copy-start | bytes 3145732
  72.3 18.3 %collective-permute-start = (bf16[256,1024]{1,0:T(8,128)(2,1)}, bf16[256,1024]{1,0:T(8,128)(2,1)S(1)}, u32[]{:S(2)}, u32[]{:S(2)}) collective-permute-start(bf16[256,1024]{1,0:T(8,128)(2,1)} %get-tuple-element.38), channel_id=1, source_target_pairs={{0,96},{96,0},{32,64},{64,32},{1,97},{97,1},{33,65},{65,33},{2,98}... | collective-permute-start | bytes 1572872 | tf_op jit(solution)/shard_map/ppermute | solution.py:500
  81.1 16.4 %all-to-all-start.2 = ((bf16[32,8,1024]{2,1,0:T(8,128)(2,1)}), bf16[32,8,1024]{2,1,0:T(8,128)(2,1)S(1)}, u32[]{:S(2)}, u32[]{:S(2)}) async-start(bf16[32,8,1024]{2,1,0:T(8,128)(2,1)} %bitcast.25), calls=%async_computation.2 | async-start | bytes 1048576 | tf_op jit(solution)/shard_map/all_to_all | solution.py:494
  90.6 7.0 %copy-start.8 = (bf16[256,1024]{1,0:T(8,128)(2,1)}, bf16[256,1024]{1,0:T(8,128)(2,1)S(1)}, u32[]{:S(2)}) copy-start(bf16[256,1024]{1,0:T(8,128)(2,1)S(1)} %collective-permute-done.refs_7_) | copy-start | bytes 1572868
  90.6 17.0 %collective-permute-start.1 = (bf16[256,1024]{1,0:T(8,128)(2,1)}, bf16[256,1024]{1,0:T(8,128)(2,1)}, u32[]{:S(2)}, u32[]{:S(2)}) collective-permute-start(bf16[256,1024]{1,0:T(8,128)(2,1)} %get-tuple-element.44), channel_id=1, source_target_pairs={{0,96},{96,0},{32,64},{64,32},{1,97},{97,1},{33,65},{65,33},{2,98}... | collective-permute-start | bytes 1572872 | tf_op jit(solution)/shard_map/ppermute | solution.py:500
  93.8 17.1 %collective-permute-start.4 = (bf16[256,2048]{1,0:T(8,128)(2,1)S(1)}, bf16[256,2048]{1,0:T(8,128)(2,1)}, u32[]{:S(2)}, u32[]{:S(2)}) collective-permute-start(bf16[256,2048]{1,0:T(8,128)(2,1)S(1)} %copy-done.7), channel_id=1, source_target_pairs={{0,32},{32,0},{64,96},{96,64},{1,33},{33,1},{65,97},{97,65},{2,34}... | collective-permute-start | bytes 3145736 | tf_op jit(solution)/shard_map/ppermute | solution.py:497
  97.5 9.2 %copy-start.9 = (bf16[2,1024]{1,0:T(2,128)(2,1)S(1)}, bf16[2,1024]{1,0:T(2,128)(2,1)}, u32[]{:S(2)}) copy-start(bf16[2,1024]{1,0:T(2,128)(2,1)} %param.25) | copy-start | bytes 12292
  97.5 12.1 %copy-start.10 = (s32[1,2]{1,0:T(1,128)S(1)}, s32[1,2]{1,0:T(1,128)}, u32[]{:S(2)}) copy-start(s32[1,2]{1,0:T(1,128)} %param.18) | copy-start | bytes 28
  105.4 5.6 %collective-permute-start.5 = (bf16[256,2048]{1,0:T(8,128)(2,1)}, bf16[256,2048]{1,0:T(8,128)(2,1)}, u32[]{:S(2)}, u32[]{:S(2)}) collective-permute-start(bf16[256,2048]{1,0:T(8,128)(2,1)} %get-tuple-element.51.refs_4_), channel_id=1, source_target_pairs={{0,32},{32,0},{64,96},{96,64},{1,33},{33,1},{65,97},{97,65},{2,34}... | collective-permute-start | bytes 3145736 | tf_op jit(solution)/shard_map/ppermute | solution.py:497
  105.5 21.9 %collective-permute-start.6 = (bf16[256,1536]{1,0:T(8,128)(2,1)}, bf16[256,1536]{1,0:T(8,128)(2,1)S(1)}, u32[]{:S(2)}, u32[]{:S(2)}) collective-permute-start(bf16[256,1536]{1,0:T(8,128)(2,1)} %get-tuple-element.58), channel_id=1, source_target_pairs={{0,96},{96,0},{32,64},{64,32},{1,97},{97,1},{33,65},{65,33},{2,98}... | collective-permute-start | bytes 2359304 | tf_op jit(solution)/shard_map/ppermute | solution.py:500
  107.5 2.1 %collective-permute-start.2 = (bf16[2,128]{1,0:T(2,128)(2,1)S(1)}, bf16[2,128]{1,0:T(2,128)(2,1)S(1)}, u32[]{:S(2)}, u32[]{:S(2)}) collective-permute-start(bf16[2,128]{1,0:T(2,128)(2,1)S(1)} %slice.10), channel_id=1, source_target_pairs={{0,32},{32,0},{64,96},{96,64},{1,33},{33,1},{65,97},{97,65},{2,34}... | collective-permute-start | bytes 1544 | tf_op jit(solution)/shard_map/ppermute | solution.py:497
  108.4 24.2 %collective-permute-start.7 = (bf16[256,512]{1,0:T(8,128)(2,1)}, bf16[256,512]{1,0:T(8,128)(2,1)S(1)}, u32[]{:S(2)}, u32[]{:S(2)}) collective-permute-start(bf16[256,512]{1,0:T(8,128)(2,1)} %get-tuple-element.62), channel_id=1, source_target_pairs={{0,96},{96,0},{32,64},{64,32},{1,97},{97,1},{33,65},{65,33},{2,98}... | collective-permute-start | bytes 786440 | tf_op jit(solution)/shard_map/ppermute | solution.py:500
  109.7 1.2 collective-permute-start.3
  127.4 5.1 %copy-start.4 = (bf16[1024,2048]{1,0:T(8,128)(2,1)S(1)}, bf16[1024,2048]{1,0:T(8,128)(2,1)}, u32[]{:S(2)}) copy-start(bf16[1024,2048]{1,0:T(8,128)(2,1)} %w_ref.1) | copy-start | bytes 12582916
  127.4 5.1 %copy-start.5 = (bf16[256,2048]{1,0:T(8,128)(2,1)S(1)}, bf16[256,2048]{1,0:T(8,128)(2,1)}, u32[]{:S(2)}) copy-start(bf16[256,2048]{1,0:T(8,128)(2,1)} %get-tuple-element.63.stream_a_ref) | copy-start | bytes 3145732

commit v6 on v5

--- a/solution.py
+++ b/solution.py
@@ -247,16 +247,17 @@
     part = 512
     get_hidden = pltpu.make_async_copy(hidden_hbm.at[rows:, :], hidden_ref, arrived.at[9])
     get_hidden.start()
-    cuts = [(0, slice(i, i + part)) for i in range(0, w_hbm[0].shape[1], part)]
-    for at in KV_CUTS:
-        first = at.start % inner
-        cuts.append((1 + at.start // inner, slice(first, first + at.stop - at.start)))
-    copies = []
-    for i, (which, at) in enumerate(cuts):
-        copies.append(
-            pltpu.make_async_copy(w_hbm[which].at[:, at], w_refs[which].at[:, at], arrived.at[i])
-        )
-        copies[-1].start()
+    copies = [
+        pltpu.make_async_copy(a, b, arrived.at[i]) for i, (a, b) in enumerate(zip(w_hbm, w_refs))
+    ]
+    for copy in copies:
+        copy.start()
+    first_use = {0: 0, w_hbm[0].shape[1] // part: 1, w_hbm[0].shape[1] // part + inner // part: 2}
+
+    def ready(i):
+        if i in first_use:
+            copies[first_use[i]].wait()
+
     leaving = []
 
     def leave(a, b):
@@ -282,7 +283,7 @@
         outs[0],
         normed_ref,
         kv_ref,
-        lambda i: copies[i].wait(),
+        ready,
         done,
     )
     for copy in leaving:

time: 137 us -> 136 us (level)
  no operation moved by 1% of the time
where the time goes in v6:
time: 136 us
  blocking collectives  62.7 us (46%)
  Pallas kernels  37.7 us (28%)
  waiting for transfers between devices  18.4 us (14%)
  starting transfers between devices  15.8 us (12%)
    all_to_all x2, blocking collectives, exchange(): lax.all_to_all(value, 'frame', split_axis=0, concat_axis=0, tiled=True)  62.7 us
    ppermute x4, waiting for transfers between devices, to_far(): return lax.ppermute(value, 'cam', [(0, 3), (3, 0), (1, 2), (2, 1)])  13.7 us
    pallas_call x1, Pallas kernels, first_part(): pl.pallas_call(first_kernel, in_specs=[VMEM] + [HBM] * len(fetched), out_...  12.3 us
    ppermute x4, starting transfers between devices, to_far(): return lax.ppermute(value, 'cam', [(0, 3), (3, 0), (1, 2), (2, 1)])  11.1 us
    pallas_call x1, Pallas kernels, project_second(): pl.pallas_call(project_second_kernel, in_specs=[VMEM] * 2 + [HBM] * 4, ou...  7.68 us
    pallas_call x2, Pallas kernels, temporal(): pl.pallas_call(functools.partial(temporal_kernel, group), in_specs=[VMEM]...  5.89 us
    pallas_call x1, Pallas kernels, project_first(): pl.pallas_call(functools.partial(project_first_kernel, t_at), in_specs=[V...  4.71 us
    all_to_all x1, starting transfers between devices, exchange(): lax.all_to_all(value, 'frame', split_axis=0, concat_axis=0, tiled=True)  3.9 us
  transfers between devices with their start and end apart: 9, of which 6 were waited for; matrix products, arithmetic and copies ran while one was open for 0% of the time, Pallas kernels for 19%

profile of v6, /device:TPU:1, one launch (start us, length us, event | category | flops | bytes accessed | tf_op | source)
XLA Modules:
  0.0 136.1 jit_solution(12800928911869736200)
XLA Ops:
  0.0 0.7 convert_element_type.14
  0.7 0.1 maximum_bitcast_fusion.frequency_ref
  0.7 0.1 broadcast_in_dim.4.offset_ref
  0.8 1.4 %pack.1 = (bf16[256,3072]{1,0:T(8,128)(2,1)S(1)}, f32[256,128]{1,0:T(8,128)S(1)}, f32[256,128]{1,0:T(8,128)S(1)}) custom-call(bf16[512,1024]{1,0:T(8,128)(2,1)} %bitcast.26, bf16[512,1024]{1,0:T(8,128)(2,1)} %bitcast.28, bf16[512,1024]{1,0:T(8,128)(2,1)} %bitcast.30, f32[32,128]{1,0:T(8,128)S(1)} %broadcast_in_dim.4.offset_ref, ...), custom_call_target="tpu_custom_call" | custom-call | bytes 3145728 | tf_op jit(solution)/shard_map/pack/pallas_call | solution.py:95
  2.2 31.9 %all_to_all.33 = bf16[32,8,3072]{2,1,0:T(8,128)(2,1)S(1)} all-to-all(bf16[32,8,3072]{2,1,0:T(8,128)(2,1)S(1)} %bitcast.23), channel_id=1, replica_groups=mesh['cam'=4,'frame'=32] {'frame'}, dimensions={0} | all-to-all | bytes 3145728 | tf_op jit(solution)/shard_map/all_to_all | solution.py:495
  34.2 0.0 copy-start.1
  34.2 0.0 copy-start.2
  34.2 0.0 copy-start.3
  34.2 0.0 copy-start.6
  34.2 2.6 %temporal.2 = bf16[256,4096]{1,0:T(8,128)(2,1)S(1)} custom-call(bf16[256,3072]{1,0:T(8,128)(2,1)S(1)} %bitcast.24, f32[256,128]{1,0:T(8,128)S(1)} %get-tuple-element.36.cos_ref, f32[256,128]{1,0:T(8,128)S(1)} %get-tuple-element.37.sin_ref, bf16[512,1024]{1,0:T(8,128)(2,1)} %bitcast.27, bf16[512,1024]{1,0:T(8,128)(2,1)} %bitcast.29, bf16[512,1024]{1,0:T(8,128)(2,1)} %bitcast.31), custom_call_target="tpu_custom_call" | custom-call | flops 20000000000 | bytes 1 | tf_op jit(solution)/shard_map/temporal/pallas_call | solution.py:154
  36.8 0.0 copy-start
  36.8 30.7 %all_to_all.34 = bf16[32,8,4096]{2,1,0:T(8,128)(2,1)S(1)} all-to-all(bf16[32,8,4096]{2,1,0:T(8,128)(2,1)S(1)} %bitcast.22), channel_id=1, replica_groups=mesh['cam'=4,'frame'=32] {'frame'}, dimensions={0} | all-to-all | bytes 4194304 | tf_op jit(solution)/shard_map/all_to_all | solution.py:495
  67.5 0.0 copy-done.1
  67.6 0.0 copy-done.2
  67.6 0.0 copy-done.3
  67.6 0.0 copy-done.6
  67.6 0.0 copy-done
  67.6 4.7 %project_first.1 = (bf16[256,2048]{1,0:T(8,128)(2,1)}, bf16[256,2048]{1,0:T(8,128)(2,1)}, bf16[256,2048]{1,0:T(8,128)(2,1)}, bf16[256,1024]{1,0:T(8,128)(2,1)}, bf16[256,1024]{1,0:T(8,128)(2,1)}) custom-call(bf16[256,4096]{1,0:T(8,128)(2,1)S(1)} %bitcast.17, bf16[512,2048]{1,0:T(8,128)(2,1)S(1)} %bitcast.20, bf16[1024,2048]{1,0:T(8,128)(2,1)S(1)} %copy-done, ...), custom_call_target="tpu_custom_call" | custom-call | flops 1 | bytes 1 | tf_op jit(solution)/shard_map/project_first/pallas_call | solution.py:229
  72.3 0.0 copy-start.7
  72.3 5.5 %collective-permute-start = (bf16[256,1024]{1,0:T(8,128)(2,1)}, bf16[256,1024]{1,0:T(8,128)(2,1)S(1)}, u32[]{:S(2)}, u32[]{:S(2)}) collective-permute-start(bf16[256,1024]{1,0:T(8,128)(2,1)} %get-tuple-element.38), channel_id=1, source_target_pairs={{0,96},{96,0},{32,64},{64,32},{1,97},{97,1},{33,65},{65,33},{2,98}... | collective-permute-start | bytes 1572872 | tf_op jit(solution)/shard_map/ppermute | solution.py:501
  77.8 3.3 %temporal.3 = bf16[256,1024]{1,0:T(8,128)(2,1)} custom-call(bf16[256,4096]{1,0:T(8,128)(2,1)S(1)} %bitcast.18, f32[256,128]{1,0:T(8,128)S(1)} %get-tuple-element.36.cos_ref, f32[256,128]{1,0:T(8,128)S(1)} %get-tuple-element.37.sin_ref), custom_call_target="tpu_custom_call" | custom-call | flops 1 | bytes 1 | tf_op jit(solution)/shard_map/temporal/pallas_call | solution.py:154
  81.1 3.9 %all-to-all-start.2 = ((bf16[32,8,1024]{2,1,0:T(8,128)(2,1)}), bf16[32,8,1024]{2,1,0:T(8,128)(2,1)S(1)}, u32[]{:S(2)}, u32[]{:S(2)}) async-start(bf16[32,8,1024]{2,1,0:T(8,128)(2,1)} %bitcast.25), calls=%async_computation.2 | async-start | bytes 1048576 | tf_op jit(solution)/shard_map/all_to_all | solution.py:495
  85.0 5.6 %collective-permute-done.refs_7_ = bf16[256,1024]{1,0:T(8,128)(2,1)S(1)} collective-permute-done((bf16[256,1024]{1,0:T(8,128)(2,1)}, bf16[256,1024]{1,0:T(8,128)(2,1)S(1)}, u32[]{:S(2)}, u32[]{:S(2)}) %collective-permute-start) | collective-permute-done | bytes 524320 | tf_op jit(solution)/shard_map/ppermute | solution.py:501
  90.6 0.0 copy-start.8
  90.6 3.2 %collective-permute-start.1 = (bf16[256,1024]{1,0:T(8,128)(2,1)}, bf16[256,1024]{1,0:T(8,128)(2,1)}, u32[]{:S(2)}, u32[]{:S(2)}) collective-permute-start(bf16[256,1024]{1,0:T(8,128)(2,1)} %get-tuple-element.44), channel_id=1, source_target_pairs={{0,96},{96,0},{32,64},{64,32},{1,97},{97,1},{33,65},{65,33},{2,98}... | collective-permute-start | bytes 1572872 | tf_op jit(solution)/shard_map/ppermute | solution.py:501
  93.8 0.0 copy-done.7
  93.8 0.0 collective-permute-start.4
  93.8 3.7 %all-to-all-done.2 = bf16[32,8,1024]{2,1,0:T(8,128)(2,1)S(1)} async-done(((bf16[32,8,1024]{2,1,0:T(8,128)(2,1)}), bf16[32,8,1024]{2,1,0:T(8,128)(2,1)S(1)}, u32[]{:S(2)}, u32[]{:S(2)}) %all-to-all-start.2) | async-done | bytes 524320 | tf_op jit(solution)/shard_map/all_to_all | solution.py:495
  97.5 0.0 copy-done.8
  97.5 0.0 copy-start.9
  97.5 0.0 copy-start.10
  97.5 7.7 %project_second.1 = (bf16[256,2048]{1,0:T(8,128)(2,1)S(1)}, bf16[256,2048]{1,0:T(8,128)(2,1)}, bf16[256,2048]{1,0:T(8,128)(2,1)}, bf16[256,1536]{1,0:T(8,128)(2,1)}, bf16[256,512]{1,0:T(8,128)(2,1)}) custom-call(bf16[256,1024]{1,0:T(8,128)(2,1)S(1)} %bitcast.21, bf16[2048]{0:T(1024)(128)(2,1)S(1)} %copy-done.6, bf16[512,2048]{1,0:T(8,128)(2,1)} %bitcast.19, ...), custom_call_target="tpu_custom_call" | custom-call | flops 1 | bytes 1 | tf_op jit(solution)/shard_map/project_second/pallas_call | solution.py:299
  105.2 0.1 collective-permute-start.5
  105.3 1.2 collective-permute-start.6
  106.6 0.0 copy-done.9
  106.6 1.0 collective-permute-done.1.refs_8_
  107.5 0.6 collective-permute-start.2
  108.2 0.2 rev.3
  108.4 1.1 collective-permute-start.7
  109.4 0.0 copy-done.10
  109.5 0.0 collective-permute-done.2
  109.5 0.2 collective-permute-start.3
  109.7 1.0 collective-permute-done.3
  110.8 0.0 collective-permute-done.4.refs_5_
  110.8 0.0 collective-permute-done.5.refs_6_
  110.8 12.3 %first_part.1 = (bf16[512,1024]{1,0:T(8,128)(2,1)S(1)}, f32[512,1024]{1,0:T(8,128)S(1)}, f32[512,1024]{1,0:T(8,128)S(1)}, f32[512,1024]{1,0:T(8,128)S(1)}) custom-call(f32[2,1024]{1,0:T(2,128)S(1)} %broadcast_add_fusion.embed_ref, bf16[256,2048]{1,0:T(8,128)(2,1)} %get-tuple-element.48.refs_0_, bf16[256,2048]{1,0:T(8,128)(2,1)} %get-tuple-element.49.refs_1_, ...), custom_call_target="tpu_custom_call" | custom-call | flops 1 | bytes 1 | tf_op jit(solution)/shard_map/first_part/pallas_call | solution.py:373
  123.1 4.1 %collective-permute-done.6.key_ref.piece_a_ref = bf16[256,1536]{1,0:T(8,128)(2,1)S(1)} collective-permute-done((bf16[256,1536]{1,0:T(8,128)(2,1)}, bf16[256,1536]{1,0:T(8,128)(2,1)S(1)}, u32[]{:S(2)}, u32[]{:S(2)}) %collective-permute-start.6) | collective-permute-done | bytes 786464 | tf_op jit(solution)/shard_map/ppermute | solution.py:501
  127.3 0.0 copy-start.4
  127.3 0.0 copy-start.5
  127.3 2.0 %weigh.1 = (f32[512,1024]{1,0:T(8,128)S(1)}, f32[512,1024]{1,0:T(8,128)S(1)}, bf16[512,2048]{1,0:T(8,128)(2,1)S(1)}) custom-call(bf16[512,1024]{1,0:T(8,128)(2,1)S(1)} %get-tuple-element.54.q_ref, f32[512,1024]{1,0:T(8,128)S(1)} %get-tuple-element.55.acc_ref, f32[512,1024]{1,0:T(8,128)S(1)} %get-tuple-element.56.top_ref, ...), custom_call_target="tpu_custom_call" | custom-call | flops 1 | bytes 1 | tf_op jit(solution)/shard_map/weigh/pallas_call | solution.py:407
  129.3 3.0 %collective-permute-done.7.piece_b_ref = bf16[256,512]{1,0:T(8,128)(2,1)S(1)} collective-permute-done((bf16[256,512]{1,0:T(8,128)(2,1)}, bf16[256,512]{1,0:T(8,128)(2,1)S(1)}, u32[]{:S(2)}, u32[]{:S(2)}) %collective-permute-start.7) | collective-permute-done | bytes 262176 | tf_op jit(solution)/shard_map/ppermute | solution.py:501
  132.3 0.0 copy-done.4
  132.3 0.0 copy-done.5
  132.3 3.6 %last_part.1 = bf16[512,2048]{1,0:T(8,128)(2,1)} custom-call(f32[512,1024]{1,0:T(8,128)S(1)} %get-tuple-element.59.acc_ref, f32[512,1024]{1,0:T(8,128)S(1)} %get-tuple-element.60.inverse_ref, bf16[512,2048]{1,0:T(8,128)(2,1)S(1)} %get-tuple-element.61.weight_ref, bf16[256,1536]{1,0:T(8,128)(2,1)S(1)} %collective-permute-done.6.key_ref.piece_a_ref, ...), custom_call_target="tpu_custom_call" | custom-call | flops 1 | bytes 1 | tf_op jit(solution)/shard_map/last_part/pallas_call | solution.py:450
  (5 shorter events, 0.0 us)
Async XLA Ops:
  34.2 33.4 %copy-start.1 = (bf16[2048,1024]{1,0:T(8,128)(2,1)S(1)}, bf16[2048,1024]{1,0:T(8,128)(2,1)}, u32[]{:S(2)}) copy-start(bf16[2048,1024]{1,0:T(8,128)(2,1)} %refs_1_.1) | copy-start | bytes 12582916
  34.2 33.4 %copy-start.2 = (bf16[2048,1024]{1,0:T(8,128)(2,1)S(1)}, bf16[2048,1024]{1,0:T(8,128)(2,1)}, u32[]{:S(2)}) copy-start(bf16[2048,1024]{1,0:T(8,128)(2,1)} %refs_2_.2) | copy-start | bytes 12582916
  34.2 33.4 %copy-start.3 = (bf16[1,1,512,2048]{3,2,1,0:T(8,128)(2,1)S(1)}, bf16[1,1,512,2048]{3,2,1,0:T(8,128)(2,1)}, u32[]{:S(2)}) copy-start(bf16[1,1,512,2048]{3,2,1,0:T(8,128)(2,1)} %param.13) | copy-start | bytes 6291460
  34.2 33.4 %copy-start.6 = (bf16[2048]{0:T(1024)(128)(2,1)S(1)}, bf16[2048]{0:T(1024)(128)(2,1)}, u32[]{:S(2)}) copy-start(bf16[2048]{0:T(1024)(128)(2,1)} %gain_ref.3) | copy-start | bytes 12292
  36.8 30.8 %copy-start = (bf16[1024,2048]{1,0:T(8,128)(2,1)S(1)}, bf16[1024,2048]{1,0:T(8,128)(2,1)}, u32[]{:S(2)}) copy-start(bf16[1024,2048]{1,0:T(8,128)(2,1)} %refs_0_.1) | copy-start | bytes 12582916
  72.3 21.5 %copy-start.7 = (bf16[256,2048]{1,0:T(8,128)(2,1)S(1)}, bf16[256,2048]{1,0:T(8,128)(2,1)}, u32[]{:S(2)}) copy-start(bf16[256,2048]{1,0:T(8,128)(2,1)} %get-tuple-element.50.refs_3_) | copy-start | bytes 3145732
  72.3 18.3 %collective-permute-start = (bf16[256,1024]{1,0:T(8,128)(2,1)}, bf16[256,1024]{1,0:T(8,128)(2,1)S(1)}, u32[]{:S(2)}, u32[]{:S(2)}) collective-permute-start(bf16[256,1024]{1,0:T(8,128)(2,1)} %get-tuple-element.38), channel_id=1, source_target_pairs={{0,96},{96,0},{32,64},{64,32},{1,97},{97,1},{33,65},{65,33},{2,98}... | collective-permute-start | bytes 1572872 | tf_op jit(solution)/shard_map/ppermute | solution.py:501
  81.1 16.4 %all-to-all-start.2 = ((bf16[32,8,1024]{2,1,0:T(8,128)(2,1)}), bf16[32,8,1024]{2,1,0:T(8,128)(2,1)S(1)}, u32[]{:S(2)}, u32[]{:S(2)}) async-start(bf16[32,8,1024]{2,1,0:T(8,128)(2,1)} %bitcast.25), calls=%async_computation.2 | async-start | bytes 1048576 | tf_op jit(solution)/shard_map/all_to_all | solution.py:495
  90.6 7.0 %copy-start.8 = (bf16[256,1024]{1,0:T(8,128)(2,1)}, bf16[256,1024]{1,0:T(8,128)(2,1)S(1)}, u32[]{:S(2)}) copy-start(bf16[256,1024]{1,0:T(8,128)(2,1)S(1)} %collective-permute-done.refs_7_) | copy-start | bytes 1572868
  90.6 17.0 %collective-permute-start.1 = (bf16[256,1024]{1,0:T(8,128)(2,1)}, bf16[256,1024]{1,0:T(8,128)(2,1)}, u32[]{:S(2)}, u32[]{:S(2)}) collective-permute-start(bf16[256,1024]{1,0:T(8,128)(2,1)} %get-tuple-element.44), channel_id=1, source_target_pairs={{0,96},{96,0},{32,64},{64,32},{1,97},{97,1},{33,65},{65,33},{2,98}... | collective-permute-start | bytes 1572872 | tf_op jit(solution)/shard_map/ppermute | solution.py:501
  93.8 17.0 %collective-permute-start.4 = (bf16[256,2048]{1,0:T(8,128)(2,1)S(1)}, bf16[256,2048]{1,0:T(8,128)(2,1)}, u32[]{:S(2)}, u32[]{:S(2)}) collective-permute-start(bf16[256,2048]{1,0:T(8,128)(2,1)S(1)} %copy-done.7), channel_id=1, source_target_pairs={{0,32},{32,0},{64,96},{96,64},{1,33},{33,1},{65,97},{97,65},{2,34}... | collective-permute-start | bytes 3145736 | tf_op jit(solution)/shard_map/ppermute | solution.py:498
  97.5 9.0 %copy-start.9 = (bf16[2,1024]{1,0:T(2,128)(2,1)S(1)}, bf16[2,1024]{1,0:T(2,128)(2,1)}, u32[]{:S(2)}) copy-start(bf16[2,1024]{1,0:T(2,128)(2,1)} %param.25) | copy-start | bytes 12292
  97.5 11.9 %copy-start.10 = (s32[1,2]{1,0:T(1,128)S(1)}, s32[1,2]{1,0:T(1,128)}, u32[]{:S(2)}) copy-start(s32[1,2]{1,0:T(1,128)} %param.18) | copy-start | bytes 28
  105.2 5.6 %collective-permute-start.5 = (bf16[256,2048]{1,0:T(8,128)(2,1)}, bf16[256,2048]{1,0:T(8,128)(2,1)}, u32[]{:S(2)}, u32[]{:S(2)}) collective-permute-start(bf16[256,2048]{1,0:T(8,128)(2,1)} %get-tuple-element.51.refs_4_), channel_id=1, source_target_pairs={{0,32},{32,0},{64,96},{96,64},{1,33},{33,1},{65,97},{97,65},{2,34}... | collective-permute-start | bytes 3145736 | tf_op jit(solution)/shard_map/ppermute | solution.py:498
  105.3 21.9 %collective-permute-start.6 = (bf16[256,1536]{1,0:T(8,128)(2,1)}, bf16[256,1536]{1,0:T(8,128)(2,1)S(1)}, u32[]{:S(2)}, u32[]{:S(2)}) collective-permute-start(bf16[256,1536]{1,0:T(8,128)(2,1)} %get-tuple-element.58), channel_id=1, source_target_pairs={{0,96},{96,0},{32,64},{64,32},{1,97},{97,1},{33,65},{65,33},{2,98}... | collective-permute-start | bytes 2359304 | tf_op jit(solution)/shard_map/ppermute | solution.py:501
  107.5 1.9 %collective-permute-start.2 = (bf16[2,128]{1,0:T(2,128)(2,1)S(1)}, bf16[2,128]{1,0:T(2,128)(2,1)S(1)}, u32[]{:S(2)}, u32[]{:S(2)}) collective-permute-start(bf16[2,128]{1,0:T(2,128)(2,1)S(1)} %slice.10), channel_id=1, source_target_pairs={{0,32},{32,0},{64,96},{96,64},{1,33},{33,1},{65,97},{97,65},{2,34}... | collective-permute-start | bytes 1544 | tf_op jit(solution)/shard_map/ppermute | solution.py:498
  108.4 24.0 %collective-permute-start.7 = (bf16[256,512]{1,0:T(8,128)(2,1)}, bf16[256,512]{1,0:T(8,128)(2,1)S(1)}, u32[]{:S(2)}, u32[]{:S(2)}) collective-permute-start(bf16[256,512]{1,0:T(8,128)(2,1)} %get-tuple-element.62), channel_id=1, source_target_pairs={{0,96},{96,0},{32,64},{64,32},{1,97},{97,1},{33,65},{65,33},{2,98}... | collective-permute-start | bytes 786440 | tf_op jit(solution)/shard_map/ppermute | solution.py:501
  109.5 1.2 collective-permute-start.3
  127.3 5.1 %copy-start.4 = (bf16[1024,2048]{1,0:T(8,128)(2,1)S(1)}, bf16[1024,2048]{1,0:T(8,128)(2,1)}, u32[]{:S(2)}) copy-start(bf16[1024,2048]{1,0:T(8,128)(2,1)} %w_ref.1) | copy-start | bytes 12582916
  127.3 5.1 %copy-start.5 = (bf16[256,2048]{1,0:T(8,128)(2,1)S(1)}, bf16[256,2048]{1,0:T(8,128)(2,1)}, u32[]{:S(2)}) copy-start(bf16[256,2048]{1,0:T(8,128)(2,1)} %get-tuple-element.63.stream_a_ref) | copy-start | bytes 3145732
